TPU v7x, 32 devices: a whole 2x2x4 slice. The times are simulated.
32 devices in a mesh: dp: 2 (over x), expert: 16 (over z, y, core).
Axes of the slice: x: 2, y: 2, z: 4, core: 2. Of those that a mesh axis runs over, the one named last changes fastest.
Arguments:
- tokens: bfloat16 [1024, 3584], P('expert'), may hold values from -6 to 6
- expert_ids: int32 [1024, 8], P('expert'), may hold values from 0 to 15, all different within a row; in each aligned block of 64 rows (0 to 63, 64 to 127, ...) at most 32 rows name the same one
- weight_num: int32 [1024, 8], P('expert'), may hold values from 64 to 1023
- gate_proj: bfloat16 [16, 3584, 2048], P('expert', None, 'dp'), may hold values from -0.09375 to 0.09375
- up_proj: bfloat16 [16, 3584, 2048], P('expert', None, 'dp'), may hold values from -0.09375 to 0.09375
- down_proj: bfloat16 [16, 2048, 3584], P('expert', 'dp'), may hold values from -0.125 to 0.125
Outputs:
- combined: bfloat16 [1024, 3584], P('expert', 'dp')
Inputs may be any that keep to these rules, and one draw needn't show every extreme that they name: `expert_ids`: in the 64 rows of one device no expert is named by more than 32 rows, and some device has an expert named by exactly 32 of its rows.
All inputs are finite; a program needn't handle non-finite values.
Results may differ from a plain program's by a relative error of at most 0.015.
Values may be sent and summed in bfloat16 or wider, within the bound.
No kernel may reach another device: no remote copies, remote signals or barrier semaphores. Data moves between devices by JAX's collectives and lax.ppermute only.
A program may use at most 192 MiB of HBM per device.

v0:
```python
import jax
import jax.numpy as jnp
from jax import lax
from jax.sharding import PartitionSpec as P

ROOM = 8


def routing_table(block_ids, expert_total, capacity):
    row_count = block_ids.shape[0]
    top_count = block_ids.shape[1]
    flat_ids = block_ids.reshape(-1)
    onehot = (flat_ids[:, None] == jnp.arange(expert_total, dtype=jnp.int32)[None, :]).astype(
        jnp.int32
    )
    before = jnp.cumsum(onehot, axis=0) - onehot
    position = jnp.sum(before * onehot, axis=1)
    target = flat_ids * capacity + position
    owners = jnp.full((expert_total * capacity,), row_count * top_count, jnp.int32)
    owners = owners.at[target].set(jnp.arange(row_count * top_count, dtype=jnp.int32))
    return (target, owners)


def local(tokens, expert_ids, weight_num, gate_proj, up_proj, down_proj):
    experts = lax.axis_size("expert")
    row_count, top_count = expert_ids.shape
    feature_width = tokens.shape[1]
    capacity = max(ROOM, (row_count * top_count + experts - 1) // experts)
    target, owners = routing_table(expert_ids, experts, capacity)
    usable = owners < row_count * top_count
    source_row = jnp.where(usable, owners // top_count, 0)
    outgoing = jnp.where(usable[:, None], tokens[source_row], jnp.zeros((), tokens.dtype))
    outgoing = outgoing.reshape(experts, capacity, feature_width)
    gate_share = gate_proj[0]
    up_share = up_proj[0]
    down_share = down_proj[0]
    block_rows = lax.all_to_all(outgoing, "expert", split_axis=0, concat_axis=0, tiled=True)
    flat_rows = block_rows.reshape(-1, feature_width)
    gate_out = jnp.dot(flat_rows, gate_share, preferred_element_type=jnp.float32)
    up_out = jnp.dot(flat_rows, up_share, preferred_element_type=jnp.float32)
    hidden = (jax.nn.silu(gate_out) * up_out).astype(jnp.bfloat16)
    share_out = jnp.dot(hidden, down_share, preferred_element_type=jnp.float32).astype(jnp.bfloat16)
    partial_value = share_out.reshape(block_rows.shape[0], block_rows.shape[1], feature_width)
    weights = weight_num.astype(jnp.float32) / 1024.0
    summed = lax.psum_scatter(partial_value, "dp", scatter_dimension=2, tiled=True).astype(
        jnp.float32
    )
    returned = lax.all_to_all(
        summed.astype(jnp.bfloat16), "expert", split_axis=0, concat_axis=0, tiled=True
    ).astype(summed.dtype)
    quarter_width = returned.shape[2]
    picked = returned.reshape(experts * capacity, quarter_width)[target].reshape(
        row_count, top_count, quarter_width
    )
    combined = jnp.sum(picked * weights[:, :, None], axis=1)
    return combined.astype(jnp.bfloat16)


def solution(mesh):
    placed = (
        P("expert", None),
        P("expert", None),
        P("expert", None),
        P("expert", None, "dp"),
        P("expert", None, "dp"),
        P("expert", "dp", None),
    )
    return jax.shard_map(
        local, mesh=mesh, in_specs=placed, out_specs=P("expert", "dp"), check_vma=False
    )
```

profile of v0, /device:TPU:0, one launch (start us, length us, event | category | flops | bytes accessed | tf_op | source)
XLA Modules:
  0.0 243.4 jit_solution(5895719573418907979)
XLA Ops:
  6.5 0.0 copy-start
  6.5 0.0 reduce-scatter.2.cloned.1.call-start
  6.5 0.8 copy.9
  7.4 0.1 eq.29
  7.5 0.1 eq.25
  7.5 0.7 broadcast_multiply_fusion
  8.2 1.1 reduce-window.6
  9.4 0.2 slice_reduce_fusion
  9.7 0.1 copy.8
  9.7 0.1 mul.36
  9.8 0.1 fusion.16
  10.0 2.4 %scatter_custom_fusion = s32[512]{0:T(512)S(1)} fusion(s32[512]{0:T(512)S(1)} %bitcast.52, s32[512]{0:T(512)S(1)} %iota.11, s32[]{:T(128)} %constant.26.clone.1), kind=kCustom, calls=%fused_computation.39 | custom fusion | bytes 2052 | tf_op jit(solution)/shard_map/scatter | solution.py:20
  12.4 0.1 broadcast_in_dim.24
  12.5 0.0 copy-done
  12.5 4.2 %gather_fusion = bf16[512,3584]{1,0:T(8,128)(2,1)} fusion(bf16[64,3584]{1,0:T(8,128)(2,1)S(1)} %copy-done, s32[1024]{0:T(1024)S(1)} %pad_clamp_fusion.1), kind=kCustom, calls=%fused_computation | custom fusion | bytes 7342080 | tf_op jit(solution)/shard_map/gather | solution.py:32
  16.7 2.3 broadcast_select_fusion
  19.0 0.0 copy-start.3
  19.1 88.5 %all_to_all.10 = bf16[16,32,3584]{2,1,0:T(8,128)(2,1)S(1)} all-to-all(bf16[16,32,3584]{2,1,0:T(8,128)(2,1)S(1)} %broadcast_select_fusion), channel_id=1, replica_groups=mesh['dp'=2,'expert'=16] {'expert'}, dimensions={0} | all-to-all | bytes 7340032 | tf_op jit(solution)/shard_map/all_to_all | solution.py:37
  107.5 0.0 copy-start.1
  107.5 1.8 copy-done.1
  109.4 0.0 copy-done.3
  109.4 5.5 %fusion.2 = f32[512,1024]{1,0:T(8,128)} fusion(bf16[512,3584]{1,0:T(8,128)(2,1)S(1)} %bitcast.50, bf16[1,3584,1024]{2,1,0:T(8,128)(2,1)S(1)} %copy-done.3), kind=kOutput, calls=%fused_computation.5 | convolution fusion | flops 3758096384 | bytes 13107200 | tf_op jit(solution)/shard_map/dot_general | solution.py:40
  114.8 16.6 %fusion.6 = bf16[512,3584]{1,0:T(8,128)(2,1)} fusion(bf16[1,1024,3584]{2,1,0:T(8,128)(2,1)} %param.11, f32[512,1024]{1,0:T(8,128)} %fusion.2, bf16[512,3584]{1,0:T(8,128)(2,1)} %bitcast.51, bf16[1,3584,1024]{2,1,0:T(8,128)(2,1)} %param.9), kind=kOutput, calls=%fused_computation.9 | convolution fusion | flops 7521173504 | bytes 24117248 | tf_op jit(solution)/shard_map/dot_general | solution.py:42
  131.5 0.0 reduce-scatter.2.cloned.1.call-update
  131.5 49.8 %reduce-scatter.2.cloned.1.call-done = bf16[16,32,1792]{2,1,0:T(8,128)(2,1)} async-done(((bf16[16,32,3584]{2,1,0:T(8,128)(2,1)}), bf16[16,32,1792]{2,1,0:T(8,128)(2,1)}) %reduce-scatter.2.cloned.1.call-update) | async-done | bytes 1835024 | tf_op jit(solution)/shard_map/reduce_scatter | solution.py:45
  181.3 5.6 %all-to-all-start.1 = ((bf16[16,32,1792]{2,1,0:T(8,128)(2,1)}), bf16[16,32,1792]{2,1,0:T(8,128)(2,1)S(1)}, u32[]{:S(2)}, u32[]{:S(2)}) async-start(bf16[16,32,1792]{2,1,0:T(8,128)(2,1)} %reduce-scatter.2.cloned.1.call-done), calls=%async_computation.2 | async-start | bytes 3670016 | tf_op jit(solution)/shard_map/all_to_all | solution.py:48
  186.9 0.0 copy-done.2
  187.0 0.1 copy.12
  187.0 36.4 %all-to-all-done.1 = bf16[16,32,1792]{2,1,0:T(8,128)(2,1)S(1)} async-done(((bf16[16,32,1792]{2,1,0:T(8,128)(2,1)}), bf16[16,32,1792]{2,1,0:T(8,128)(2,1)S(1)}, u32[]{:S(2)}, u32[]{:S(2)}) %all-to-all-start.1) | async-done | bytes 1835040 | tf_op jit(solution)/shard_map/all_to_all | solution.py:48
  223.5 2.2 bitcast_convert_fusion
  225.6 7.0 %gather_fusion.1 = f32[512,1792]{1,0:T(8,128)} fusion(f32[512,1792]{1,0:T(8,128)} %bitcast_convert_fusion, s32[1024]{0:T(1024)S(1)} %pad_clamp_fusion), kind=kCustom, calls=%fused_computation.1 | custom fusion | bytes 7342080 | tf_op jit(solution)/shard_map/gather | solution.py:52
  232.6 3.9 %fusion.9 = bf16[64,1792]{1,0:T(8,128)(2,1)} fusion(f32[512,1792]{1,0:T(8,128)} %gather_fusion.1, f32[64,8]{1,0:T(8,128)S(1)} %copy.12), kind=kLoop, calls=%fused_computation.11 | loop fusion | flops 1720320 | bytes 3901440 | tf_op jit(solution)/shard_map/reduce_sum | solution.py:55
  (11 shorter events, 0.1 us)
Async XLA Ops:
  6.5 6.0 %copy-start = (bf16[64,3584]{1,0:T(8,128)(2,1)S(1)}, bf16[64,3584]{1,0:T(8,128)(2,1)}, u32[]{:S(2)}) copy-start(bf16[64,3584]{1,0:T(8,128)(2,1)} %param.6) | copy-start | bytes 1376260
  6.5 174.8 %reduce-scatter.2.cloned.1.call-start = ((), (), s32[]{:S(2)}) async-start(), calls=%async_computation.3 | async-start | bytes 5505024 | tf_op jit(solution)/shard_map/reduce_scatter | solution.py:45
  19.0 90.3 %copy-start.3 = (bf16[1,3584,1024]{2,1,0:T(8,128)(2,1)S(1)}, bf16[1,3584,1024]{2,1,0:T(8,128)(2,1)}, u32[]{:S(2)}) copy-start(bf16[1,3584,1024]{2,1,0:T(8,128)(2,1)} %param.10) | copy-start | bytes 22020100
  107.5 1.8 copy-start.1
  131.5 55.5 %copy-start.2 = (s32[64,8]{0,1:T(8,128)S(1)}, s32[64,8]{0,1:T(8,128)}, u32[]{:S(2)}) copy-start(s32[64,8]{0,1:T(8,128)} %param.8) | copy-start | bytes 6148
  181.3 42.2 %all-to-all-start.1 = ((bf16[16,32,1792]{2,1,0:T(8,128)(2,1)}), bf16[16,32,1792]{2,1,0:T(8,128)(2,1)S(1)}, u32[]{:S(2)}, u32[]{:S(2)}) async-start(bf16[16,32,1792]{2,1,0:T(8,128)(2,1)} %reduce-scatter.2.cloned.1.call-done), calls=%async_computation.2 | async-start | bytes 3670016 | tf_op jit(solution)/shard_map/all_to_all | solution.py:48
Sparse Core Ops, SparseCore 0:
  131.6 49.6 reduce-scatter.1
where the time goes:
time: 248 us; the launch traced here: 243 us
  blocking collectives  88.5 us (36%)
  waiting for transfers between devices  86.2 us (35%)
  matrix products  22.1 us (9%)
  local copies, waits for them, and re-layouts  17 us (7%)
  between operations  13.5 us (5%)
  other arithmetic  10.5 us (4%)
  starting transfers between devices  5.62 us (2%)
    all_to_all x1, blocking collectives, local(): lax.all_to_all(outgoing, 'expert', split_axis=0, concat_axis=0, tiled=True)  88.5 us
    reduce_scatter x1, waiting for transfers between devices, local(): lax.psum_scatter(partial_value, 'dp', scatter_dimension=2, tiled=True)  49.8 us
    all_to_all x1, waiting for transfers between devices, local(): lax.all_to_all(summed.astype(jnp.bfloat16), 'expert', split_axis=0, conca...  36.4 us
    dot_general x1, matrix products, local(): jnp.dot(hidden, down_share, preferred_element_type=jnp.float32)  16.6 us
    gather x1, local copies, waits for them, and re-layouts, local(): returned.reshape(experts * capacity, quarter_width)[target]  7 us
    all_to_all x1, starting transfers between devices, local(): lax.all_to_all(summed.astype(jnp.bfloat16), 'expert', split_axis=0, conca...  5.62 us
    dot_general x1, matrix products, local(): up_out = jnp.dot(flat_rows, up_share, preferred_element_type=jnp.float32)  5.48 us
  transfers between devices with their start and end apart: 2, of which 2 were waited for; matrix products, arithmetic and copies ran while one was open for 0% of the time, Pallas kernels for 0%

commit v1 on v0

v1 whole, which is shorter than its diff:
```python
import jax
import jax.numpy as jnp
from jax import lax
from jax.experimental import pallas as pl
from jax.experimental.pallas import tpu as pltpu
from jax.sharding import PartitionSpec as P

ROOM = 8
BF = jnp.bfloat16
F32 = jnp.float32


def routing_table(block_ids, expert_total, capacity):
    row_count = block_ids.shape[0]
    top_count = block_ids.shape[1]
    flat_ids = block_ids.reshape(-1)
    onehot = (flat_ids[:, None] == jnp.arange(expert_total, dtype=jnp.int32)[None, :]).astype(
        jnp.int32
    )
    before = jnp.cumsum(onehot, axis=0) - onehot
    position = jnp.sum(before * onehot, axis=1)
    target = flat_ids * capacity + position
    owners = jnp.full((expert_total * capacity,), row_count * top_count, jnp.int32)
    owners = owners.at[target].set(jnp.arange(row_count * top_count, dtype=jnp.int32))
    return (target, owners)


def any_mesh(tokens, expert_ids, weight_num, gate_proj, up_proj, down_proj):
    experts = lax.axis_size("expert")
    row_count, top_count = expert_ids.shape
    feature_width = tokens.shape[1]
    capacity = max(ROOM, (row_count * top_count + experts - 1) // experts)
    target, owners = routing_table(expert_ids, experts, capacity)
    usable = owners < row_count * top_count
    source_row = jnp.where(usable, owners // top_count, 0)
    outgoing = jnp.where(usable[:, None], tokens[source_row], jnp.zeros((), tokens.dtype))
    outgoing = outgoing.reshape(experts, capacity, feature_width)
    block_rows = lax.all_to_all(outgoing, "expert", split_axis=0, concat_axis=0, tiled=True)
    flat_rows = block_rows.reshape(-1, feature_width)
    gate_out = jnp.dot(flat_rows, gate_proj[0], preferred_element_type=F32)
    up_out = jnp.dot(flat_rows, up_proj[0], preferred_element_type=F32)
    hidden = (jax.nn.silu(gate_out) * up_out).astype(BF)
    share_out = jnp.dot(hidden, down_proj[0], preferred_element_type=F32).astype(BF)
    partial_value = share_out.reshape(block_rows.shape[0], block_rows.shape[1], feature_width)
    weights = weight_num.astype(F32) / 1024.0
    summed = lax.psum_scatter(partial_value, "dp", scatter_dimension=2, tiled=True)
    returned = lax.all_to_all(summed, "expert", split_axis=0, concat_axis=0, tiled=True)
    part_width = returned.shape[2]
    picked = returned.astype(F32).reshape(experts * capacity, part_width)[target].reshape(
        row_count, top_count, part_width
    )
    return jnp.sum(picked * weights[:, :, None], axis=1).astype(BF)


NZ, NY, NC = 4, 2, 2
KJ = [(k, j) for k in range(NZ) for j in range(NY)]


def swap_expert(value, flip):
    pairs = [(i, i ^ flip) for i in range(NZ * NY * NC)]
    return lax.ppermute(value, "expert", pairs)


def swap_z(value, k):
    return swap_expert(value, k * NY * NC)


def swap_y(value):
    return swap_expert(value, NC)


def swap_core(value):
    return swap_expert(value, 1)


def swap_x(value):
    return lax.ppermute(value, "dp", [(0, 1), (1, 0)])


def gate_up_kernel(x_ref, rows_m, rows_f, gate_m, gate_f, up_m, up_f, weight, out):
    del x_ref
    a, b = rows_m[...], rows_f[...]
    gate = jnp.dot(a, gate_m[0], preferred_element_type=F32)
    gate += jnp.dot(b, gate_f[0], preferred_element_type=F32)
    up = jnp.dot(a, up_m[0], preferred_element_type=F32)
    up += jnp.dot(b, up_f[0], preferred_element_type=F32)
    out[...] = (gate / (1.0 + jnp.exp(-gate)) * up * weight[...]).astype(BF)


def gate_up(x, rows_m, rows_f, gate, up, weight):
    rows, half = rows_m.shape
    width = gate.shape[2]
    tile = 256
    whole = pl.BlockSpec((rows, half), lambda n, x: (0, 0))
    mine = pl.BlockSpec((1, half, tile), lambda n, x: (0, x[0], n))
    far = pl.BlockSpec((1, half, tile), lambda n, x: (0, 1 - x[0], n))
    return pl.pallas_call(
        gate_up_kernel,
        out_shape=jax.ShapeDtypeStruct((rows, width), BF),
        grid_spec=pltpu.PrefetchScalarGridSpec(
            num_scalar_prefetch=1,
            grid=(width // tile,),
            in_specs=[whole, whole, mine, far, mine, far, pl.BlockSpec((rows, 1), lambda n, x: (0, 0))],
            out_specs=pl.BlockSpec((rows, tile), lambda n, x: (0, n)),
        ),
        compiler_params=pltpu.CompilerParams(vmem_limit_bytes=48 << 20),
        cost_estimate=pl.CostEstimate(
            flops=8 * rows * half * width, bytes_accessed=8 * half * width, transcendentals=rows * width
        ),
    )(x, rows_m, rows_f, gate, gate, up, up, weight)


def down_kernel(hidden, down, near, away):
    value = jnp.dot(hidden[...], down[0], preferred_element_type=F32).astype(BF)
    rows = near.shape[0]
    near[...] = value[:rows]
    away[...] = value[rows:]


def down(hidden, weights):
    rows, depth = hidden.shape
    width = weights.shape[2]
    tile = 512
    out = jax.ShapeDtypeStruct((rows // 2, width), BF)
    return pl.pallas_call(
        down_kernel,
        out_shape=(out, out),
        grid=(width // tile,),
        in_specs=[
            pl.BlockSpec((rows, depth), lambda n: (0, 0)),
            pl.BlockSpec((1, depth, tile), lambda n: (0, 0, n)),
        ],
        out_specs=[pl.BlockSpec((rows // 2, tile), lambda n: (0, n))] * 2,
        compiler_params=pltpu.CompilerParams(vmem_limit_bytes=48 << 20),
        cost_estimate=pl.CostEstimate(
            flops=2 * rows * depth * width, bytes_accessed=2 * depth * width, transcendentals=0
        ),
    )(hidden, weights)


def slots(table, expert, room):
    top = table.shape[2] // 2
    named = table[:, :, :top] == expert
    numerator = jnp.sum(jnp.where(named, table[:, :, top:], 0), axis=2)
    chosen = jnp.any(named, axis=2)
    rows = table.shape[1]
    before = jnp.arange(rows)[:, None] < jnp.arange(rows)[None, :]
    place = jnp.sum(jnp.where(chosen[:, :, None] & before[None], 1, 0), axis=1)
    onehot = (place[:, None, :] == jnp.arange(room)[None, :, None]) & chosen[:, None, :]
    weight = jnp.sum(jnp.where(onehot, numerator[:, None, :], 0), axis=2).astype(F32) / 1024.0
    return onehot, weight.reshape(-1, 1)


def diagonal(onehot):
    count, room, rows = onehot.shape
    same = jnp.eye(count, dtype=bool)
    return (onehot[:, :, None, :] & same[:, None, :, None]).astype(BF).reshape(count * room, count * rows)


def add(*values):
    total = values[0].astype(F32)
    for value in values[1:]:
        total = total + value.astype(F32)
    return total.astype(BF)


def block_mesh(tokens, expert_ids, weight_num, gate_proj, up_proj, down_proj):
    x = lax.axis_index("dp")
    me = lax.axis_index("expert")
    rows, width = tokens.shape
    half = width // 2
    room = rows * expert_ids.shape[1] // (NZ * NY * NC)

    info = lax.all_gather(jnp.concatenate([expert_ids, weight_num], axis=1), "expert")
    order = jnp.array([k * NY * NC + j * NC for k, j in KJ], jnp.int32) ^ me
    near_table, away_table = info[order], info[order ^ 1]
    near_mine, near_weight = slots(near_table, me, room)
    near_other, _ = slots(near_table, me ^ 1, room)
    _, away_weight = slots(away_table, me, room)
    pick_mine, pick_other = diagonal(near_mine), diagonal(near_other)
    weight = jnp.concatenate([near_weight, away_weight], axis=0)

    mine = lax.dynamic_slice_in_dim(tokens, x * half, half, 1)
    far = lax.dynamic_slice_in_dim(tokens, (1 - x) * half, half, 1)
    got_m, got_f = {(0, 0): mine}, {(0, 0): far}
    for k in range(1, NZ):
        got_m[k, 0] = swap_z(mine, k)
    got_m[0, 1] = swap_y(mine)
    got_f[0, 1] = swap_y(far)
    for k in range(1, NZ):
        got_m[k, 1] = swap_y(got_m[k, 0])
        got_f[k, 0] = swap_x(got_m[k, 0])
    for k in range(1, NZ):
        got_f[k, 1] = swap_x(got_m[k, 1])

    def chosen(got):
        blocks = jnp.concatenate([got[kj] for kj in KJ], axis=0)
        keep = jnp.dot(pick_mine, blocks, preferred_element_type=F32).astype(BF)
        give = jnp.dot(pick_other, blocks, preferred_element_type=F32).astype(BF)
        return jnp.concatenate([keep, swap_core(give)], axis=0)

    rows_m = chosen(got_m)
    rows_f = chosen(got_f)
    hidden = gate_up(x.reshape(1), rows_m, rows_f, gate_proj, up_proj, weight)
    near, away = down(hidden, down_proj)
    back = swap_core(away)

    spread = jnp.dot(pick_mine.T, near, preferred_element_type=F32)
    spread = (spread + jnp.dot(pick_other.T, back, preferred_element_type=F32)).astype(BF)
    spread = spread.reshape(NZ, NY, rows, width)
    spread_m = lax.dynamic_slice_in_dim(spread, x * half, half, 3)
    spread_f = lax.dynamic_slice_in_dim(spread, (1 - x) * half, half, 3)
    quarter = half // 2
    first, second = slice(0, quarter), slice(quarter, half)
    columns = []
    summed = {}
    for part in (slice(2, 4), slice(0, 2)):
        a = add(spread_m[part, :, :, first], swap_x(spread_f[part, :, :, first]))
        b_m = add(spread_m[part, 0, :, second], swap_y(spread_m[part, 1, :, second]))
        b_f = add(spread_f[part, 0, :, second], swap_y(spread_f[part, 1, :, second]))
        a = add(a[:, 0], swap_y(a[:, 1]))
        b = add(b_m, swap_x(b_f))
        for i, k in enumerate(range(part.start, part.stop)):
            summed[k, 0], summed[k, 1] = a[i], b[i]
    for q in range(2):
        terms = [summed[0, q]] + [swap_z(summed[k, q], k) for k in (2, 3, 1)]
        columns.append(add(*terms))
    return jnp.concatenate(columns, axis=1)


def solution(mesh):
    placed = (
        P("expert", None),
        P("expert", None),
        P("expert", None),
        P("expert", None, "dp"),
        P("expert", None, "dp"),
        P("expert", "dp", None),
    )
    blocked = mesh.shape["dp"] == 2 and mesh.shape["expert"] == NZ * NY * NC
    return jax.shard_map(
        block_mesh if blocked else any_mesh,
        mesh=mesh,
        in_specs=placed,
        out_specs=P("expert", "dp"),
        check_vma=False,
    )
```

time: 248 us -> 171 us (0.69); the launches traced: 243 us -> 171 us
  blocking collectives: 88.5 us -> 25.3 us
  starting transfers between devices: 5.62 us -> 38.1 us
  waiting for transfers between devices: 86.2 us -> 58.2 us
  Pallas kernels: 0 us -> 19.7 us
  between operations: 13.5 us -> 0.43 us
  matrix products: 22.1 us -> 11.3 us
  other arithmetic: 10.5 us -> 5 us
  local copies, waits for them, and re-layouts: 17 us -> 12.6 us
    all_to_all x1 -> x0, blocking collectives: 88.5 us -> none  [local(): lax.all_to_all(outgoing, 'expert', split_axis=0, concat_axis=0, tiled=True)]
    ppermute x0 -> x33, waiting for transfers between devices: none -> 58.2 us  [the longest x10 30.7 us: swap_x(): return lax.ppermute(value, 'dp', [(0, 1), (1, 0)])]
    reduce_scatter x1 -> x0, waiting for transfers between devices: 49.8 us -> none  [local(): lax.psum_scatter(partial_value, 'dp', scatter_dimension=2, tiled=True)]
    ppermute x0 -> x33, starting transfers between devices: none -> 38.1 us  [the longest x23 27.5 us: swap_expert(): return lax.ppermute(value, 'expert', pairs)]
    all_to_all x1 -> x0, waiting for transfers between devices: 36.4 us -> none  [local(): lax.all_to_all(summed.astype(jnp.bfloat16), 'expert', split_axis=0, conca...]
    all_gather x0 -> x1, blocking collectives: none -> 25.3 us  [block_mesh(): lax.all_gather(jnp.concatenate([expert_ids, weight_num], axis=1), 'expert')]
    pallas_call x0 -> x2, Pallas kernels: none -> 19.7 us  [the longest x1 10.9 us: gate_up(): pl.pallas_call(gate_up_kernel, out_shape=jax.ShapeDtypeStruct((rows, widt...]
    dot_general x2 -> x6, matrix products: 22.1 us -> 11.3 us  [the longest x2 4.66 us: chosen(): give = jnp.dot(pick_other, blocks, preferred_element_type=F32).astype(BF)]
  transfers between devices with their start and end apart: 2 -> 33, of which waited for: 2 -> 13; matrix products, arithmetic and copies ran while one was open for 0% -> 13% of each run, Pallas kernels for 0% -> 0%
where the time goes in v1:
time: 171 us
  waiting for transfers between devices  58.2 us (34%)
  starting transfers between devices  38.1 us (22%)
  blocking collectives  25.3 us (15%)
  Pallas kernels  19.7 us (12%)
  local copies, waits for them, and re-layouts  12.6 us (7%)
  matrix products  11.3 us (7%)
  other arithmetic  5 us (3%)
    ppermute x10, waiting for transfers between devices, swap_x(): return lax.ppermute(value, 'dp', [(0, 1), (1, 0)])  30.7 us
    ppermute x23, starting transfers between devices, swap_expert(): return lax.ppermute(value, 'expert', pairs)  27.5 us
    ppermute x23, waiting for transfers between devices, swap_expert(): return lax.ppermute(value, 'expert', pairs)  27.5 us
    all_gather x1, blocking collectives, block_mesh(): lax.all_gather(jnp.concatenate([expert_ids, weight_num], axis=1), 'expert')  25.3 us
    pallas_call x1, Pallas kernels, gate_up(): pl.pallas_call(gate_up_kernel, out_shape=jax.ShapeDtypeStruct((rows, widt...  10.9 us
    ppermute x10, starting transfers between devices, swap_x(): return lax.ppermute(value, 'dp', [(0, 1), (1, 0)])  10.6 us
    unnamed x15, local copies, waits for them, and re-layouts  8.99 us
    pallas_call x1, Pallas kernels, down(): pl.pallas_call(down_kernel, out_shape=(out, out), grid=(width // tile,),...  8.84 us
  transfers between devices with their start and end apart: 33, of which 13 were waited for; matrix products, arithmetic and copies ran while one was open for 13% of the time, Pallas kernels for 0%

profile of v1, /device:TPU:0, one launch (start us, length us, event | category | flops | bytes accessed | tf_op | source)
XLA Modules:
  0.0 170.7 jit_solution(14637473636367968214)
XLA Ops:
  0.0 1.8 %constant_dynamic-update-slice_fusion.15 = (bf16[512,1792]{1,0:T(8,128)(2,1)S(1)}, bf16[64,1792]{1,0:T(8,128)(2,1)S(1)}, bf16[512,1792]{1,0:T(8,128)(2,1)}, bf16[64,1792]{1,0:T(8,128)(2,1)S(1)}) fusion(bf16[64,3584]{1,0:T(8,128)(2,1)} %param.7, s32[]{:T(128)S(6)} %select_n.42, s32[]{:T(128)S(6)} %select_n.40), kind=kLoop, calls=%fused_computation.87 | loop fusion | bytes 1376264
  1.8 3.0 %collective-permute-start.1 = (bf16[64,1792]{1,0:T(8,128)(2,1)S(1)}, bf16[64,1792]{1,0:T(8,128)(2,1)}, u32[]{:S(2)}, u32[]{:S(2)}) collective-permute-start(bf16[64,1792]{1,0:T(8,128)(2,1)S(1)} %get-tuple-element.31), channel_id=1, source_target_pairs={{0,4},{1,5},{2,6},{3,7},{4,0},{5,1},{6,2},{7,3},{8,12},{9,13},{10,... | collective-permute-start | bytes 688136 | tf_op jit(solution)/shard_map/ppermute | solution.py:61
  4.8 2.6 %collective-permute-start.3 = (bf16[64,1792]{1,0:T(8,128)(2,1)S(1)}, bf16[64,1792]{1,0:T(8,128)(2,1)}, u32[]{:S(2)}, u32[]{:S(2)}) collective-permute-start(bf16[64,1792]{1,0:T(8,128)(2,1)S(1)} %get-tuple-element.31), channel_id=1, source_target_pairs={{0,8},{1,9},{2,10},{3,11},{4,12},{5,13},{6,14},{7,15},{8,0},{9,1},... | collective-permute-start | bytes 688136 | tf_op jit(solution)/shard_map/ppermute | solution.py:61
  7.4 1.7 %collective-permute-start = (bf16[64,1792]{1,0:T(8,128)(2,1)S(1)}, bf16[64,1792]{1,0:T(8,128)(2,1)}, u32[]{:S(2)}, u32[]{:S(2)}) collective-permute-start(bf16[64,1792]{1,0:T(8,128)(2,1)S(1)} %get-tuple-element.31), channel_id=1, source_target_pairs={{0,2},{1,3},{2,0},{3,1},{4,6},{5,7},{6,4},{7,5},{8,10},{9,11},{10,... | collective-permute-start | bytes 688136 | tf_op jit(solution)/shard_map/ppermute | solution.py:61
  10.2 25.3 %all-gather.1 = s32[16,64,16]{1,2,0:T(8,128)S(1)} all-gather(s32[1,64,16]{1,2,0:T(8,128)S(1)} %add_bitcast_fusion), channel_id=2, replica_groups=mesh['dp'=2,'expert'=16] {'expert'}, dimensions={0}, use_global_device_ids=true | all-gather | bytes 69632 | tf_op jit(solution)/shard_map/all_gather | solution.py:174
  38.6 1.5 collective-permute-start.9
  41.5 1.6 constant_dynamic-update-slice_fusion.6
  43.2 1.6 constant_dynamic-update-slice_fusion.5
  46.0 1.5 collective-permute-start.13
  49.7 1.6 constant_dynamic-update-slice_fusion.3
  51.3 2.4 %collective-permute-done.4 = bf16[64,1792]{1,0:T(8,128)(2,1)S(1)} collective-permute-done((bf16[64,1792]{1,0:T(8,128)(2,1)}, bf16[64,1792]{1,0:T(8,128)(2,1)S(1)}, u32[]{:S(2)}, u32[]{:S(2)}) %collective-permute-start.4) | collective-permute-done | bytes 229408 | tf_op jit(solution)/shard_map/ppermute | solution.py:61
  55.2 2.6 %collective-permute-done.6 = bf16[64,1792]{1,0:T(8,128)(2,1)S(1)} collective-permute-done((bf16[64,1792]{1,0:T(8,128)(2,1)S(1)}, bf16[64,1792]{1,0:T(8,128)(2,1)S(1)}, u32[]{:S(2)}, u32[]{:S(2)}) %collective-permute-start.6) | collective-permute-done | bytes 229408 | tf_op jit(solution)/shard_map/ppermute | solution.py:61
  58.5 3.1 %convolution_convert_fusion.2 = bf16[256,1792]{1,0:T(8,128)(2,1)} fusion(pred[256,512]{1,0:T(32,128)(4,1)S(1)} %and.122, bf16[512,1792]{1,0:T(8,128)(2,1)} %constant_dynamic-update-slice_fusion), kind=kOutput, calls=%fused_computation.5 | convolution fusion | flops 470220800 | bytes 2883584 | tf_op jit(solution)/shard_map/dot_general | solution.py:199
  63.6 6.4 %collective-permute-done.10 = bf16[64,1792]{1,0:T(8,128)(2,1)S(1)} collective-permute-done((bf16[64,1792]{1,0:T(8,128)(2,1)S(1)}, bf16[64,1792]{1,0:T(8,128)(2,1)S(1)}, u32[]{:S(2)}, u32[]{:S(2)}) %collective-permute-start.10) | collective-permute-done | bytes 229408 | tf_op jit(solution)/shard_map/ppermute | solution.py:77
  70.6 4.3 %collective-permute-done.12 = bf16[64,1792]{1,0:T(8,128)(2,1)S(1)} collective-permute-done((bf16[64,1792]{1,0:T(8,128)(2,1)S(1)}, bf16[64,1792]{1,0:T(8,128)(2,1)S(1)}, u32[]{:S(2)}, u32[]{:S(2)}) %collective-permute-start.12) | collective-permute-done | bytes 229408 | tf_op jit(solution)/shard_map/ppermute | solution.py:77
  74.9 4.5 %collective-permute-done.14 = bf16[64,1792]{1,0:T(8,128)(2,1)S(1)} collective-permute-done((bf16[64,1792]{1,0:T(8,128)(2,1)S(1)}, bf16[64,1792]{1,0:T(8,128)(2,1)S(1)}, u32[]{:S(2)}, u32[]{:S(2)}) %collective-permute-start.14) | collective-permute-done | bytes 229408 | tf_op jit(solution)/shard_map/ppermute | solution.py:77
  79.4 1.6 convolution_convert_fusion
  81.7 2.2 %convolution_convert_fusion.3 = bf16[256,1792]{1,0:T(8,128)(2,1)S(1)} fusion(pred[256,512]{1,0:T(32,128)(4,1)S(1)} %and.115, bf16[512,1792]{1,0:T(8,128)(2,1)} %constant_dynamic-update-slice_fusion), kind=kOutput, calls=%fused_computation.6 | convolution fusion | flops 470220800 | bytes 2883584 | tf_op jit(solution)/shard_map/dot_general | solution.py:198
  85.9 10.9 %shard_map.73.hidden = bf16[512,1024]{1,0:T(8,128)(2,1)S(1)} custom-call(s32[1]{0:T(128)} %bitcast.1.x_ref, bf16[512,1792]{1,0:T(8,128)(2,1)S(1)} %pad_maximum_fusion.rows_m, bf16[512,1792]{1,0:T(8,128)(2,1)S(1)} %pad_maximum_fusion.1.rows_f, bf16[1,3584,1024]{2,1,0:T(8,128)(2,1)} %gate_f.1, bf16[1,3584,1024]{2,1,0:T(8,128)(2,1)} %gate_f.1, ...), custom_call_target="tpu_custom_call" | custom-call | flops 7516192768 | bytes 14680064 | tf_op jit(solution)/shard_map/pallas_call | solution.py:97
  96.8 8.8 %shard_map.74 = (bf16[256,3584]{1,0:T(8,128)(2,1)S(1)}, bf16[256,3584]{1,0:T(8,128)(2,1)}) custom-call(bf16[512,1024]{1,0:T(8,128)(2,1)S(1)} %shard_map.73.hidden, bf16[1,1024,3584]{2,1,0:T(8,128)(2,1)} %down.1), custom_call_target="tpu_custom_call" | custom-call | flops 3758096384 | bytes 7340032 | tf_op jit(solution)/shard_map/pallas_call | solution.py:125
  107.4 2.6 %collective-permute-done.16 = bf16[256,3584]{1,0:T(8,128)(2,1)} collective-permute-done((bf16[256,3584]{1,0:T(8,128)(2,1)}, bf16[256,3584]{1,0:T(8,128)(2,1)}, u32[]{:S(2)}, u32[]{:S(2)}) %collective-permute-start.16) | collective-permute-done | bytes 1835040 | tf_op jit(solution)/shard_map/ppermute | solution.py:61
  110.0 2.7 %add_convert_fusion = bf16[512,3584]{1,0:T(8,128)(2,1)S(1)} fusion(f32[512,3584]{1,0:T(8,128)S(1)} %fusion.17, pred[256,512]{1,0:T(32,128)(4,1)S(1)} %and.122, bf16[256,3584]{1,0:T(8,128)(2,1)} %collective-permute-done.16), kind=kOutput, calls=%fused_computation.2 | convolution fusion | flops 943194112 | bytes 12976128 | tf_op jit(solution)/shard_map/dot_general | solution.py:209
  118.1 3.2 %collective-permute-done.28 = bf16[2,64,896]{2,1,0:T(8,128)(2,1)S(1)} collective-permute-done((bf16[2,64,896]{2,1,0:T(8,128)(2,1)S(1)}, bf16[2,64,896]{2,1,0:T(8,128)(2,1)S(1)}, u32[]{:S(2)}, u32[]{:S(2)}) %collective-permute-start.28) | collective-permute-done | bytes 229408 | tf_op jit(solution)/shard_map/ppermute | solution.py:61
  122.1 5.2 %collective-permute-done.19 = bf16[2,2,64,896]{3,2,0,1:T(8,128)(2,1)S(1)} collective-permute-done((bf16[2,2,64,896]{3,2,0,1:T(8,128)(2,1)S(1)}, bf16[2,2,64,896]{3,2,0,1:T(8,128)(2,1)S(1)}, u32[]{:S(2)}, u32[]{:S(2)}) %collective-permute-start.19) | collective-permute-done | bytes 458784 | tf_op jit(solution)/shard_map/ppermute | solution.py:77
  128.6 8.5 %collective-permute-done.17 = bf16[2,2,64,896]{3,2,0,1:T(8,128)(2,1)S(1)} collective-permute-done((bf16[2,2,64,896]{3,2,0,1:T(8,128)(2,1)S(1)}, bf16[2,2,64,896]{3,2,0,1:T(8,128)(2,1)S(1)}, u32[]{:S(2)}, u32[]{:S(2)}) %collective-permute-start.17) | collective-permute-done | bytes 458784 | tf_op jit(solution)/shard_map/ppermute | solution.py:77
  139.5 1.8 %collective-permute-done.29 = bf16[2,64,896]{2,1,0:T(8,128)(2,1)S(1)} collective-permute-done((bf16[2,64,896]{2,1,0:T(8,128)(2,1)S(1)}, bf16[2,64,896]{2,1,0:T(8,128)(2,1)S(1)}, u32[]{:S(2)}, u32[]{:S(2)}) %collective-permute-start.29) | collective-permute-done | bytes 229408 | tf_op jit(solution)/shard_map/ppermute | solution.py:77
  142.6 4.2 %collective-permute-start.30 = (bf16[64,896]{1,0:T(8,128)(2,1)S(1)}, bf16[64,896]{1,0:T(8,128)(2,1)S(1)}, u32[]{:S(2)}, u32[]{:S(2)}) collective-permute-start(bf16[64,896]{1,0:T(8,128)(2,1)S(1)} %get-tuple-element.34), channel_id=1, source_target_pairs={{0,8},{1,9},{2,10},{3,11},{4,12},{5,13},{6,14},{7,15},{8,0},{9,1},... | collective-permute-start | bytes 344072 | tf_op jit(solution)/shard_map/ppermute | solution.py:61
  146.9 3.4 %collective-permute-start.31 = (bf16[64,896]{1,0:T(8,128)(2,1)S(1)}, bf16[64,896]{1,0:T(8,128)(2,1)S(1)}, u32[]{:S(2)}, u32[]{:S(2)}) collective-permute-start(bf16[64,896]{1,0:T(8,128)(2,1)S(1)} %get-tuple-element.35), channel_id=1, source_target_pairs={{0,12},{1,13},{2,14},{3,15},{4,8},{5,9},{6,10},{7,11},{8,4},{9,5},... | collective-permute-start | bytes 344072 | tf_op jit(solution)/shard_map/ppermute | solution.py:61
  150.4 2.4 %collective-permute-start.21 = (bf16[64,896]{1,0:T(8,128)(2,1)S(1)}, bf16[64,896]{1,0:T(8,128)(2,1)S(1)}, u32[]{:S(2)}, u32[]{:S(2)}) collective-permute-start(bf16[64,896]{1,0:T(8,128)(2,1)S(1)} %get-tuple-element.32), channel_id=1, source_target_pairs={{0,8},{1,9},{2,10},{3,11},{4,12},{5,13},{6,14},{7,15},{8,0},{9,1},... | collective-permute-start | bytes 344072 | tf_op jit(solution)/shard_map/ppermute | solution.py:61
  152.8 1.5 collective-permute-start.22
  154.5 10.7 %collective-permute-done.21 = bf16[64,896]{1,0:T(8,128)(2,1)S(1)} collective-permute-done((bf16[64,896]{1,0:T(8,128)(2,1)S(1)}, bf16[64,896]{1,0:T(8,128)(2,1)S(1)}, u32[]{:S(2)}, u32[]{:S(2)}) %collective-permute-start.21) | collective-permute-done | bytes 114720 | tf_op jit(solution)/shard_map/ppermute | solution.py:61
  165.3 4.7 %collective-permute-done.32 = bf16[64,896]{1,0:T(8,128)(2,1)S(1)} collective-permute-done((bf16[64,896]{1,0:T(8,128)(2,1)S(1)}, bf16[64,896]{1,0:T(8,128)(2,1)S(1)}, u32[]{:S(2)}, u32[]{:S(2)}) %collective-permute-start.32) | collective-permute-done | bytes 114720 | tf_op jit(solution)/shard_map/ppermute | solution.py:61
  (107 shorter events, 30.3 us)
Async XLA Ops:
  1.8 36.9 %collective-permute-start.1 = (bf16[64,1792]{1,0:T(8,128)(2,1)S(1)}, bf16[64,1792]{1,0:T(8,128)(2,1)}, u32[]{:S(2)}, u32[]{:S(2)}) collective-permute-start(bf16[64,1792]{1,0:T(8,128)(2,1)S(1)} %get-tuple-element.31), channel_id=1, source_target_pairs={{0,4},{1,5},{2,6},{3,7},{4,0},{5,1},{6,2},{7,3},{8,12},{9,13},{10,... | collective-permute-start | bytes 688136 | tf_op jit(solution)/shard_map/ppermute | solution.py:61
  4.8 35.3 %collective-permute-start.3 = (bf16[64,1792]{1,0:T(8,128)(2,1)S(1)}, bf16[64,1792]{1,0:T(8,128)(2,1)}, u32[]{:S(2)}, u32[]{:S(2)}) collective-permute-start(bf16[64,1792]{1,0:T(8,128)(2,1)S(1)} %get-tuple-element.31), channel_id=1, source_target_pairs={{0,8},{1,9},{2,10},{3,11},{4,12},{5,13},{6,14},{7,15},{8,0},{9,1},... | collective-permute-start | bytes 688136 | tf_op jit(solution)/shard_map/ppermute | solution.py:61
  7.4 38.6 %collective-permute-start.5 = (bf16[64,1792]{1,0:T(8,128)(2,1)S(1)}, bf16[64,1792]{1,0:T(8,128)(2,1)S(1)}, u32[]{:S(2)}, u32[]{:S(2)}) collective-permute-start(bf16[64,1792]{1,0:T(8,128)(2,1)S(1)} %get-tuple-element.31), channel_id=1, source_target_pairs={{0,12},{1,13},{2,14},{3,15},{4,8},{5,9},{6,10},{7,11},{8,4},{9,5},... | collective-permute-start | bytes 688136 | tf_op jit(solution)/shard_map/ppermute | solution.py:61
  7.4 33.6 %collective-permute-start = (bf16[64,1792]{1,0:T(8,128)(2,1)S(1)}, bf16[64,1792]{1,0:T(8,128)(2,1)}, u32[]{:S(2)}, u32[]{:S(2)}) collective-permute-start(bf16[64,1792]{1,0:T(8,128)(2,1)S(1)} %get-tuple-element.31), channel_id=1, source_target_pairs={{0,2},{1,3},{2,0},{3,1},{4,6},{5,7},{6,4},{7,5},{8,10},{9,11},{10,... | collective-permute-start | bytes 688136 | tf_op jit(solution)/shard_map/ppermute | solution.py:61
  9.1 35.7 %collective-permute-start.8 = (bf16[64,1792]{1,0:T(8,128)(2,1)S(1)}, bf16[64,1792]{1,0:T(8,128)(2,1)S(1)}, u32[]{:S(2)}, u32[]{:S(2)}) collective-permute-start(bf16[64,1792]{1,0:T(8,128)(2,1)S(1)} %get-tuple-element.17), channel_id=1, source_target_pairs={{0,2},{1,3},{2,0},{3,1},{4,6},{5,7},{6,4},{7,5},{8,10},{9,11},{10,... | collective-permute-start | bytes 688136 | tf_op jit(solution)/shard_map/ppermute | solution.py:61
  38.6 23.5 %collective-permute-start.9 = (bf16[64,1792]{1,0:T(8,128)(2,1)}, bf16[64,1792]{1,0:T(8,128)(2,1)S(1)}, u32[]{:S(2)}, u32[]{:S(2)}) collective-permute-start(bf16[64,1792]{1,0:T(8,128)(2,1)} %collective-permute-done.1), channel_id=1, source_target_pairs={{0,16},{16,0},{1,17},{17,1},{2,18},{18,2},{3,19},{19,3},{4,20},{20... | collective-permute-start | bytes 688136 | tf_op jit(solution)/shard_map/ppermute | solution.py:77
  40.1 8.7 %collective-permute-start.2 = (bf16[64,1792]{1,0:T(8,128)(2,1)}, bf16[64,1792]{1,0:T(8,128)(2,1)S(1)}, u32[]{:S(2)}, u32[]{:S(2)}) collective-permute-start(bf16[64,1792]{1,0:T(8,128)(2,1)} %collective-permute-done.1), channel_id=1, source_target_pairs={{0,2},{1,3},{2,0},{3,1},{4,6},{5,7},{6,4},{7,5},{8,10},{9,11},{10,... | collective-permute-start | bytes 688136 | tf_op jit(solution)/shard_map/ppermute | solution.py:61
  41.0 29.6 %collective-permute-start.11 = (bf16[64,1792]{1,0:T(8,128)(2,1)}, bf16[64,1792]{1,0:T(8,128)(2,1)S(1)}, u32[]{:S(2)}, u32[]{:S(2)}) collective-permute-start(bf16[64,1792]{1,0:T(8,128)(2,1)} %collective-permute-done.3), channel_id=1, source_target_pairs={{0,16},{16,0},{1,17},{17,1},{2,18},{18,2},{3,19},{19,3},{4,20},{20... | collective-permute-start | bytes 688136 | tf_op jit(solution)/shard_map/ppermute | solution.py:77
  44.8 8.9 %collective-permute-start.4 = (bf16[64,1792]{1,0:T(8,128)(2,1)}, bf16[64,1792]{1,0:T(8,128)(2,1)S(1)}, u32[]{:S(2)}, u32[]{:S(2)}) collective-permute-start(bf16[64,1792]{1,0:T(8,128)(2,1)} %collective-permute-done.3), channel_id=1, source_target_pairs={{0,2},{1,3},{2,0},{3,1},{4,6},{5,7},{6,4},{7,5},{8,10},{9,11},{10,... | collective-permute-start | bytes 688136 | tf_op jit(solution)/shard_map/ppermute | solution.py:61
  46.0 28.9 %collective-permute-start.13 = (bf16[64,1792]{1,0:T(8,128)(2,1)S(1)}, bf16[64,1792]{1,0:T(8,128)(2,1)S(1)}, u32[]{:S(2)}, u32[]{:S(2)}) collective-permute-start(bf16[64,1792]{1,0:T(8,128)(2,1)S(1)} %collective-permute-done.5), channel_id=1, source_target_pairs={{0,16},{16,0},{1,17},{17,1},{2,18},{18,2},{3,19},{19,3},{4,20},{20... | collective-permute-start | bytes 688136 | tf_op jit(solution)/shard_map/ppermute | solution.py:77
  48.8 8.9 %collective-permute-start.6 = (bf16[64,1792]{1,0:T(8,128)(2,1)S(1)}, bf16[64,1792]{1,0:T(8,128)(2,1)S(1)}, u32[]{:S(2)}, u32[]{:S(2)}) collective-permute-start(bf16[64,1792]{1,0:T(8,128)(2,1)S(1)} %collective-permute-done.5), channel_id=1, source_target_pairs={{0,2},{1,3},{2,0},{3,1},{4,6},{5,7},{6,4},{7,5},{8,10},{9,11},{10,... | collective-permute-start | bytes 688136 | tf_op jit(solution)/shard_map/ppermute | solution.py:61
  61.6 22.9 %collective-permute-start.7 = (bf16[256,1792]{1,0:T(8,128)(2,1)}, bf16[256,1792]{1,0:T(8,128)(2,1)S(1)}, u32[]{:S(2)}, u32[]{:S(2)}) collective-permute-start(bf16[256,1792]{1,0:T(8,128)(2,1)} %convolution_convert_fusion.2), channel_id=1, source_target_pairs={{0,1},{1,0},{2,3},{3,2},{4,5},{5,4},{6,7},{7,6},{8,9},{9,8},{10,11... | collective-permute-start | bytes 2752520 | tf_op jit(solution)/shard_map/ppermute | solution.py:61
  61.6 8.4 %collective-permute-start.10 = (bf16[64,1792]{1,0:T(8,128)(2,1)S(1)}, bf16[64,1792]{1,0:T(8,128)(2,1)S(1)}, u32[]{:S(2)}, u32[]{:S(2)}) collective-permute-start(bf16[64,1792]{1,0:T(8,128)(2,1)S(1)} %collective-permute-done.2), channel_id=1, source_target_pairs={{0,16},{16,0},{1,17},{17,1},{2,18},{18,2},{3,19},{19,3},{4,20},{20... | collective-permute-start | bytes 688136 | tf_op jit(solution)/shard_map/ppermute | solution.py:77
  62.1 12.7 %collective-permute-start.12 = (bf16[64,1792]{1,0:T(8,128)(2,1)S(1)}, bf16[64,1792]{1,0:T(8,128)(2,1)S(1)}, u32[]{:S(2)}, u32[]{:S(2)}) collective-permute-start(bf16[64,1792]{1,0:T(8,128)(2,1)S(1)} %collective-permute-done.4), channel_id=1, source_target_pairs={{0,16},{16,0},{1,17},{17,1},{2,18},{18,2},{3,19},{19,3},{4,20},{20... | collective-permute-start | bytes 688136 | tf_op jit(solution)/shard_map/ppermute | solution.py:77
  70.0 9.4 %collective-permute-start.14 = (bf16[64,1792]{1,0:T(8,128)(2,1)S(1)}, bf16[64,1792]{1,0:T(8,128)(2,1)S(1)}, u32[]{:S(2)}, u32[]{:S(2)}) collective-permute-start(bf16[64,1792]{1,0:T(8,128)(2,1)S(1)} %collective-permute-done.6), channel_id=1, source_target_pairs={{0,16},{16,0},{1,17},{17,1},{2,18},{18,2},{3,19},{19,3},{4,20},{20... | collective-permute-start | bytes 688136 | tf_op jit(solution)/shard_map/ppermute | solution.py:77
  105.7 4.3 %collective-permute-start.16 = (bf16[256,3584]{1,0:T(8,128)(2,1)}, bf16[256,3584]{1,0:T(8,128)(2,1)}, u32[]{:S(2)}, u32[]{:S(2)}) collective-permute-start(bf16[256,3584]{1,0:T(8,128)(2,1)} %get-tuple-element.8), channel_id=1, source_target_pairs={{0,1},{1,0},{2,3},{3,2},{4,5},{5,4},{6,7},{7,6},{8,9},{9,8},{10,11... | collective-permute-start | bytes 5505032 | tf_op jit(solution)/shard_map/ppermute | solution.py:61
  112.8 8.5 %collective-permute-start.28 = (bf16[2,64,896]{2,1,0:T(8,128)(2,1)S(1)}, bf16[2,64,896]{2,1,0:T(8,128)(2,1)S(1)}, u32[]{:S(2)}, u32[]{:S(2)}) collective-permute-start(bf16[2,64,896]{2,1,0:T(8,128)(2,1)S(1)} %get-tuple-element.29), channel_id=1, source_target_pairs={{0,2},{1,3},{2,0},{3,1},{4,6},{5,7},{6,4},{7,5},{8,10},{9,11},{10,... | collective-permute-start | bytes 688136 | tf_op jit(solution)/shard_map/ppermute | solution.py:61
  113.9 13.4 %collective-permute-start.19 = (bf16[2,2,64,896]{3,2,0,1:T(8,128)(2,1)S(1)}, bf16[2,2,64,896]{3,2,0,1:T(8,128)(2,1)S(1)}, u32[]{:S(2)}, u32[]{:S(2)}) collective-permute-start(bf16[2,2,64,896]{3,2,0,1:T(8,128)(2,1)S(1)} %copy.25), channel_id=1, source_target_pairs={{0,16},{16,0},{1,17},{17,1},{2,18},{18,2},{3,19},{19,3},{4,20},{20... | collective-permute-start | bytes 1376264 | tf_op jit(solution)/shard_map/ppermute | solution.py:77
  115.2 22.0 %collective-permute-start.17 = (bf16[2,2,64,896]{3,2,0,1:T(8,128)(2,1)S(1)}, bf16[2,2,64,896]{3,2,0,1:T(8,128)(2,1)S(1)}, u32[]{:S(2)}, u32[]{:S(2)}) collective-permute-start(bf16[2,2,64,896]{3,2,0,1:T(8,128)(2,1)S(1)} %copy.23), channel_id=1, source_target_pairs={{0,16},{16,0},{1,17},{17,1},{2,18},{18,2},{3,19},{19,3},{4,20},{20... | collective-permute-start | bytes 1376264 | tf_op jit(solution)/shard_map/ppermute | solution.py:77
  116.1 22.5 %collective-permute-start.25 = (bf16[2,64,896]{2,1,0:T(8,128)(2,1)S(1)}, bf16[2,64,896]{2,1,0:T(8,128)(2,1)S(1)}, u32[]{:S(2)}, u32[]{:S(2)}) collective-permute-start(bf16[2,64,896]{2,1,0:T(8,128)(2,1)S(1)} %get-tuple-element.27), channel_id=1, source_target_pairs={{0,2},{1,3},{2,0},{3,1},{4,6},{5,7},{6,4},{7,5},{8,10},{9,11},{10,... | collective-permute-start | bytes 688136 | tf_op jit(solution)/shard_map/ppermute | solution.py:61
  117.4 22.0 %collective-permute-start.27 = (bf16[2,64,896]{2,1,0:T(8,128)(2,1)S(1)}, bf16[2,64,896]{2,1,0:T(8,128)(2,1)S(1)}, u32[]{:S(2)}, u32[]{:S(2)}) collective-permute-start(bf16[2,64,896]{2,1,0:T(8,128)(2,1)S(1)} %get-tuple-element.26), channel_id=1, source_target_pairs={{0,2},{1,3},{2,0},{3,1},{4,6},{5,7},{6,4},{7,5},{8,10},{9,11},{10,... | collective-permute-start | bytes 688136 | tf_op jit(solution)/shard_map/ppermute | solution.py:61
  121.3 31.5 %collective-permute-start.24 = (bf16[2,64,896]{2,1,0:T(8,128)(2,1)S(1)}, bf16[2,64,896]{2,1,0:T(8,128)(2,1)S(1)}, u32[]{:S(2)}, u32[]{:S(2)}) collective-permute-start(bf16[2,64,896]{2,1,0:T(8,128)(2,1)S(1)} %get-tuple-element.28), channel_id=1, source_target_pairs={{0,2},{1,3},{2,0},{3,1},{4,6},{5,7},{6,4},{7,5},{8,10},{9,11},{10,... | collective-permute-start | bytes 688136 | tf_op jit(solution)/shard_map/ppermute | solution.py:61
  127.4 13.9 %collective-permute-start.29 = (bf16[2,64,896]{2,1,0:T(8,128)(2,1)S(1)}, bf16[2,64,896]{2,1,0:T(8,128)(2,1)S(1)}, u32[]{:S(2)}, u32[]{:S(2)}) collective-permute-start(bf16[2,64,896]{2,1,0:T(8,128)(2,1)S(1)} %fusion), channel_id=1, source_target_pairs={{0,16},{16,0},{1,17},{17,1},{2,18},{18,2},{3,19},{19,3},{4,20},{20... | collective-permute-start | bytes 688136 | tf_op jit(solution)/shard_map/ppermute | solution.py:77
  137.2 9.7 %collective-permute-start.20 = (bf16[2,64,896]{2,1,0:T(8,128)(2,1)S(1)}, bf16[2,64,896]{2,1,0:T(8,128)(2,1)S(1)}, u32[]{:S(2)}, u32[]{:S(2)}) collective-permute-start(bf16[2,64,896]{2,1,0:T(8,128)(2,1)S(1)} %slice_bitcast_fusion), channel_id=1, source_target_pairs={{0,2},{1,3},{2,0},{3,1},{4,6},{5,7},{6,4},{7,5},{8,10},{9,11},{10,... | collective-permute-start | bytes 688136 | tf_op jit(solution)/shard_map/ppermute | solution.py:61
  138.7 11.7 %collective-permute-start.18 = (bf16[2,64,896]{2,1,0:T(8,128)(2,1)S(1)}, bf16[2,64,896]{2,1,0:T(8,128)(2,1)S(1)}, u32[]{:S(2)}, u32[]{:S(2)}) collective-permute-start(bf16[2,64,896]{2,1,0:T(8,128)(2,1)S(1)} %slice_bitcast_fusion.2), channel_id=1, source_target_pairs={{0,2},{1,3},{2,0},{3,1},{4,6},{5,7},{6,4},{7,5},{8,10},{9,11},{10,... | collective-permute-start | bytes 688136 | tf_op jit(solution)/shard_map/ppermute | solution.py:61
  141.4 13.0 %collective-permute-start.26 = (bf16[2,64,896]{2,1,0:T(8,128)(2,1)S(1)}, bf16[2,64,896]{2,1,0:T(8,128)(2,1)S(1)}, u32[]{:S(2)}, u32[]{:S(2)}) collective-permute-start(bf16[2,64,896]{2,1,0:T(8,128)(2,1)S(1)} %get-tuple-element.25), channel_id=1, source_target_pairs={{0,16},{16,0},{1,17},{17,1},{2,18},{18,2},{3,19},{19,3},{4,20},{20... | collective-permute-start | bytes 688136 | tf_op jit(solution)/shard_map/ppermute | solution.py:77
  142.6 22.6 %collective-permute-start.30 = (bf16[64,896]{1,0:T(8,128)(2,1)S(1)}, bf16[64,896]{1,0:T(8,128)(2,1)S(1)}, u32[]{:S(2)}, u32[]{:S(2)}) collective-permute-start(bf16[64,896]{1,0:T(8,128)(2,1)S(1)} %get-tuple-element.34), channel_id=1, source_target_pairs={{0,8},{1,9},{2,10},{3,11},{4,12},{5,13},{6,14},{7,15},{8,0},{9,1},... | collective-permute-start | bytes 344072 | tf_op jit(solution)/shard_map/ppermute | solution.py:61
  146.9 18.4 %collective-permute-start.31 = (bf16[64,896]{1,0:T(8,128)(2,1)S(1)}, bf16[64,896]{1,0:T(8,128)(2,1)S(1)}, u32[]{:S(2)}, u32[]{:S(2)}) collective-permute-start(bf16[64,896]{1,0:T(8,128)(2,1)S(1)} %get-tuple-element.35), channel_id=1, source_target_pairs={{0,12},{1,13},{2,14},{3,15},{4,8},{5,9},{6,10},{7,11},{8,4},{9,5},... | collective-permute-start | bytes 344072 | tf_op jit(solution)/shard_map/ppermute | solution.py:61
  150.4 14.8 %collective-permute-start.21 = (bf16[64,896]{1,0:T(8,128)(2,1)S(1)}, bf16[64,896]{1,0:T(8,128)(2,1)S(1)}, u32[]{:S(2)}, u32[]{:S(2)}) collective-permute-start(bf16[64,896]{1,0:T(8,128)(2,1)S(1)} %get-tuple-element.32), channel_id=1, source_target_pairs={{0,8},{1,9},{2,10},{3,11},{4,12},{5,13},{6,14},{7,15},{8,0},{9,1},... | collective-permute-start | bytes 344072 | tf_op jit(solution)/shard_map/ppermute | solution.py:61
  152.8 12.3 %collective-permute-start.22 = (bf16[64,896]{1,0:T(8,128)(2,1)S(1)}, bf16[64,896]{1,0:T(8,128)(2,1)S(1)}, u32[]{:S(2)}, u32[]{:S(2)}) collective-permute-start(bf16[64,896]{1,0:T(8,128)(2,1)S(1)} %get-tuple-element.33), channel_id=1, source_target_pairs={{0,12},{1,13},{2,14},{3,15},{4,8},{5,9},{6,10},{7,11},{8,4},{9,5},... | collective-permute-start | bytes 344072 | tf_op jit(solution)/shard_map/ppermute | solution.py:61
  154.4 10.8 %collective-permute-start.23 = (bf16[64,896]{1,0:T(8,128)(2,1)S(1)}, bf16[64,896]{1,0:T(8,128)(2,1)S(1)}, u32[]{:S(2)}, u32[]{:S(2)}) collective-permute-start(bf16[64,896]{1,0:T(8,128)(2,1)S(1)} %slice_bitcast_fusion.8), channel_id=1, source_target_pairs={{0,4},{1,5},{2,6},{3,7},{4,0},{5,1},{6,2},{7,3},{8,12},{9,13},{10,... | collective-permute-start | bytes 344072 | tf_op jit(solution)/shard_map/ppermute | solution.py:61
  165.2 4.8 %collective-permute-start.32 = (bf16[64,896]{1,0:T(8,128)(2,1)S(1)}, bf16[64,896]{1,0:T(8,128)(2,1)S(1)}, u32[]{:S(2)}, u32[]{:S(2)}) collective-permute-start(bf16[64,896]{1,0:T(8,128)(2,1)S(1)} %slice_bitcast_fusion.4), channel_id=1, source_target_pairs={{0,4},{1,5},{2,6},{3,7},{4,0},{5,1},{6,2},{7,3},{8,12},{9,13},{10,... | collective-permute-start | bytes 344072 | tf_op jit(solution)/shard_map/ppermute | solution.py:61
  (1 other events, 3.6 us)

commit v2 on v0

v2 whole, which is shorter than its diff:
```python
import jax
import jax.numpy as jnp
from jax import lax
from jax.experimental import pallas as pl
from jax.experimental.pallas import tpu as pltpu
from jax.sharding import PartitionSpec as P

ROOM = 8
BF = jnp.bfloat16
F32 = jnp.float32


def routing_table(block_ids, expert_total, capacity):
    row_count = block_ids.shape[0]
    top_count = block_ids.shape[1]
    flat_ids = block_ids.reshape(-1)
    onehot = (flat_ids[:, None] == jnp.arange(expert_total, dtype=jnp.int32)[None, :]).astype(
        jnp.int32
    )
    before = jnp.cumsum(onehot, axis=0) - onehot
    position = jnp.sum(before * onehot, axis=1)
    target = flat_ids * capacity + position
    owners = jnp.full((expert_total * capacity,), row_count * top_count, jnp.int32)
    owners = owners.at[target].set(jnp.arange(row_count * top_count, dtype=jnp.int32))
    return (target, owners)


def any_mesh(tokens, expert_ids, weight_num, gate_proj, up_proj, down_proj):
    experts = lax.axis_size("expert")
    row_count, top_count = expert_ids.shape
    feature_width = tokens.shape[1]
    capacity = max(ROOM, (row_count * top_count + experts - 1) // experts)
    target, owners = routing_table(expert_ids, experts, capacity)
    usable = owners < row_count * top_count
    source_row = jnp.where(usable, owners // top_count, 0)
    outgoing = jnp.where(usable[:, None], tokens[source_row], jnp.zeros((), tokens.dtype))
    outgoing = outgoing.reshape(experts, capacity, feature_width)
    block_rows = lax.all_to_all(outgoing, "expert", split_axis=0, concat_axis=0, tiled=True)
    flat_rows = block_rows.reshape(-1, feature_width)
    gate_out = jnp.dot(flat_rows, gate_proj[0], preferred_element_type=F32)
    up_out = jnp.dot(flat_rows, up_proj[0], preferred_element_type=F32)
    hidden = (jax.nn.silu(gate_out) * up_out).astype(BF)
    share_out = jnp.dot(hidden, down_proj[0], preferred_element_type=F32).astype(BF)
    partial_value = share_out.reshape(block_rows.shape[0], block_rows.shape[1], feature_width)
    weights = weight_num.astype(F32) / 1024.0
    summed = lax.psum_scatter(partial_value, "dp", scatter_dimension=2, tiled=True)
    returned = lax.all_to_all(summed, "expert", split_axis=0, concat_axis=0, tiled=True)
    part_width = returned.shape[2]
    picked = returned.astype(F32).reshape(experts * capacity, part_width)[target].reshape(
        row_count, top_count, part_width
    )
    return jnp.sum(picked * weights[:, :, None], axis=1).astype(BF)


NZ, NY, NC = 4, 2, 2
TABLE = 128
SMALL = 16
KJ = [(k, j) for k in range(NZ) for j in range(NY)]


def swap_expert(value, flip, name):
    pairs = [(i, i ^ flip) for i in range(NZ * NY * NC)]
    with jax.named_scope(name):
        return lax.ppermute(value, "expert", pairs)


def swap_z(value, k, name):
    return swap_expert(value, k * NY * NC, name)


def swap_y(value, name):
    return swap_expert(value, NC, name)


def swap_core(value, name):
    return swap_expert(value, 1, name)


def swap_x(value, name):
    with jax.named_scope(name):
        return lax.ppermute(value, "dp", [(0, 1), (1, 0)])


COST = pl.CostEstimate(flops=1, bytes_accessed=1, transcendentals=0)


def call(kernel, out, ins):
    spec = [
        pl.BlockSpec(memory_space=pltpu.SMEM if v.dtype == jnp.int32 else pltpu.VMEM) for v in ins
    ]
    return pl.pallas_call(
        kernel,
        out_shape=out,
        in_specs=spec,
        out_specs=jax.tree.map(lambda _: pl.BlockSpec(memory_space=pltpu.VMEM), out),
        compiler_params=pltpu.CompilerParams(vmem_limit_bytes=SMALL << 20),
        cost_estimate=COST,
    )(*ins)


def prepare(x, tokens, ids, numerators):
    rows, width = tokens.shape
    half = width // 2

    def kernel(x_ref, tokens_ref, ids_ref, numerators_ref, mine, whole):
        side = x_ref[0]
        near = tokens_ref[:, pl.ds(pl.multiple_of(side * half, 128), half)]
        mine[:, :half] = near
        whole[:, :half] = near
        whole[:, half + TABLE :] = tokens_ref[:, pl.ds(pl.multiple_of((1 - side) * half, 128), half)]
        column = lax.broadcasted_iota(jnp.int32, (TABLE, rows), 0)
        expert = jnp.where(column < TABLE // 2, column, column - TABLE // 2)
        total = jnp.zeros((TABLE, rows), jnp.int32)
        for k in range(ids_ref.shape[0]):
            total += jnp.where(expert == ids_ref[pl.ds(k, 1)], numerators_ref[pl.ds(k, 1)], 0)
        high = lax.shift_right_logical(total, 5)
        code = jnp.where(column < TABLE // 2, high, total - high * 32)
        table = code.astype(F32).T.astype(BF)
        mine[:, half:] = table
        whole[:, half : half + TABLE] = table

    out = (
        jax.ShapeDtypeStruct((rows, half + TABLE), BF),
        jax.ShapeDtypeStruct((rows, width + TABLE), BF),
    )
    vmem = pl.BlockSpec(memory_space=pltpu.VMEM)
    return pl.pallas_call(
        kernel,
        out_shape=out,
        in_specs=[pl.BlockSpec(memory_space=pltpu.SMEM), vmem, vmem, vmem],
        out_specs=(vmem, vmem),
        cost_estimate=COST,
    )(x.reshape(1), tokens, ids.T, numerators.T)


def lookup(table, expert):
    row = lax.broadcasted_iota(jnp.int32, (TABLE, TABLE), 0)
    whose = jnp.where(lax.broadcasted_iota(jnp.int32, (TABLE, TABLE), 1) == 0, expert, expert + 1 - 2 * (expert % 2))
    code = jnp.where(row == whose, 32.0, 0.0) + jnp.where(row == whose + TABLE // 2, 1.0, 0.0)
    return jnp.dot(table, code.astype(BF), preferred_element_type=F32)


def select(me, room, half, blocks):
    rows, full = blocks[0].shape
    count = len(blocks)

    def kernel(me_ref, *refs):
        keep, give, put_ref = refs[-3:]
        mine = me_ref[0]
        before = lax.broadcasted_iota(jnp.int32, (rows, rows), 1) < lax.broadcasted_iota(
            jnp.int32, (rows, rows), 0
        )
        before = jnp.where(before, 1.0, 0.0).astype(BF)
        slot = lax.broadcasted_iota(jnp.int32, (rows, 2 * room), 1)
        first = slot < room
        for b, ref in enumerate(refs[:count]):
            chosen = jnp.where(lookup(ref[:, half : half + TABLE], mine) > 0, 1.0, 0.0)
            place = jnp.dot(before, chosen.astype(BF), preferred_element_type=F32)
            want = jnp.where(first, place[:, :1], place[:, 1:2] + room)
            here = jnp.where(first, chosen[:, :1], chosen[:, 1:2])
            put = jnp.where(want == slot.astype(F32), here, 0.0)
            put_ref[b] = put.astype(BF)
            got = jnp.dot(put.T.astype(BF), ref[...], preferred_element_type=F32).astype(BF)
            keep[pl.ds(b * room, room)] = got[:room]
            give[pl.ds(b * room, room)] = got[room:]

    out = jax.ShapeDtypeStruct((count * room, full), BF)
    put = jax.ShapeDtypeStruct((count, rows, 2 * room), BF)
    return call(kernel, (out, out, put), [me.reshape(1), *blocks])


def select_far(put, blocks):
    rows, full = blocks[0].shape
    half = full - TABLE
    room = put.shape[2] // 2

    def kernel(put_ref, *refs):
        keep, give = refs[-2:]
        for b, ref in enumerate(refs[:-2]):
            pick = put_ref[b].astype(F32).T.astype(BF)
            got = jnp.dot(pick, ref[:, :half], preferred_element_type=F32).astype(BF)
            keep[pl.ds(b * room, room)] = got[:room]
            give[pl.ds(b * room, room)] = got[room:]

    out = jax.ShapeDtypeStruct((len(blocks) * room, half), BF)
    return call(kernel, (out, out), [put, *blocks])


def touch(*weights):
    def kernel(*refs):
        total = jnp.zeros((16, 128), F32)
        for ref in refs[:-1]:
            total += ref[0, :16, :128].astype(F32)
        refs[-1][...] = total

    return call(kernel, jax.ShapeDtypeStruct((16, 128), F32), weights)


def gate_up(scalars, keep, got, gate, up, part, first=()):
    rows = keep.shape[0]
    depth, width = gate.shape[1:]
    half = depth // 2
    tile = 256

    def kernel(scalar_ref, keep_ref, got_ref, gate_ref, up_ref, *refs):
        x = scalar_ref[0]
        near = pl.ds(pl.multiple_of(x * half, half), half)
        far = pl.ds(pl.multiple_of((1 - x) * half, half), half)
        both = lambda start, size: jnp.concatenate(
            [ref[:, start : start + size] for ref in (keep_ref, got_ref)], axis=0
        )
        if part == 2:
            table = jnp.concatenate([refs[2][...], refs[3][...]], axis=0)[:, half:]
        elif part == 0:
            table = both(half, TABLE)
        if part != 1:
            weight = lookup(table, scalar_ref[1])[:, :1] / 1024.0
        for n in range(width // tile):
            columns = pl.ds(n * tile, tile)

            def product(ref):
                if part == 1:
                    return jnp.dot(both(0, half), ref[0, near, columns], preferred_element_type=F32)
                if part == 2:
                    return jnp.dot(both(0, half), ref[0, far, columns], preferred_element_type=F32)
                value = jnp.dot(both(0, half), ref[0, near, columns], preferred_element_type=F32)
                return value + jnp.dot(
                    both(half + TABLE, half), ref[0, far, columns], preferred_element_type=F32
                )

            g, u = product(gate_ref), product(up_ref)
            if part == 1:
                refs[0][:, columns] = g
                refs[1][:, columns] = u
                continue
            if part == 2:
                g += refs[0][:, columns]
                u += refs[1][:, columns]
            refs[-1][:, columns] = (g / (1.0 + jnp.exp(-g)) * u * weight).astype(BF)

    shape = lambda kind: jax.ShapeDtypeStruct((2 * rows, width), kind)
    out = (shape(F32), shape(F32)) if part == 1 else shape(BF)
    return call(kernel, out, [scalars, keep, got, gate, up, *first])


def down(scalars, hidden, weights, quarter, *tokens):
    rows, depth = hidden.shape
    tile = weights.shape[2] // 4

    def kernel(scalar_ref, hidden_ref, down_ref, *refs):
        near, away = refs[-2:]
        x = scalar_ref[0]
        for n in range(2):
            side = x if n else 1 - x
            start = (2 * side + quarter) * tile
            weight = down_ref[0, :, pl.ds(pl.multiple_of(start, 128), tile)]
            value = jnp.dot(hidden_ref[...], weight, preferred_element_type=F32).astype(BF)
            near[n] = value[: rows // 2]
            away[n] = value[rows // 2 :]

    out = jax.ShapeDtypeStruct((2, rows // 2, tile), BF)
    return call(kernel, (out, out), [scalars, hidden, weights, *tokens])


def spread(put, near, back, quarter, split):
    rows, room = put.shape[1], put.shape[2] // 2
    width = near.shape[2]
    whole = jax.ShapeDtypeStruct((2, 2, rows, width), BF)
    part = jax.ShapeDtypeStruct((2, rows, width), BF)
    out = (part, part, whole) if split else (whole, whole)

    def kernel(put_ref, near_ref, back_ref, *refs):
        *give, keep = refs
        for h in range(2):
            for b, (k, j) in enumerate(KJ[:4]):
                place = pl.ds(b * room, room)
                value = jnp.concatenate([near_ref[h, place], back_ref[h, place]], axis=0)
                got = jnp.dot(put_ref[b], value, preferred_element_type=F32).astype(BF)
                stays, index = (h == 1, j) if quarter == 0 else (j == 0, h)
                if stays:
                    keep[k, index] = got
                elif split:
                    give[k][index] = got
                else:
                    give[0][k, index] = got

    return call(kernel, out, [put, near, back])


def in_order(values, earlier):
    return lax.optimization_barrier((*values, *earlier))[: len(values)]


def after(value, *earlier):
    return in_order((value,), earlier)[0]


def add(*values):
    total = values[0].astype(F32)
    for value in values[1:]:
        total = total + value.astype(F32)
    return total.astype(BF)


def block_mesh(tokens, expert_ids, weight_num, gate_proj, up_proj, down_proj):
    x = lax.axis_index("dp")
    me = lax.axis_index("expert")
    rows, width = tokens.shape
    half = width // 2
    room = rows * expert_ids.shape[1] // (NZ * NY * NC)

    scalars = jnp.stack([x, me])

    mine, whole = prepare(x, tokens, expert_ids, weight_num)
    w0y = swap_y(whole, "w0y")
    w1 = swap_z(whole, 1, "w1")
    m2 = swap_z(mine, 2, "m2")
    touched = touch(*in_order((gate_proj, up_proj, down_proj), (mine,)))
    w1, m2, w0y = in_order((w1, m2, w0y), (touched,))
    m2y = swap_y(m2, "m2y")
    f2 = swap_x(m2, "f2")
    m3 = swap_z(m2, 1, "m3")
    w1y = swap_y(after(w1, m3), "w1y")
    f3 = swap_x(m3, "f3")
    m3y = swap_y(m3, "m3y")
    f2y = swap_x(m2y, "f2y")
    f3y = swap_x(m3y, "f3y")

    keep, give, put_f = select(after(me, f2), room, half, [m2, m2y, m3, m3y])
    got = swap_core(give, "rows_m")
    first = gate_up(scalars, keep, got, gate_proj, up_proj, 1, ())
    keep_f, give_f = select_far(after(put_f, first[0]), [f2, f2y, f3, f3y])
    got_f = swap_core(give_f, "rows_f")
    keep_n, give, put_n = select(after(me, keep_f), room, half, [whole, w0y, w1, w1y])
    got_n = swap_core(give, "rows_n")
    hidden_f = gate_up(after(scalars, keep_n), keep_f, got_f, gate_proj, up_proj, 2, [*first, keep, got])
    near_a, away = down(scalars, hidden_f, down_proj, 0, touched)
    back = swap_core(away, "back_a")
    near_b, away = down(after(scalars, near_a), hidden_f, down_proj, 1)
    a2, a3, keep_a = spread(put_f, near_a, back, 0, True)
    back = swap_core(away, "back_b")
    b2, b3, keep_b = spread(after(put_f, keep_a), near_b, back, 1, True)
    hidden_n = gate_up(after(scalars, keep_b), keep_n, got_n, gate_proj, up_proj, 0)
    near_n, away = down(scalars, hidden_n, down_proj, 0)
    back_n = swap_core(away, "back_n")
    near_o, away = down(after(scalars, near_n), hidden_n, down_proj, 1)
    back_o = swap_core(away, "back_o")

    b3, a3 = swap_y(b3, "b3"), swap_x(a3, "a3")
    put_n = after(put_n, a3, b3)
    a3, b3 = add(keep_a[1], a3), add(keep_b[1], b3)
    n, keep_n = spread(put_n, near_n, back_n, 0, False)
    o, keep_o = spread(put_n, near_o, back_o, 1, False)
    a2, b2 = in_order((a2, b2), (a3, b3))
    n, o = in_order((n, o), (a3, b3))
    o, n = swap_y(o, "o"), swap_x(n, "n")
    b2, a2 = swap_y(b2, "b2"), swap_x(a2, "a2")
    p3, q3 = swap_y(a3[1], "p3"), swap_x(b3[0], "q3")
    a2, b2 = add(keep_a[0], a2), add(keep_b[0], b2)
    p2, q2 = swap_y(a2[1], "p2"), swap_x(b2[0], "q2")
    s3 = jnp.stack([add(a3[0], p3), add(b3[1], q3)])
    p2, q2 = in_order((p2, q2), (s3,))
    s3 = swap_z(s3, 3, "s3")
    s2 = jnp.stack([add(a2[0], p2), add(b2[1], q2)])
    n, o = in_order((n, o), (s2,))
    s2 = swap_z(s2, 2, "s2")
    n, o = add(keep_n, n), add(keep_o, o)
    np, nq = swap_y(n[:, 1], "np"), swap_x(o[:, 0], "nq")
    n = jnp.stack([add(n[:, 0], np), add(o[:, 1], nq)])
    s1 = swap_z(n[:, 1], 1, "s1")
    total = add(n[:, 0], s1, s2, s3)
    return jnp.concatenate([total[0], total[1]], axis=1)


def solution(mesh):
    placed = (
        P("expert", None),
        P("expert", None),
        P("expert", None),
        P("expert", None, "dp"),
        P("expert", None, "dp"),
        P("expert", "dp", None),
    )
    blocked = mesh.shape["dp"] == 2 and mesh.shape["expert"] == NZ * NY * NC
    return jax.shard_map(
        block_mesh if blocked else any_mesh,
        mesh=mesh,
        in_specs=placed,
        out_specs=P("expert", "dp"),
        check_vma=False,
    )
```

time: 248 us -> 125 us (0.50); the launches traced: 243 us -> 125 us
  blocking collectives: 88.5 us -> 0 us
  waiting for transfers between devices: 86.2 us -> 50.9 us
  Pallas kernels: 0 us -> 25.7 us
  starting transfers between devices: 5.62 us -> 30.7 us
  matrix products: 22.1 us -> 0 us
  between operations: 13.5 us -> 0.39 us
  other arithmetic: 10.5 us -> 1.71 us
    all_to_all x1 -> x0, blocking collectives: 88.5 us -> none  [local(): lax.all_to_all(outgoing, 'expert', split_axis=0, concat_axis=0, tiled=True)]
    ppermute x0 -> x33, waiting for transfers between devices: none -> 50.9 us  [the longest x23 31.4 us: swap_expert(): return lax.ppermute(value, 'expert', pairs)]
    reduce_scatter x1 -> x0, waiting for transfers between devices: 49.8 us -> none  [local(): lax.psum_scatter(partial_value, 'dp', scatter_dimension=2, tiled=True)]
    all_to_all x1 -> x0, waiting for transfers between devices: 36.4 us -> none  [local(): lax.all_to_all(summed.astype(jnp.bfloat16), 'expert', split_axis=0, conca...]
    ppermute x0 -> x33, starting transfers between devices: none -> 30.7 us  [the longest x23 20.4 us: swap_expert(): return lax.ppermute(value, 'expert', pairs)]
    pallas_call x0 -> x16, Pallas kernels: none -> 25.7 us  [the longest x15 23.7 us: call(): pl.pallas_call(kernel, out_shape=out, in_specs=spec, out_specs=jax.tree.m...]
    dot_general x2 -> x0, matrix products: 22.1 us -> none  [the longest x1 16.6 us: local(): jnp.dot(hidden, down_share, preferred_element_type=jnp.float32)]
    unnamed x9 -> x22, local copies, waits for them, and re-layouts: 2.67 us -> 15.4 us
  transfers between devices with their start and end apart: 2 -> 33, of which waited for: 2 -> 21; matrix products, arithmetic and copies ran while one was open for 0% -> 1% of each run, Pallas kernels for 0% -> 17%
where the time goes in v2:
time: 125 us
  waiting for transfers between devices  50.9 us (41%)
  starting transfers between devices  30.7 us (25%)
  Pallas kernels  25.7 us (21%)
  local copies, waits for them, and re-layouts  15.6 us (12%)
  other arithmetic  1.71 us (1%)
    ppermute x23, waiting for transfers between devices, swap_expert(): return lax.ppermute(value, 'expert', pairs)  31.4 us
    pallas_call x15, Pallas kernels, call(): pl.pallas_call(kernel, out_shape=out, in_specs=spec, out_specs=jax.tree.m...  23.7 us
    ppermute x23, starting transfers between devices, swap_expert(): return lax.ppermute(value, 'expert', pairs)  20.4 us
    ppermute x10, waiting for transfers between devices, swap_x(): return lax.ppermute(value, 'dp', [(0, 1), (1, 0)])  19.6 us
    unnamed x22, local copies, waits for them, and re-layouts  15.4 us
    ppermute x10, starting transfers between devices, swap_x(): return lax.ppermute(value, 'dp', [(0, 1), (1, 0)])  10.3 us
  transfers between devices with their start and end apart: 33, of which 21 were waited for; matrix products, arithmetic and copies ran while one was open for 1% of the time, Pallas kernels for 17%

profile of v2, /device:TPU:0, one launch (start us, length us, event | category | flops | bytes accessed | tf_op | source)
XLA Modules:
  0.0 125.0 jit_solution(10201164183950520833)
XLA Ops:
  0.0 2.0 %shard_map.64 = (bf16[64,1920]{1,0:T(8,128)(2,1)}, bf16[64,3712]{1,0:T(8,128)(2,1)}) custom-call(s32[1]{0:T(128)} %bitcast.x_ref, bf16[64,3584]{1,0:T(8,128)(2,1)} %tokens_ref.1, s32[8,64]{1,0:T(8,128)} %bitcast.91, s32[8,64]{1,0:T(8,128)} %bitcast.92), custom_call_target="tpu_custom_call" | custom-call | flops 1 | bytes 1 | tf_op jit(solution)/shard_map/pallas_call | solution.py:127
  2.0 3.0 %collective-permute-start.2 = (bf16[64,3712]{1,0:T(8,128)(2,1)}, bf16[64,3712]{1,0:T(8,128)(2,1)S(1)}, u32[]{:S(2)}, u32[]{:S(2)}) collective-permute-start(bf16[64,3712]{1,0:T(8,128)(2,1)} %get-tuple-element.59.refs_0_), channel_id=1, source_target_pairs={{0,2},{1,3},{2,0},{3,1},{4,6},{5,7},{6,4},{7,5},{8,10},{9,11},{10,... | collective-permute-start | bytes 1425416 | tf_op jit(solution)/shard_map/w0y/ppermute | solution.py:64
  6.6 2.6 %collective-permute-start.1 = (bf16[64,1920]{1,0:T(8,128)(2,1)}, bf16[64,1920]{1,0:T(8,128)(2,1)S(1)}, u32[]{:S(2)}, u32[]{:S(2)}) collective-permute-start(bf16[64,1920]{1,0:T(8,128)(2,1)} %get-tuple-element.60), channel_id=1, source_target_pairs={{0,8},{1,9},{2,10},{3,11},{4,12},{5,13},{6,14},{7,15},{8,0},{9,1},... | collective-permute-start | bytes 737288 | tf_op jit(solution)/shard_map/m2/ppermute | solution.py:64
  9.2 3.1 %copy-done = bf16[1,1024,3584]{2,1,0:T(8,128)(2,1)S(1)} copy-done((bf16[1,1024,3584]{2,1,0:T(8,128)(2,1)S(1)}, bf16[1,1024,3584]{2,1,0:T(8,128)(2,1)}, u32[]{:S(2)}) %copy-start) | copy-done | bytes 7340056
  12.2 3.1 %copy-done.1 = bf16[1,3584,1024]{2,1,0:T(8,128)(2,1)S(1)} copy-done((bf16[1,3584,1024]{2,1,0:T(8,128)(2,1)S(1)}, bf16[1,3584,1024]{2,1,0:T(8,128)(2,1)}, u32[]{:S(2)}) %copy-start.1) | copy-done | bytes 7340056
  15.3 3.1 %copy-done.4 = bf16[1,3584,1024]{2,1,0:T(8,128)(2,1)S(1)} copy-done((bf16[1,3584,1024]{2,1,0:T(8,128)(2,1)S(1)}, bf16[1,3584,1024]{2,1,0:T(8,128)(2,1)}, u32[]{:S(2)}) %copy-start.4) | copy-done | bytes 7340056
  18.4 3.6 %collective-permute-done.1.refs_0_ = bf16[64,1920]{1,0:T(8,128)(2,1)S(1)} collective-permute-done((bf16[64,1920]{1,0:T(8,128)(2,1)}, bf16[64,1920]{1,0:T(8,128)(2,1)S(1)}, u32[]{:S(2)}, u32[]{:S(2)}) %collective-permute-start.1) | collective-permute-done | bytes 245792 | tf_op jit(solution)/shard_map/m2/ppermute | solution.py:64
  22.8 2.6 %collective-permute-start.5 = (bf16[64,1920]{1,0:T(8,128)(2,1)S(1)}, bf16[64,1920]{1,0:T(8,128)(2,1)S(1)}, u32[]{:S(2)}, u32[]{:S(2)}) collective-permute-start(bf16[64,1920]{1,0:T(8,128)(2,1)S(1)} %collective-permute-done.1.refs_0_), channel_id=1, source_target_pairs={{0,4},{1,5},{2,6},{3,7},{4,0},{5,1},{6,2},{7,3},{8,12},{9,13},{10,... | collective-permute-start | bytes 737288 | tf_op jit(solution)/shard_map/m3/ppermute | solution.py:64
  27.4 2.8 %collective-permute-done.5.refs_2_ = bf16[64,1920]{1,0:T(8,128)(2,1)S(1)} collective-permute-done((bf16[64,1920]{1,0:T(8,128)(2,1)S(1)}, bf16[64,1920]{1,0:T(8,128)(2,1)S(1)}, u32[]{:S(2)}, u32[]{:S(2)}) %collective-permute-start.5) | collective-permute-done | bytes 245792 | tf_op jit(solution)/shard_map/m3/ppermute | solution.py:64
  31.6 3.8 %collective-permute-done.4.refs_1_ = bf16[64,1920]{1,0:T(8,128)(2,1)S(1)} collective-permute-done((bf16[64,1920]{1,0:T(8,128)(2,1)S(1)}, bf16[64,1920]{1,0:T(8,128)(2,1)S(1)}, u32[]{:S(2)}, u32[]{:S(2)}) %collective-permute-start.4) | collective-permute-done | bytes 245792 | tf_op jit(solution)/shard_map/m2y/ppermute | solution.py:64
  35.4 2.9 %collective-permute-done.6.refs_3_ = bf16[64,1920]{1,0:T(8,128)(2,1)S(1)} collective-permute-done((bf16[64,1920]{1,0:T(8,128)(2,1)S(1)}, bf16[64,1920]{1,0:T(8,128)(2,1)S(1)}, u32[]{:S(2)}, u32[]{:S(2)}) %collective-permute-start.6) | collective-permute-done | bytes 245792 | tf_op jit(solution)/shard_map/m3y/ppermute | solution.py:64
  38.3 2.1 %shard_map.66 = (bf16[128,1920]{1,0:T(8,128)(2,1)S(1)}, bf16[128,1920]{1,0:T(8,128)(2,1)S(1)}, bf16[4,64,64]{2,1,0:T(8,128)(2,1)S(1)}) custom-call(s32[1]{0:T(128)} %bitcast.3.me_ref, bf16[64,1920]{1,0:T(8,128)(2,1)S(1)} %collective-permute-done.1.refs_0_, bf16[64,1920]{1,0:T(8,128)(2,1)S(1)} %collective-permute-done.4.refs_1_, ...), custom_call_target="tpu_custom_call" | custom-call | flops 1 | bytes 1 | tf_op jit(solution)/shard_map/pallas_call | solution.py:91
  43.7 3.1 %copy-done.2 = bf16[1,3584,1024]{2,1,0:T(8,128)(2,1)S(1)} copy-done((bf16[1,3584,1024]{2,1,0:T(8,128)(2,1)S(1)}, bf16[1,3584,1024]{2,1,0:T(8,128)(2,1)}, u32[]{:S(2)}) %copy-start.2) | copy-done | bytes 7340056
  46.8 3.1 %copy-done.5 = bf16[1,3584,1024]{2,1,0:T(8,128)(2,1)S(1)} copy-done((bf16[1,3584,1024]{2,1,0:T(8,128)(2,1)S(1)}, bf16[1,3584,1024]{2,1,0:T(8,128)(2,1)}, u32[]{:S(2)}) %copy-start.5) | copy-done | bytes 7340056
  49.9 2.6 %shard_map.67 = (f32[256,1024]{1,0:T(8,128)S(1)}, f32[256,1024]{1,0:T(8,128)S(1)}) custom-call(s32[2]{0:T(128)S(1)} %pad_add_fusion.scalar_ref, bf16[128,1920]{1,0:T(8,128)(2,1)S(1)} %get-tuple-element.67.keep_ref.refs_2_, bf16[128,1920]{1,0:T(8,128)(2,1)S(1)} %collective-permute-done.7.got_ref.refs_3_, bf16[1,3584,1024]{2,1,0:T(8,128)(2,1)S(1)} %copy-done.2, ...), custom_call_target="tpu_custom_call" | custom-call | flops 1 | bytes 1 | tf_op jit(solution)/shard_map/pallas_call | solution.py:91
  52.5 2.6 %collective-permute-done.8.refs_1_ = bf16[64,1920]{1,0:T(8,128)(2,1)S(1)} collective-permute-done((bf16[64,1920]{1,0:T(8,128)(2,1)S(1)}, bf16[64,1920]{1,0:T(8,128)(2,1)S(1)}, u32[]{:S(2)}, u32[]{:S(2)}) %collective-permute-start.8) | collective-permute-done | bytes 245792 | tf_op jit(solution)/shard_map/f2y/ppermute | solution.py:81
  55.1 4.5 %collective-permute-done.10.refs_3_ = bf16[64,1920]{1,0:T(8,128)(2,1)S(1)} collective-permute-done((bf16[64,1920]{1,0:T(8,128)(2,1)S(1)}, bf16[64,1920]{1,0:T(8,128)(2,1)S(1)}, u32[]{:S(2)}, u32[]{:S(2)}) %collective-permute-start.10) | collective-permute-done | bytes 245792 | tf_op jit(solution)/shard_map/f3y/ppermute | solution.py:81
  60.2 2.3 %shard_map.69 = (bf16[128,3712]{1,0:T(8,128)(2,1)S(1)}, bf16[128,3712]{1,0:T(8,128)(2,1)S(1)}, bf16[4,64,64]{2,1,0:T(8,128)(2,1)S(1)}) custom-call(s32[1]{0:T(128)} %bitcast.5.me_ref, bf16[64,3712]{1,0:T(8,128)(2,1)S(1)} %copy-done.6, bf16[64,3712]{1,0:T(8,128)(2,1)S(1)} %collective-permute-done.2.refs_1_, ...), custom_call_target="tpu_custom_call" | custom-call | flops 1 | bytes 1 | tf_op jit(solution)/shard_map/pallas_call | solution.py:91
  63.0 2.8 %shard_map.70.hidden_ref = bf16[256,1024]{1,0:T(8,128)(2,1)S(1)} custom-call(s32[2]{0:T(128)S(1)} %pad_add_fusion.scalar_ref, bf16[128,1792]{1,0:T(8,128)(2,1)S(1)} %get-tuple-element.71.keep_ref, bf16[128,1792]{1,0:T(8,128)(2,1)S(1)} %collective-permute-done.12.got_ref, bf16[1,3584,1024]{2,1,0:T(8,128)(2,1)S(1)} %copy-done.3, ...), custom_call_target="tpu_custom_call" | custom-call | flops 1 | bytes 1 | tf_op jit(solution)/shard_map/pallas_call | solution.py:91
  65.8 1.8 %shard_map.71 = (bf16[2,128,896]{2,1,0:T(8,128)(2,1)S(1)}, bf16[2,128,896]{2,1,0:T(8,128)(2,1)S(1)}) custom-call(s32[2]{0:T(128)S(1)} %pad_add_fusion.scalar_ref, bf16[256,1024]{1,0:T(8,128)(2,1)S(1)} %shard_map.70.hidden_ref, bf16[1,1024,3584]{2,1,0:T(8,128)(2,1)S(1)} %bitcast.88, f32[16,128]{1,0:T(8,128)S(1)} %shard_map.65.refs_0_), custom_call_target="tpu_custom_call" | custom-call | flops 1 | bytes 1 | tf_op jit(solution)/shard_map/pallas_call | solution.py:91
  67.8 1.8 %shard_map.73 = (bf16[2,128,896]{2,1,0:T(8,128)(2,1)S(1)}, bf16[2,128,896]{2,1,0:T(8,128)(2,1)S(1)}) custom-call(s32[2]{0:T(128)S(1)} %pad_add_fusion.scalar_ref, bf16[256,1024]{1,0:T(8,128)(2,1)S(1)} %shard_map.70.hidden_ref, bf16[1,1024,3584]{2,1,0:T(8,128)(2,1)S(1)} %bitcast.88), custom_call_target="tpu_custom_call" | custom-call | flops 1 | bytes 1 | tf_op jit(solution)/shard_map/pallas_call | solution.py:91
  73.6 4.7 %shard_map.75.hidden_ref = bf16[256,1024]{1,0:T(8,128)(2,1)S(1)} custom-call(s32[2]{0:T(128)S(1)} %pad_add_fusion.scalar_ref, bf16[128,3712]{1,0:T(8,128)(2,1)S(1)} %get-tuple-element.77.keep_ref, bf16[128,3712]{1,0:T(8,128)(2,1)S(1)} %collective-permute-done.17.got_ref, bf16[1,3584,1024]{2,1,0:T(8,128)(2,1)S(1)} %copy-done.3, ...), custom_call_target="tpu_custom_call" | custom-call | flops 1 | bytes 1 | tf_op jit(solution)/shard_map/pallas_call | solution.py:91
  78.9 1.8 %shard_map.76 = (bf16[2,128,896]{2,1,0:T(8,128)(2,1)S(1)}, bf16[2,128,896]{2,1,0:T(8,128)(2,1)S(1)}) custom-call(s32[2]{0:T(128)S(1)} %pad_add_fusion.scalar_ref, bf16[256,1024]{1,0:T(8,128)(2,1)S(1)} %shard_map.75.hidden_ref, bf16[1,1024,3584]{2,1,0:T(8,128)(2,1)S(1)} %bitcast.88), custom_call_target="tpu_custom_call" | custom-call | flops 1 | bytes 1 | tf_op jit(solution)/shard_map/pallas_call | solution.py:91
  80.7 1.8 %shard_map.78 = (bf16[2,128,896]{2,1,0:T(8,128)(2,1)S(1)}, bf16[2,128,896]{2,1,0:T(8,128)(2,1)S(1)}) custom-call(s32[2]{0:T(128)S(1)} %pad_add_fusion.scalar_ref, bf16[256,1024]{1,0:T(8,128)(2,1)S(1)} %shard_map.75.hidden_ref, bf16[1,1024,3584]{2,1,0:T(8,128)(2,1)S(1)} %bitcast.88), custom_call_target="tpu_custom_call" | custom-call | flops 1 | bytes 1 | tf_op jit(solution)/shard_map/pallas_call | solution.py:91
  88.9 2.6 %collective-permute-done.26 = bf16[64,896]{1,0:T(8,128)(2,1)S(1)} collective-permute-done((bf16[64,896]{1,0:T(8,128)(2,1)S(1)}, bf16[64,896]{1,0:T(8,128)(2,1)S(1)}, u32[]{:S(2)}, u32[]{:S(2)}) %collective-permute-start.26) | collective-permute-done | bytes 114720 | tf_op jit(solution)/shard_map/p3/ppermute | solution.py:64
  94.8 2.3 %collective-permute-done.24 = bf16[2,64,896]{2,1,0:T(8,128)(2,1)S(1)} collective-permute-done((bf16[2,64,896]{2,1,0:T(8,128)(2,1)S(1)}, bf16[2,64,896]{2,1,0:T(8,128)(2,1)S(1)}, u32[]{:S(2)}, u32[]{:S(2)}) %collective-permute-start.24) | collective-permute-done | bytes 229408 | tf_op jit(solution)/shard_map/b2/ppermute | solution.py:64
  98.1 2.1 %collective-permute-start.20 = (bf16[2,2,64,896]{3,2,0,1:T(8,128)(2,1)S(1)}, bf16[2,2,64,896]{3,2,0,1:T(8,128)(2,1)S(1)}, u32[]{:S(2)}, u32[]{:S(2)}) collective-permute-start(bf16[2,2,64,896]{3,2,0,1:T(8,128)(2,1)S(1)} %copy.8), channel_id=1, source_target_pairs={{0,16},{16,0},{1,17},{17,1},{2,18},{18,2},{3,19},{19,3},{4,20},{20... | collective-permute-start | bytes 1376264 | tf_op jit(solution)/shard_map/n/ppermute | solution.py:81
  101.3 2.0 %collective-permute-done.25 = bf16[64,896]{1,0:T(8,128)(2,1)S(1)} collective-permute-done((bf16[64,896]{1,0:T(8,128)(2,1)S(1)}, bf16[64,896]{1,0:T(8,128)(2,1)S(1)}, u32[]{:S(2)}, u32[]{:S(2)}) %collective-permute-start.25) | collective-permute-done | bytes 114720 | tf_op jit(solution)/shard_map/q2/ppermute | solution.py:81
  105.0 4.6 %collective-permute-done.20 = bf16[2,2,64,896]{3,2,0,1:T(8,128)(2,1)S(1)} collective-permute-done((bf16[2,2,64,896]{3,2,0,1:T(8,128)(2,1)S(1)}, bf16[2,2,64,896]{3,2,0,1:T(8,128)(2,1)S(1)}, u32[]{:S(2)}, u32[]{:S(2)}) %collective-permute-start.20) | collective-permute-done | bytes 458784 | tf_op jit(solution)/shard_map/n/ppermute | solution.py:81
  112.2 4.1 %collective-permute-done.28 = bf16[2,64,896]{2,1,0:T(8,128)(2,1)S(1)} collective-permute-done((bf16[2,64,896]{2,1,0:T(8,128)(2,1)S(1)}, bf16[2,64,896]{2,1,0:T(8,128)(2,1)S(1)}, u32[]{:S(2)}, u32[]{:S(2)}) %collective-permute-start.28) | collective-permute-done | bytes 229408 | tf_op jit(solution)/shard_map/np/ppermute | solution.py:64
  117.1 2.7 %collective-permute-done.31 = bf16[2,64,896]{2,1,0:T(8,128)(2,1)S(1)} collective-permute-done((bf16[2,64,896]{2,1,0:T(8,128)(2,1)S(1)}, bf16[2,64,896]{2,1,0:T(8,128)(2,1)S(1)}, u32[]{:S(2)}, u32[]{:S(2)}) %collective-permute-start.31) | collective-permute-done | bytes 229408 | tf_op jit(solution)/shard_map/s2/ppermute | solution.py:64
  119.8 4.3 %collective-permute-done.30 = bf16[2,64,896]{2,1,0:T(8,128)(2,1)S(1)} collective-permute-done((bf16[2,64,896]{2,1,0:T(8,128)(2,1)S(1)}, bf16[2,64,896]{2,1,0:T(8,128)(2,1)S(1)}, u32[]{:S(2)}, u32[]{:S(2)}) %collective-permute-start.30) | collective-permute-done | bytes 229408 | tf_op jit(solution)/shard_map/s1/ppermute | solution.py:64
  (99 shorter events, 32.6 us)
Async XLA Ops:
  2.0 20.0 %collective-permute-start.2 = (bf16[64,3712]{1,0:T(8,128)(2,1)}, bf16[64,3712]{1,0:T(8,128)(2,1)S(1)}, u32[]{:S(2)}, u32[]{:S(2)}) collective-permute-start(bf16[64,3712]{1,0:T(8,128)(2,1)} %get-tuple-element.59.refs_0_), channel_id=1, source_target_pairs={{0,2},{1,3},{2,0},{3,1},{4,6},{5,7},{6,4},{7,5},{8,10},{9,11},{10,... | collective-permute-start | bytes 1425416 | tf_op jit(solution)/shard_map/w0y/ppermute | solution.py:64
  5.0 17.8 %collective-permute-start = (bf16[64,3712]{1,0:T(8,128)(2,1)}, bf16[64,3712]{1,0:T(8,128)(2,1)S(1)}, u32[]{:S(2)}, u32[]{:S(2)}) collective-permute-start(bf16[64,3712]{1,0:T(8,128)(2,1)} %get-tuple-element.59.refs_0_), channel_id=1, source_target_pairs={{0,4},{1,5},{2,6},{3,7},{4,0},{5,1},{6,2},{7,3},{8,12},{9,13},{10,... | collective-permute-start | bytes 1425416 | tf_op jit(solution)/shard_map/w1/ppermute | solution.py:64
  6.6 15.4 %collective-permute-start.1 = (bf16[64,1920]{1,0:T(8,128)(2,1)}, bf16[64,1920]{1,0:T(8,128)(2,1)S(1)}, u32[]{:S(2)}, u32[]{:S(2)}) collective-permute-start(bf16[64,1920]{1,0:T(8,128)(2,1)} %get-tuple-element.60), channel_id=1, source_target_pairs={{0,8},{1,9},{2,10},{3,11},{4,12},{5,13},{6,14},{7,15},{8,0},{9,1},... | collective-permute-start | bytes 737288 | tf_op jit(solution)/shard_map/m2/ppermute | solution.py:64
  22.8 7.4 %collective-permute-start.5 = (bf16[64,1920]{1,0:T(8,128)(2,1)S(1)}, bf16[64,1920]{1,0:T(8,128)(2,1)S(1)}, u32[]{:S(2)}, u32[]{:S(2)}) collective-permute-start(bf16[64,1920]{1,0:T(8,128)(2,1)S(1)} %collective-permute-done.1.refs_0_), channel_id=1, source_target_pairs={{0,4},{1,5},{2,6},{3,7},{4,0},{5,1},{6,2},{7,3},{8,12},{9,13},{10,... | collective-permute-start | bytes 737288 | tf_op jit(solution)/shard_map/m3/ppermute | solution.py:64
  25.4 6.2 %collective-permute-start.3 = (bf16[64,1920]{1,0:T(8,128)(2,1)S(1)}, bf16[64,1920]{1,0:T(8,128)(2,1)S(1)}, u32[]{:S(2)}, u32[]{:S(2)}) collective-permute-start(bf16[64,1920]{1,0:T(8,128)(2,1)S(1)} %collective-permute-done.1.refs_0_), channel_id=1, source_target_pairs={{0,16},{16,0},{1,17},{17,1},{2,18},{18,2},{3,19},{19,3},{4,20},{20... | collective-permute-start | bytes 737288 | tf_op jit(solution)/shard_map/f2/ppermute | solution.py:81
  26.9 8.5 %collective-permute-start.4 = (bf16[64,1920]{1,0:T(8,128)(2,1)S(1)}, bf16[64,1920]{1,0:T(8,128)(2,1)S(1)}, u32[]{:S(2)}, u32[]{:S(2)}) collective-permute-start(bf16[64,1920]{1,0:T(8,128)(2,1)S(1)} %collective-permute-done.1.refs_0_), channel_id=1, source_target_pairs={{0,2},{1,3},{2,0},{3,1},{4,6},{5,7},{6,4},{7,5},{8,10},{9,11},{10,... | collective-permute-start | bytes 737288 | tf_op jit(solution)/shard_map/m2y/ppermute | solution.py:64
  30.2 8.2 %collective-permute-start.6 = (bf16[64,1920]{1,0:T(8,128)(2,1)S(1)}, bf16[64,1920]{1,0:T(8,128)(2,1)S(1)}, u32[]{:S(2)}, u32[]{:S(2)}) collective-permute-start(bf16[64,1920]{1,0:T(8,128)(2,1)S(1)} %collective-permute-done.5.refs_2_), channel_id=1, source_target_pairs={{0,2},{1,3},{2,0},{3,1},{4,6},{5,7},{6,4},{7,5},{8,10},{9,11},{10,... | collective-permute-start | bytes 737288 | tf_op jit(solution)/shard_map/m3y/ppermute | solution.py:64
  40.4 3.3 %collective-permute-start.7 = (bf16[128,1920]{1,0:T(8,128)(2,1)S(1)}, bf16[128,1920]{1,0:T(8,128)(2,1)S(1)}, u32[]{:S(2)}, u32[]{:S(2)}) collective-permute-start(bf16[128,1920]{1,0:T(8,128)(2,1)S(1)} %get-tuple-element.68), channel_id=1, source_target_pairs={{0,1},{1,0},{2,3},{3,2},{4,5},{5,4},{6,7},{7,6},{8,9},{9,8},{10,11... | collective-permute-start | bytes 1474568 | tf_op jit(solution)/shard_map/rows_m/ppermute | solution.py:64
  40.5 19.7 %collective-permute-start.11 = (bf16[64,3712]{1,0:T(8,128)(2,1)S(1)}, bf16[64,3712]{1,0:T(8,128)(2,1)S(1)}, u32[]{:S(2)}, u32[]{:S(2)}) collective-permute-start(bf16[64,3712]{1,0:T(8,128)(2,1)S(1)} %collective-permute-done.refs_2_), channel_id=1, source_target_pairs={{0,2},{1,3},{2,0},{3,1},{4,6},{5,7},{6,4},{7,5},{8,10},{9,11},{10,... | collective-permute-start | bytes 1425416 | tf_op jit(solution)/shard_map/w1y/ppermute | solution.py:64
  41.1 11.5 %collective-permute-start.9 = (bf16[64,1920]{1,0:T(8,128)(2,1)S(1)}, bf16[64,1920]{1,0:T(8,128)(2,1)S(1)}, u32[]{:S(2)}, u32[]{:S(2)}) collective-permute-start(bf16[64,1920]{1,0:T(8,128)(2,1)S(1)} %collective-permute-done.5.refs_2_), channel_id=1, source_target_pairs={{0,16},{16,0},{1,17},{17,1},{2,18},{18,2},{3,19},{19,3},{4,20},{20... | collective-permute-start | bytes 737288 | tf_op jit(solution)/shard_map/f3/ppermute | solution.py:81
  41.6 13.5 %collective-permute-start.8 = (bf16[64,1920]{1,0:T(8,128)(2,1)S(1)}, bf16[64,1920]{1,0:T(8,128)(2,1)S(1)}, u32[]{:S(2)}, u32[]{:S(2)}) collective-permute-start(bf16[64,1920]{1,0:T(8,128)(2,1)S(1)} %collective-permute-done.4.refs_1_), channel_id=1, source_target_pairs={{0,16},{16,0},{1,17},{17,1},{2,18},{18,2},{3,19},{19,3},{4,20},{20... | collective-permute-start | bytes 737288 | tf_op jit(solution)/shard_map/f2y/ppermute | solution.py:81
  43.1 16.5 %collective-permute-start.10 = (bf16[64,1920]{1,0:T(8,128)(2,1)S(1)}, bf16[64,1920]{1,0:T(8,128)(2,1)S(1)}, u32[]{:S(2)}, u32[]{:S(2)}) collective-permute-start(bf16[64,1920]{1,0:T(8,128)(2,1)S(1)} %collective-permute-done.6.refs_3_), channel_id=1, source_target_pairs={{0,16},{16,0},{1,17},{17,1},{2,18},{18,2},{3,19},{19,3},{4,20},{20... | collective-permute-start | bytes 737288 | tf_op jit(solution)/shard_map/f3y/ppermute | solution.py:81
  60.1 2.9 %collective-permute-start.12 = (bf16[128,1792]{1,0:T(8,128)(2,1)S(1)}, bf16[128,1792]{1,0:T(8,128)(2,1)S(1)}, u32[]{:S(2)}, u32[]{:S(2)}) collective-permute-start(bf16[128,1792]{1,0:T(8,128)(2,1)S(1)} %get-tuple-element.79), channel_id=1, source_target_pairs={{0,1},{1,0},{2,3},{3,2},{4,5},{5,4},{6,7},{7,6},{8,9},{9,8},{10,11... | collective-permute-start | bytes 1376264 | tf_op jit(solution)/shard_map/rows_f/ppermute | solution.py:64
  62.5 11.1 %collective-permute-start.17 = (bf16[128,3712]{1,0:T(8,128)(2,1)S(1)}, bf16[128,3712]{1,0:T(8,128)(2,1)S(1)}, u32[]{:S(2)}, u32[]{:S(2)}) collective-permute-start(bf16[128,3712]{1,0:T(8,128)(2,1)S(1)} %get-tuple-element.93), channel_id=1, source_target_pairs={{0,1},{1,0},{2,3},{3,2},{4,5},{5,4},{6,7},{7,6},{8,9},{9,8},{10,11... | collective-permute-start | bytes 2850824 | tf_op jit(solution)/shard_map/rows_n/ppermute | solution.py:64
  67.7 2.5 %collective-permute-start.13 = (bf16[2,128,896]{2,1,0:T(8,128)(2,1)S(1)}, bf16[2,128,896]{2,1,0:T(8,128)(2,1)S(1)}, u32[]{:S(2)}, u32[]{:S(2)}) collective-permute-start(bf16[2,128,896]{2,1,0:T(8,128)(2,1)S(1)} %get-tuple-element.82), channel_id=1, source_target_pairs={{0,1},{1,0},{2,3},{3,2},{4,5},{5,4},{6,7},{7,6},{8,9},{9,8},{10,11... | collective-permute-start | bytes 1376264 | tf_op jit(solution)/shard_map/back_a/ppermute | solution.py:64
  71.9 11.2 %collective-permute-start.16 = (bf16[2,64,896]{2,1,0:T(8,128)(2,1)S(1)}, bf16[2,64,896]{2,1,0:T(8,128)(2,1)S(1)}, u32[]{:S(2)}, u32[]{:S(2)}) collective-permute-start(bf16[2,64,896]{2,1,0:T(8,128)(2,1)S(1)} %get-tuple-element.89), channel_id=1, source_target_pairs={{0,2},{1,3},{2,0},{3,1},{4,6},{5,7},{6,4},{7,5},{8,10},{9,11},{10,... | collective-permute-start | bytes 688136 | tf_op jit(solution)/shard_map/b3/ppermute | solution.py:64
  78.3 7.7 %collective-permute-start.14 = (bf16[2,64,896]{2,1,0:T(8,128)(2,1)S(1)}, bf16[2,64,896]{2,1,0:T(8,128)(2,1)S(1)}, u32[]{:S(2)}, u32[]{:S(2)}) collective-permute-start(bf16[2,64,896]{2,1,0:T(8,128)(2,1)S(1)} %get-tuple-element.83), channel_id=1, source_target_pairs={{0,16},{16,0},{1,17},{17,1},{2,18},{18,2},{3,19},{19,3},{4,20},{20... | collective-permute-start | bytes 688136 | tf_op jit(solution)/shard_map/a3/ppermute | solution.py:81
  82.5 15.1 %collective-permute-start.19 = (bf16[2,128,896]{2,1,0:T(8,128)(2,1)S(1)}, bf16[2,128,896]{2,1,0:T(8,128)(2,1)S(1)}, u32[]{:S(2)}, u32[]{:S(2)}) collective-permute-start(bf16[2,128,896]{2,1,0:T(8,128)(2,1)S(1)} %get-tuple-element.100), channel_id=1, source_target_pairs={{0,1},{1,0},{2,3},{3,2},{4,5},{5,4},{6,7},{7,6},{8,9},{9,8},{10,11... | collective-permute-start | bytes 1376264 | tf_op jit(solution)/shard_map/back_o/ppermute | solution.py:64
  82.6 14.6 %collective-permute-start.18 = (bf16[2,128,896]{2,1,0:T(8,128)(2,1)S(1)}, bf16[2,128,896]{2,1,0:T(8,128)(2,1)S(1)}, u32[]{:S(2)}, u32[]{:S(2)}) collective-permute-start(bf16[2,128,896]{2,1,0:T(8,128)(2,1)S(1)} %get-tuple-element.95), channel_id=1, source_target_pairs={{0,1},{1,0},{2,3},{3,2},{4,5},{5,4},{6,7},{7,6},{8,9},{9,8},{10,11... | collective-permute-start | bytes 1376264 | tf_op jit(solution)/shard_map/back_n/ppermute | solution.py:64
  83.2 5.5 %collective-permute-start.27 = (bf16[64,896]{1,0:T(8,128)(2,1)S(1)}, bf16[64,896]{1,0:T(8,128)(2,1)S(1)}, u32[]{:S(2)}, u32[]{:S(2)}) collective-permute-start(bf16[64,896]{1,0:T(8,128)(2,1)S(1)} %slice_bitcast_fusion.7), channel_id=1, source_target_pairs={{0,16},{16,0},{1,17},{17,1},{2,18},{18,2},{3,19},{19,3},{4,20},{20... | collective-permute-start | bytes 344072 | tf_op jit(solution)/shard_map/q3/ppermute | solution.py:81
  86.1 5.5 %collective-permute-start.26 = (bf16[64,896]{1,0:T(8,128)(2,1)S(1)}, bf16[64,896]{1,0:T(8,128)(2,1)S(1)}, u32[]{:S(2)}, u32[]{:S(2)}) collective-permute-start(bf16[64,896]{1,0:T(8,128)(2,1)S(1)} %slice_bitcast_fusion.9), channel_id=1, source_target_pairs={{0,2},{1,3},{2,0},{3,1},{4,6},{5,7},{6,4},{7,5},{8,10},{9,11},{10,... | collective-permute-start | bytes 344072 | tf_op jit(solution)/shard_map/p3/ppermute | solution.py:64
  86.6 6.7 %collective-permute-start.22 = (bf16[2,64,896]{2,1,0:T(8,128)(2,1)S(1)}, bf16[2,64,896]{2,1,0:T(8,128)(2,1)S(1)}, u32[]{:S(2)}, u32[]{:S(2)}) collective-permute-start(bf16[2,64,896]{2,1,0:T(8,128)(2,1)S(1)} %get-tuple-element.106), channel_id=1, source_target_pairs={{0,16},{16,0},{1,17},{17,1},{2,18},{18,2},{3,19},{19,3},{4,20},{20... | collective-permute-start | bytes 688136 | tf_op jit(solution)/shard_map/a2/ppermute | solution.py:81
  88.7 8.4 %collective-permute-start.24 = (bf16[2,64,896]{2,1,0:T(8,128)(2,1)S(1)}, bf16[2,64,896]{2,1,0:T(8,128)(2,1)S(1)}, u32[]{:S(2)}, u32[]{:S(2)}) collective-permute-start(bf16[2,64,896]{2,1,0:T(8,128)(2,1)S(1)} %get-tuple-element.107), channel_id=1, source_target_pairs={{0,2},{1,3},{2,0},{3,1},{4,6},{5,7},{6,4},{7,5},{8,10},{9,11},{10,... | collective-permute-start | bytes 688136 | tf_op jit(solution)/shard_map/b2/ppermute | solution.py:64
  93.4 7.9 %collective-permute-start.23 = (bf16[64,896]{1,0:T(8,128)(2,1)S(1)}, bf16[64,896]{1,0:T(8,128)(2,1)S(1)}, u32[]{:S(2)}, u32[]{:S(2)}) collective-permute-start(bf16[64,896]{1,0:T(8,128)(2,1)S(1)} %slice_bitcast_fusion.12), channel_id=1, source_target_pairs={{0,2},{1,3},{2,0},{3,1},{4,6},{5,7},{6,4},{7,5},{8,10},{9,11},{10,... | collective-permute-start | bytes 344072 | tf_op jit(solution)/shard_map/p2/ppermute | solution.py:64
  97.1 6.1 %collective-permute-start.25 = (bf16[64,896]{1,0:T(8,128)(2,1)S(1)}, bf16[64,896]{1,0:T(8,128)(2,1)S(1)}, u32[]{:S(2)}, u32[]{:S(2)}) collective-permute-start(bf16[64,896]{1,0:T(8,128)(2,1)S(1)} %slice_bitcast_fusion.11), channel_id=1, source_target_pairs={{0,16},{16,0},{1,17},{17,1},{2,18},{18,2},{3,19},{19,3},{4,20},{20... | collective-permute-start | bytes 344072 | tf_op jit(solution)/shard_map/q2/ppermute | solution.py:81
  98.1 11.5 %collective-permute-start.20 = (bf16[2,2,64,896]{3,2,0,1:T(8,128)(2,1)S(1)}, bf16[2,2,64,896]{3,2,0,1:T(8,128)(2,1)S(1)}, u32[]{:S(2)}, u32[]{:S(2)}) collective-permute-start(bf16[2,2,64,896]{3,2,0,1:T(8,128)(2,1)S(1)} %copy.8), channel_id=1, source_target_pairs={{0,16},{16,0},{1,17},{17,1},{2,18},{18,2},{3,19},{19,3},{4,20},{20... | collective-permute-start | bytes 1376264 | tf_op jit(solution)/shard_map/n/ppermute | solution.py:81
  100.1 9.9 %collective-permute-start.21 = (bf16[2,2,64,896]{3,2,1,0:T(8,128)(2,1)S(1)}, bf16[2,2,64,896]{3,2,1,0:T(8,128)(2,1)S(1)}, u32[]{:S(2)}, u32[]{:S(2)}) collective-permute-start(bf16[2,2,64,896]{3,2,1,0:T(8,128)(2,1)S(1)} %get-tuple-element.103), channel_id=1, source_target_pairs={{0,2},{1,3},{2,0},{3,1},{4,6},{5,7},{6,4},{7,5},{8,10},{9,11},{10,... | collective-permute-start | bytes 1376264 | tf_op jit(solution)/shard_map/o/ppermute | solution.py:64
  100.3 16.9 %collective-permute-start.32 = (bf16[2,64,896]{2,1,0:T(8,128)(2,1)S(1)}, bf16[2,64,896]{2,1,0:T(8,128)(2,1)S(1)}, u32[]{:S(2)}, u32[]{:S(2)}) collective-permute-start(bf16[2,64,896]{2,1,0:T(8,128)(2,1)S(1)} %pad_maximum_fusion.1), channel_id=1, source_target_pairs={{0,12},{1,13},{2,14},{3,15},{4,8},{5,9},{6,10},{7,11},{8,4},{9,5},... | collective-permute-start | bytes 688136 | tf_op jit(solution)/shard_map/s3/ppermute | solution.py:64
  103.4 16.4 %collective-permute-start.31 = (bf16[2,64,896]{2,1,0:T(8,128)(2,1)S(1)}, bf16[2,64,896]{2,1,0:T(8,128)(2,1)S(1)}, u32[]{:S(2)}, u32[]{:S(2)}) collective-permute-start(bf16[2,64,896]{2,1,0:T(8,128)(2,1)S(1)} %pad_maximum_fusion.2), channel_id=1, source_target_pairs={{0,8},{1,9},{2,10},{3,11},{4,12},{5,13},{6,14},{7,15},{8,0},{9,1},... | collective-permute-start | bytes 688136 | tf_op jit(solution)/shard_map/s2/ppermute | solution.py:64
  110.1 6.1 %collective-permute-start.28 = (bf16[2,64,896]{2,1,0:T(8,128)(2,1)S(1)}, bf16[2,64,896]{2,1,0:T(8,128)(2,1)S(1)}, u32[]{:S(2)}, u32[]{:S(2)}) collective-permute-start(bf16[2,64,896]{2,1,0:T(8,128)(2,1)S(1)} %slice_bitcast_fusion.2), channel_id=1, source_target_pairs={{0,2},{1,3},{2,0},{3,1},{4,6},{5,7},{6,4},{7,5},{8,10},{9,11},{10,... | collective-permute-start | bytes 688136 | tf_op jit(solution)/shard_map/np/ppermute | solution.py:64
  110.7 6.1 %collective-permute-start.29 = (bf16[2,64,896]{2,1,0:T(8,128)(2,1)S(1)}, bf16[2,64,896]{2,1,0:T(8,128)(2,1)S(1)}, u32[]{:S(2)}, u32[]{:S(2)}) collective-permute-start(bf16[2,64,896]{2,1,0:T(8,128)(2,1)S(1)} %slice_bitcast_fusion), channel_id=1, source_target_pairs={{0,16},{16,0},{1,17},{17,1},{2,18},{18,2},{3,19},{19,3},{4,20},{20... | collective-permute-start | bytes 688136 | tf_op jit(solution)/shard_map/nq/ppermute | solution.py:81
  116.9 7.2 %collective-permute-start.30 = (bf16[2,64,896]{2,1,0:T(8,128)(2,1)S(1)}, bf16[2,64,896]{2,1,0:T(8,128)(2,1)S(1)}, u32[]{:S(2)}, u32[]{:S(2)}) collective-permute-start(bf16[2,64,896]{2,1,0:T(8,128)(2,1)S(1)} %fusion.13), channel_id=1, source_target_pairs={{0,4},{1,5},{2,6},{3,7},{4,0},{5,1},{6,2},{7,3},{8,12},{9,13},{10,... | collective-permute-start | bytes 688136 | tf_op jit(solution)/shard_map/s1/ppermute | solution.py:64
  (12 other events, 62.9 us)

commit v3 on v2

--- a/solution.py
+++ b/solution.py
@@ -82,9 +82,10 @@
 
 
 COST = pl.CostEstimate(flops=1, bytes_accessed=1, transcendentals=0)
-
-
-def call(kernel, out, ins):
+MUCH = pl.CostEstimate(flops=1 << 35, bytes_accessed=1, transcendentals=0)
+
+
+def call(kernel, out, ins, cost=COST):
     spec = [
         pl.BlockSpec(memory_space=pltpu.SMEM if v.dtype == jnp.int32 else pltpu.VMEM) for v in ins
     ]
@@ -94,7 +95,7 @@
         in_specs=spec,
         out_specs=jax.tree.map(lambda _: pl.BlockSpec(memory_space=pltpu.VMEM), out),
         compiler_params=pltpu.CompilerParams(vmem_limit_bytes=SMALL << 20),
-        cost_estimate=COST,
+        cost_estimate=cost,
     )(*ins)
 
 
@@ -140,7 +141,7 @@
     return jnp.dot(table, code.astype(BF), preferred_element_type=F32)
 
 
-def select(me, room, half, blocks):
+def select(me, room, half, blocks, cost=COST):
     rows, full = blocks[0].shape
     count = len(blocks)
 
@@ -153,25 +154,26 @@
         before = jnp.where(before, 1.0, 0.0).astype(BF)
         slot = lax.broadcasted_iota(jnp.int32, (rows, 2 * room), 1)
         first = slot < room
-        for b, ref in enumerate(refs[:count]):
-            chosen = jnp.where(lookup(ref[:, half : half + TABLE], mine) > 0, 1.0, 0.0)
-            place = jnp.dot(before, chosen.astype(BF), preferred_element_type=F32)
-            want = jnp.where(first, place[:, :1], place[:, 1:2] + room)
-            here = jnp.where(first, chosen[:, :1], chosen[:, 1:2])
-            put = jnp.where(want == slot.astype(F32), here, 0.0)
-            put_ref[b] = put.astype(BF)
-            got = jnp.dot(put.T.astype(BF), ref[...], preferred_element_type=F32).astype(BF)
+        chosen = [jnp.where(lookup(ref[:, half : half + TABLE], mine) > 0, 1.0, 0.0) for ref in refs[:count]]
+        place = [jnp.dot(before, c.astype(BF), preferred_element_type=F32) for c in chosen]
+        put = []
+        for c, p in zip(chosen, place, strict=True):
+            want = jnp.where(first, p[:, :1], p[:, 1:2] + room)
+            here = jnp.where(first, c[:, :1], c[:, 1:2])
+            put.append(jnp.where(want == slot.astype(F32), here, 0.0))
+        pick = [p.T.astype(BF) for p in put]
+        for b in range(count):
+            put_ref[b] = put[b].astype(BF)
+            got = jnp.dot(pick[b], refs[b][...], preferred_element_type=F32).astype(BF)
             keep[pl.ds(b * room, room)] = got[:room]
             give[pl.ds(b * room, room)] = got[room:]
 
     out = jax.ShapeDtypeStruct((count * room, full), BF)
     put = jax.ShapeDtypeStruct((count, rows, 2 * room), BF)
-    return call(kernel, (out, out, put), [me.reshape(1), *blocks])
-
-
-def select_far(put, blocks):
-    rows, full = blocks[0].shape
-    half = full - TABLE
+    return call(kernel, (out, out, put), [me.reshape(1), *blocks], cost)
+
+
+def select_far(put, half, blocks):
     room = put.shape[2] // 2
 
     def kernel(put_ref, *refs):
@@ -196,7 +198,7 @@
     return call(kernel, jax.ShapeDtypeStruct((16, 128), F32), weights)
 
 
-def gate_up(scalars, keep, got, gate, up, part, first=()):
+def gate_up(scalars, keep, got, gate, up, part, first=(), tokens=()):
     rows = keep.shape[0]
     depth, width = gate.shape[1:]
     half = depth // 2
@@ -230,8 +232,8 @@
 
             g, u = product(gate_ref), product(up_ref)
             if part == 1:
-                refs[0][:, columns] = g
-                refs[1][:, columns] = u
+                refs[-2][:, columns] = g
+                refs[-1][:, columns] = u
                 continue
             if part == 2:
                 g += refs[0][:, columns]
@@ -240,51 +242,63 @@
 
     shape = lambda kind: jax.ShapeDtypeStruct((2 * rows, width), kind)
     out = (shape(F32), shape(F32)) if part == 1 else shape(BF)
-    return call(kernel, out, [scalars, keep, got, gate, up, *first])
-
-
-def down(scalars, hidden, weights, quarter, *tokens):
+    return call(kernel, out, [scalars, keep, got, gate, up, *first, *tokens])
+
+
+def down(scalars, hidden, weights, quarters, *tokens):
     rows, depth = hidden.shape
     tile = weights.shape[2] // 4
 
     def kernel(scalar_ref, hidden_ref, down_ref, *refs):
         near, away = refs[-2:]
         x = scalar_ref[0]
-        for n in range(2):
-            side = x if n else 1 - x
-            start = (2 * side + quarter) * tile
+        for n in range(2 * len(quarters)):
+            side = x if n % 2 else 1 - x
+            start = (2 * side + quarters[n // 2]) * tile
             weight = down_ref[0, :, pl.ds(pl.multiple_of(start, 128), tile)]
             value = jnp.dot(hidden_ref[...], weight, preferred_element_type=F32).astype(BF)
             near[n] = value[: rows // 2]
             away[n] = value[rows // 2 :]
 
-    out = jax.ShapeDtypeStruct((2, rows // 2, tile), BF)
+    out = jax.ShapeDtypeStruct((2 * len(quarters), rows // 2, tile), BF)
     return call(kernel, (out, out), [scalars, hidden, weights, *tokens])
 
 
-def spread(put, near, back, quarter, split):
-    rows, room = put.shape[1], put.shape[2] // 2
-    width = near.shape[2]
+def placed(put_ref, near_ref, back_ref, h, b):
+    room = put_ref.shape[2] // 2
+    part = pl.ds(b * room, room)
+    value = jnp.concatenate([near_ref[h, part], back_ref[h, part]], axis=0)
+    return jnp.dot(put_ref[b], value, preferred_element_type=F32).astype(BF)
+
+
+def spread(put, near, back, quarter):
+    rows, width = put.shape[1], near.shape[2]
+    part = jax.ShapeDtypeStruct((2, rows, width), BF)
     whole = jax.ShapeDtypeStruct((2, 2, rows, width), BF)
-    part = jax.ShapeDtypeStruct((2, rows, width), BF)
-    out = (part, part, whole) if split else (whole, whole)
 
     def kernel(put_ref, near_ref, back_ref, *refs):
-        *give, keep = refs
+        give, keep = refs[:2], refs[2]
         for h in range(2):
             for b, (k, j) in enumerate(KJ[:4]):
-                place = pl.ds(b * room, room)
-                value = jnp.concatenate([near_ref[h, place], back_ref[h, place]], axis=0)
-                got = jnp.dot(put_ref[b], value, preferred_element_type=F32).astype(BF)
+                got = placed(put_ref, near_ref, back_ref, h, b)
                 stays, index = (h == 1, j) if quarter == 0 else (j == 0, h)
                 if stays:
                     keep[k, index] = got
-                elif split:
+                else:
                     give[k][index] = got
-                else:
-                    give[0][k, index] = got
-
-    return call(kernel, out, [put, near, back])
+
+    return call(kernel, (part, part, whole), [put, near, back])
+
+
+def spread_own(put, near, back):
+    rows, width = put.shape[1], near.shape[2]
+
+    def kernel(put_ref, near_ref, back_ref, out):
+        for h in range(near.shape[0]):
+            for j in range(NY):
+                out[h, j] = placed(put_ref, near_ref, back_ref, h, j)
+
+    return call(kernel, jax.ShapeDtypeStruct((near.shape[0], NY, rows, width), BF), [put, near, back])
 
 
 def in_order(values, earlier):
@@ -312,63 +326,70 @@
     scalars = jnp.stack([x, me])
 
     mine, whole = prepare(x, tokens, expert_ids, weight_num)
+    w1 = swap_z(whole, 1, "w1")
     w0y = swap_y(whole, "w0y")
-    w1 = swap_z(whole, 1, "w1")
     m2 = swap_z(mine, 2, "m2")
-    touched = touch(*in_order((gate_proj, up_proj, down_proj), (mine,)))
-    w1, m2, w0y = in_order((w1, m2, w0y), (touched,))
+    touched = touch(*in_order((gate_proj, up_proj), (mine,)))
+    w0y, m2, _ = lax.optimization_barrier((w0y, m2, touched))
+    w1y = swap_z(w0y, 1, "w1y")
+    f2 = swap_x(m2, "f2")
     m2y = swap_y(m2, "m2y")
-    f2 = swap_x(m2, "f2")
     m3 = swap_z(m2, 1, "m3")
-    w1y = swap_y(after(w1, m3), "w1y")
+    keep_0, give, put_0 = select(after(me, w1, m2), room, half, [whole, w0y], MUCH)
+    got_0 = swap_core(after(give, f2), "rows_0")
+    m3 = after(m3, m2y, f2)
     f3 = swap_x(m3, "f3")
+    f2y = swap_x(after(m2y, m3), "f2y")
     m3y = swap_y(m3, "m3y")
-    f2y = swap_x(m2y, "f2y")
     f3y = swap_x(m3y, "f3y")
-
-    keep, give, put_f = select(after(me, f2), room, half, [m2, m2y, m3, m3y])
+    hidden_0 = gate_up(after(scalars, m3), keep_0, got_0, gate_proj, up_proj, 0)
+    near_0, away = down(scalars, hidden_0, down_proj, (0, 1))
+    back_0 = swap_core(away, "back_0")
+
+    keep, give, put = select(after(me, near_0, f3, f2y, m3y), room, half, [m2, m2y, m3, m3y], MUCH)
     got = swap_core(give, "rows_m")
-    first = gate_up(scalars, keep, got, gate_proj, up_proj, 1, ())
-    keep_f, give_f = select_far(after(put_f, first[0]), [f2, f2y, f3, f3y])
+    keep_1, give, put_1 = select(after(me, keep), room, half, [w1, w1y])
+    got_1 = swap_core(give, "rows_1")
+    own = spread_own(after(put_0, keep_1), near_0, back_0)
+    first = gate_up(after(scalars, own), keep, got, gate_proj, up_proj, 1)
+    hidden_1 = gate_up(after(scalars, first[0]), keep_1, got_1, gate_proj, up_proj, 0)
+    keep_f, give_f = select_far(after(put, hidden_1), half, [f2, f2y, f3, f3y])
     got_f = swap_core(give_f, "rows_f")
-    keep_n, give, put_n = select(after(me, keep_f), room, half, [whole, w0y, w1, w1y])
-    got_n = swap_core(give, "rows_n")
-    hidden_f = gate_up(after(scalars, keep_n), keep_f, got_f, gate_proj, up_proj, 2, [*first, keep, got])
-    near_a, away = down(scalars, hidden_f, down_proj, 0, touched)
+    near_1, away = down(after(scalars, keep_f), hidden_1, down_proj, (0, 1))
+    back_1 = swap_core(away, "back_1")
+    hidden = gate_up(after(scalars, near_1), keep_f, got_f, gate_proj, up_proj, 2, [*first, keep, got])
+    near_a, away = down(scalars, hidden, down_proj, (0,), touched)
     back = swap_core(away, "back_a")
-    near_b, away = down(after(scalars, near_a), hidden_f, down_proj, 1)
-    a2, a3, keep_a = spread(put_f, near_a, back, 0, True)
+    n = spread_own(after(put_1, near_a), near_1, back_1)
+    n0, n1 = swap_z(n[:2], 1, "n0"), swap_z(n[2:], 1, "n1")
+    near_b, away = down(after(scalars, n), hidden, down_proj, (1,))
+    a2, a3, keep_a = spread(put, near_a, back, 0)
     back = swap_core(away, "back_b")
-    b2, b3, keep_b = spread(after(put_f, keep_a), near_b, back, 1, True)
-    hidden_n = gate_up(after(scalars, keep_b), keep_n, got_n, gate_proj, up_proj, 0)
-    near_n, away = down(scalars, hidden_n, down_proj, 0)
-    back_n = swap_core(away, "back_n")
-    near_o, away = down(after(scalars, near_n), hidden_n, down_proj, 1)
-    back_o = swap_core(away, "back_o")
+    b2, b3, keep_b = spread(after(put, keep_a), near_b, back, 1)
 
     b3, a3 = swap_y(b3, "b3"), swap_x(a3, "a3")
-    put_n = after(put_n, a3, b3)
     a3, b3 = add(keep_a[1], a3), add(keep_b[1], b3)
-    n, keep_n = spread(put_n, near_n, back_n, 0, False)
-    o, keep_o = spread(put_n, near_o, back_o, 1, False)
-    a2, b2 = in_order((a2, b2), (a3, b3))
-    n, o = in_order((n, o), (a3, b3))
-    o, n = swap_y(o, "o"), swap_x(n, "n")
+    a2, b2, a3, b3 = lax.optimization_barrier((a2, b2, a3, b3))
     b2, a2 = swap_y(b2, "b2"), swap_x(a2, "a2")
     p3, q3 = swap_y(a3[1], "p3"), swap_x(b3[0], "q3")
+    s3 = jnp.stack([add(a3[0], p3), add(b3[1], q3)])
+    n0, a2, b2 = in_order((n0, a2, b2), (s3,))
+    s3 = swap_z(s3, 1, "s3")
+    n0 = add(own[:2], n0)
+    a2, b2 = in_order((a2, b2), (n0,))
+    n, n0 = swap_x(n0[0], "n"), n0[1]
     a2, b2 = add(keep_a[0], a2), add(keep_b[0], b2)
     p2, q2 = swap_y(a2[1], "p2"), swap_x(b2[0], "q2")
-    s3 = jnp.stack([add(a3[0], p3), add(b3[1], q3)])
-    p2, q2 = in_order((p2, q2), (s3,))
-    s3 = swap_z(s3, 3, "s3")
-    s2 = jnp.stack([add(a2[0], p2), add(b2[1], q2)])
+    n1 = add(own[2:], after(n1, a2, b2))
+    o, n1 = swap_y(n1[:, 1], "o"), n1[:, 0]
+    s3, p2, q2 = in_order((s3, p2, q2), (n1,))
+    s2 = jnp.stack([add(a2[0], p2, s3[0]), add(b2[1], q2, s3[1])])
     n, o = in_order((n, o), (s2,))
     s2 = swap_z(s2, 2, "s2")
-    n, o = add(keep_n, n), add(keep_o, o)
-    np, nq = swap_y(n[:, 1], "np"), swap_x(o[:, 0], "nq")
-    n = jnp.stack([add(n[:, 0], np), add(o[:, 1], nq)])
-    s1 = swap_z(n[:, 1], 1, "s1")
-    total = add(n[:, 0], s1, s2, s3)
+    n, o = add(n0, n), add(n1, o)
+    np, nq = swap_y(n[1], "np"), swap_x(o[0], "nq")
+    n = jnp.stack([add(n[0], np), add(o[1], nq)])
+    total = add(n, s2)
     return jnp.concatenate([total[0], total[1]], axis=1)
 
 

time: 125 us -> 110 us (0.88)
  waiting for transfers between devices: 50.9 us -> 34.7 us
  local copies, waits for them, and re-layouts: 15.6 us -> 7.68 us
  starting transfers between devices: 30.7 us -> 38.2 us
  Pallas kernels: 25.7 us -> 27.3 us
    ppermute x23 -> x25, waiting for transfers between devices: 31.4 us -> 22.7 us  [swap_expert(): return lax.ppermute(value, 'expert', pairs)]
    unnamed x22 -> x15, local copies, waits for them, and re-layouts: 15.4 us -> 7.47 us
    ppermute x10, waiting for transfers between devices: 19.6 us -> 11.9 us  [swap_x(): return lax.ppermute(value, 'dp', [(0, 1), (1, 0)])]
    ppermute x23 -> x25, starting transfers between devices: 20.4 us -> 27 us  [swap_expert(): return lax.ppermute(value, 'expert', pairs)]
    pallas_call x15 -> x17, Pallas kernels: 23.7 us -> 25.3 us  [call(): pl.pallas_call(kernel, out_shape=out, in_specs=spec, out_specs=jax.tree.m...]
  transfers between devices with their start and end apart: 33 -> 35, of which waited for: 21 -> 17; matrix products, arithmetic and copies ran while one was open for 1% -> 1% of each run, Pallas kernels for 17% -> 23%
where the time goes in v3:
time: 110 us
  starting transfers between devices  38.2 us (35%)
  waiting for transfers between devices  34.7 us (32%)
  Pallas kernels  27.3 us (25%)
  local copies, waits for them, and re-layouts  7.68 us (7%)
  other arithmetic  1.7 us (2%)
    ppermute x25, starting transfers between devices, swap_expert(): return lax.ppermute(value, 'expert', pairs)  27 us
    pallas_call x17, Pallas kernels, call(): pl.pallas_call(kernel, out_shape=out, in_specs=spec, out_specs=jax.tree.m...  25.3 us
    ppermute x25, waiting for transfers between devices, swap_expert(): return lax.ppermute(value, 'expert', pairs)  22.7 us
    ppermute x10, waiting for transfers between devices, swap_x(): return lax.ppermute(value, 'dp', [(0, 1), (1, 0)])  11.9 us
    ppermute x10, starting transfers between devices, swap_x(): return lax.ppermute(value, 'dp', [(0, 1), (1, 0)])  11.2 us
    unnamed x15, local copies, waits for them, and re-layouts  7.47 us
  transfers between devices with their start and end apart: 35, of which 17 were waited for; matrix products, arithmetic and copies ran while one was open for 1% of the time, Pallas kernels for 23%

profile of v3, /device:TPU:0, one launch (start us, length us, event | category | flops | bytes accessed | tf_op | source)
XLA Modules:
  0.0 110.0 jit_solution(5688441817485516621)
XLA Ops:
  0.0 2.0 %shard_map.64 = (bf16[64,1920]{1,0:T(8,128)(2,1)}, bf16[64,3712]{1,0:T(8,128)(2,1)}) custom-call(s32[1]{0:T(128)} %bitcast.x_ref, bf16[64,3584]{1,0:T(8,128)(2,1)} %tokens_ref.1, s32[8,64]{1,0:T(8,128)} %bitcast.94, s32[8,64]{1,0:T(8,128)} %bitcast.95), custom_call_target="tpu_custom_call" | custom-call | flops 1 | bytes 1 | tf_op jit(solution)/shard_map/pallas_call | solution.py:128
  2.0 3.0 %collective-permute-start.1 = (bf16[64,3712]{1,0:T(8,128)(2,1)}, bf16[64,3712]{1,0:T(8,128)(2,1)}, u32[]{:S(2)}, u32[]{:S(2)}) collective-permute-start(bf16[64,3712]{1,0:T(8,128)(2,1)} %get-tuple-element.69.refs_0_), channel_id=1, source_target_pairs={{0,2},{1,3},{2,0},{3,1},{4,6},{5,7},{6,4},{7,5},{8,10},{9,11},{10,... | collective-permute-start | bytes 1425416 | tf_op jit(solution)/shard_map/w0y/ppermute | solution.py:64
  5.0 1.6 %collective-permute-start = (bf16[64,3712]{1,0:T(8,128)(2,1)}, bf16[64,3712]{1,0:T(8,128)(2,1)}, u32[]{:S(2)}, u32[]{:S(2)}) collective-permute-start(bf16[64,3712]{1,0:T(8,128)(2,1)} %get-tuple-element.69.refs_0_), channel_id=1, source_target_pairs={{0,4},{1,5},{2,6},{3,7},{4,0},{5,1},{6,2},{7,3},{8,12},{9,13},{10,... | collective-permute-start | bytes 1425416 | tf_op jit(solution)/shard_map/w1/ppermute | solution.py:64
  6.6 2.6 %collective-permute-start.2 = (bf16[64,1920]{1,0:T(8,128)(2,1)}, bf16[64,1920]{1,0:T(8,128)(2,1)S(1)}, u32[]{:S(2)}, u32[]{:S(2)}) collective-permute-start(bf16[64,1920]{1,0:T(8,128)(2,1)} %get-tuple-element.70), channel_id=1, source_target_pairs={{0,8},{1,9},{2,10},{3,11},{4,12},{5,13},{6,14},{7,15},{8,0},{9,1},... | collective-permute-start | bytes 737288 | tf_op jit(solution)/shard_map/m2/ppermute | solution.py:64
  9.2 3.1 %copy-done = bf16[1,3584,1024]{2,1,0:T(8,128)(2,1)S(1)} copy-done((bf16[1,3584,1024]{2,1,0:T(8,128)(2,1)S(1)}, bf16[1,3584,1024]{2,1,0:T(8,128)(2,1)}, u32[]{:S(2)}) %copy-start) | copy-done | bytes 7340056
  12.3 3.1 %copy-done.1 = bf16[1,3584,1024]{2,1,0:T(8,128)(2,1)S(1)} copy-done((bf16[1,3584,1024]{2,1,0:T(8,128)(2,1)S(1)}, bf16[1,3584,1024]{2,1,0:T(8,128)(2,1)}, u32[]{:S(2)}) %copy-start.1) | copy-done | bytes 7340056
  15.3 6.7 %collective-permute-done.2.refs_0_ = bf16[64,1920]{1,0:T(8,128)(2,1)S(1)} collective-permute-done((bf16[64,1920]{1,0:T(8,128)(2,1)}, bf16[64,1920]{1,0:T(8,128)(2,1)S(1)}, u32[]{:S(2)}, u32[]{:S(2)}) %collective-permute-start.2) | collective-permute-done | bytes 245792 | tf_op jit(solution)/shard_map/m2/ppermute | solution.py:64
  22.0 1.5 %collective-permute-start.5 = (bf16[64,1920]{1,0:T(8,128)(2,1)S(1)}, bf16[64,1920]{1,0:T(8,128)(2,1)S(1)}, u32[]{:S(2)}, u32[]{:S(2)}) collective-permute-start(bf16[64,1920]{1,0:T(8,128)(2,1)S(1)} %collective-permute-done.2.refs_0_), channel_id=1, source_target_pairs={{0,16},{16,0},{1,17},{17,1},{2,18},{18,2},{3,19},{19,3},{4,20},{20... | collective-permute-start | bytes 737288 | tf_op jit(solution)/shard_map/f2/ppermute | solution.py:81
  24.0 3.4 %collective-permute-start.3 = (bf16[64,1920]{1,0:T(8,128)(2,1)S(1)}, bf16[64,1920]{1,0:T(8,128)(2,1)S(1)}, u32[]{:S(2)}, u32[]{:S(2)}) collective-permute-start(bf16[64,1920]{1,0:T(8,128)(2,1)S(1)} %collective-permute-done.2.refs_0_), channel_id=1, source_target_pairs={{0,4},{1,5},{2,6},{3,7},{4,0},{5,1},{6,2},{7,3},{8,12},{9,13},{10,... | collective-permute-start | bytes 737288 | tf_op jit(solution)/shard_map/m3/ppermute | solution.py:64
  28.4 2.0 %shard_map.66 = (bf16[64,3712]{1,0:T(8,128)(2,1)S(1)}, bf16[64,3712]{1,0:T(8,128)(2,1)S(1)}, bf16[2,64,64]{2,1,0:T(8,128)(2,1)S(1)}) custom-call(s32[1]{0:T(128)} %bitcast.3.me_ref, bf16[64,3712]{1,0:T(8,128)(2,1)S(1)} %copy-done.4, bf16[64,3712]{1,0:T(8,128)(2,1)} %collective-permute-done.1.refs_1_), custom_call_target="tpu_custom_call" | custom-call | flops 34359738368 | bytes 1 | tf_op jit(solution)/shard_map/pallas_call | solution.py:92
  32.1 1.5 %collective-permute-start.9 = (bf16[64,1920]{1,0:T(8,128)(2,1)S(1)}, bf16[64,1920]{1,0:T(8,128)(2,1)S(1)}, u32[]{:S(2)}, u32[]{:S(2)}) collective-permute-start(bf16[64,1920]{1,0:T(8,128)(2,1)S(1)} %collective-permute-done.3.refs_2_), channel_id=1, source_target_pairs={{0,2},{1,3},{2,0},{3,1},{4,6},{5,7},{6,4},{7,5},{8,10},{9,11},{10,... | collective-permute-start | bytes 737288 | tf_op jit(solution)/shard_map/m3y/ppermute | solution.py:64
  33.7 1.5 %collective-permute-start.7 = (bf16[64,1920]{1,0:T(8,128)(2,1)S(1)}, bf16[64,1920]{1,0:T(8,128)(2,1)S(1)}, u32[]{:S(2)}, u32[]{:S(2)}) collective-permute-start(bf16[64,1920]{1,0:T(8,128)(2,1)S(1)} %collective-permute-done.3.refs_2_), channel_id=1, source_target_pairs={{0,16},{16,0},{1,17},{17,1},{2,18},{18,2},{3,19},{19,3},{4,20},{20... | collective-permute-start | bytes 737288 | tf_op jit(solution)/shard_map/f3/ppermute | solution.py:81
  35.2 2.0 %collective-permute-start.10 = (bf16[64,3712]{1,0:T(8,128)(2,1)}, bf16[64,3712]{1,0:T(8,128)(2,1)S(1)}, u32[]{:S(2)}, u32[]{:S(2)}) collective-permute-start(bf16[64,3712]{1,0:T(8,128)(2,1)} %collective-permute-done.1.refs_1_), channel_id=1, source_target_pairs={{0,4},{1,5},{2,6},{3,7},{4,0},{5,1},{6,2},{7,3},{8,12},{9,13},{10,... | collective-permute-start | bytes 1425416 | tf_op jit(solution)/shard_map/w1y/ppermute | solution.py:64
  37.3 2.8 %shard_map.67.hidden_ref = bf16[128,1024]{1,0:T(8,128)(2,1)S(1)} custom-call(s32[2]{0:T(128)S(1)} %pad_add_fusion.scalar_ref, bf16[64,3712]{1,0:T(8,128)(2,1)S(1)} %get-tuple-element.79.keep_ref, bf16[64,3712]{1,0:T(8,128)(2,1)S(1)} %collective-permute-done.6.got_ref, bf16[1,3584,1024]{2,1,0:T(8,128)(2,1)S(1)} %bitcast.93, bf16[1,3584,1024]{2,1,0:T(8,128)(2,1)S(1)} %copy-done.2), custom_call_target="tpu_custom_call" | custom-call | flops 1 | bytes 1 | tf_op jit(solution)/shard_map/pallas_call | solution.py:92
  40.3 1.8 %shard_map.68 = (bf16[4,64,896]{2,1,0:T(8,128)(2,1)S(1)}, bf16[4,64,896]{2,1,0:T(8,128)(2,1)S(1)}) custom-call(s32[2]{0:T(128)S(1)} %pad_add_fusion.scalar_ref, bf16[128,1024]{1,0:T(8,128)(2,1)S(1)} %shard_map.67.hidden_ref, bf16[1,1024,3584]{2,1,0:T(8,128)(2,1)S(1)} %copy-done.3), custom_call_target="tpu_custom_call" | custom-call | flops 1 | bytes 1 | tf_op jit(solution)/shard_map/pallas_call | solution.py:92
  42.2 1.9 %collective-permute-done.7.refs_2_ = bf16[64,1920]{1,0:T(8,128)(2,1)S(1)} collective-permute-done((bf16[64,1920]{1,0:T(8,128)(2,1)S(1)}, bf16[64,1920]{1,0:T(8,128)(2,1)S(1)}, u32[]{:S(2)}, u32[]{:S(2)}) %collective-permute-start.7) | collective-permute-done | bytes 245792 | tf_op jit(solution)/shard_map/f3/ppermute | solution.py:81
  45.2 1.6 %collective-permute-done.10.refs_1_ = bf16[64,3712]{1,0:T(8,128)(2,1)S(1)} collective-permute-done((bf16[64,3712]{1,0:T(8,128)(2,1)}, bf16[64,3712]{1,0:T(8,128)(2,1)S(1)}, u32[]{:S(2)}, u32[]{:S(2)}) %collective-permute-start.10) | collective-permute-done | bytes 475168 | tf_op jit(solution)/shard_map/w1y/ppermute | solution.py:64
  46.8 1.8 %shard_map.70 = (bf16[64,3712]{1,0:T(8,128)(2,1)S(1)}, bf16[64,3712]{1,0:T(8,128)(2,1)S(1)}, bf16[2,64,64]{2,1,0:T(8,128)(2,1)S(1)}) custom-call(s32[1]{0:T(128)} %bitcast.6.me_ref, bf16[64,3712]{1,0:T(8,128)(2,1)} %collective-permute-done.refs_0_, bf16[64,3712]{1,0:T(8,128)(2,1)S(1)} %collective-permute-done.10.refs_1_), custom_call_target="tpu_custom_call" | custom-call | flops 1 | bytes 1 | tf_op jit(solution)/shard_map/pallas_call | solution.py:92
  51.5 2.7 %shard_map.72 = (f32[256,1024]{1,0:T(8,128)S(1)}, f32[256,1024]{1,0:T(8,128)S(1)}) custom-call(s32[2]{0:T(128)S(1)} %pad_add_fusion.scalar_ref, bf16[128,1920]{1,0:T(8,128)(2,1)S(1)} %get-tuple-element.85.keep_ref.refs_2_, bf16[128,1920]{1,0:T(8,128)(2,1)S(1)} %collective-permute-done.12.got_ref.refs_3_, bf16[1,3584,1024]{2,1,0:T(8,128)(2,1)S(1)} %bitcast.93, ...), custom_call_target="tpu_custom_call" | custom-call | flops 1 | bytes 1 | tf_op jit(solution)/shard_map/pallas_call | solution.py:92
  54.2 2.8 %shard_map.73.hidden_ref = bf16[128,1024]{1,0:T(8,128)(2,1)S(1)} custom-call(s32[2]{0:T(128)S(1)} %pad_add_fusion.scalar_ref, bf16[64,3712]{1,0:T(8,128)(2,1)S(1)} %get-tuple-element.87.keep_ref, bf16[64,3712]{1,0:T(8,128)(2,1)S(1)} %collective-permute-done.13.got_ref, bf16[1,3584,1024]{2,1,0:T(8,128)(2,1)S(1)} %bitcast.93, bf16[1,3584,1024]{2,1,0:T(8,128)(2,1)S(1)} %copy-done.2), custom_call_target="tpu_custom_call" | custom-call | flops 1 | bytes 1 | tf_op jit(solution)/shard_map/pallas_call | solution.py:92
  57.8 1.8 %shard_map.75 = (bf16[4,64,896]{2,1,0:T(8,128)(2,1)S(1)}, bf16[4,64,896]{2,1,0:T(8,128)(2,1)S(1)}) custom-call(s32[2]{0:T(128)S(1)} %pad_add_fusion.scalar_ref, bf16[128,1024]{1,0:T(8,128)(2,1)S(1)} %shard_map.73.hidden_ref, bf16[1,1024,3584]{2,1,0:T(8,128)(2,1)S(1)} %copy-done.3), custom_call_target="tpu_custom_call" | custom-call | flops 1 | bytes 1 | tf_op jit(solution)/shard_map/pallas_call | solution.py:92
  60.0 3.0 %shard_map.76.hidden_ref = bf16[256,1024]{1,0:T(8,128)(2,1)S(1)} custom-call(s32[2]{0:T(128)S(1)} %pad_add_fusion.scalar_ref, bf16[128,1792]{1,0:T(8,128)(2,1)S(1)} %get-tuple-element.98.keep_ref, bf16[128,1792]{1,0:T(8,128)(2,1)S(1)} %collective-permute-done.15.got_ref, bf16[1,3584,1024]{2,1,0:T(8,128)(2,1)S(1)} %bitcast.93, ...), custom_call_target="tpu_custom_call" | custom-call | flops 1 | bytes 1 | tf_op jit(solution)/shard_map/pallas_call | solution.py:92
  63.0 1.8 %shard_map.77 = (bf16[2,128,896]{2,1,0:T(8,128)(2,1)S(1)}, bf16[2,128,896]{2,1,0:T(8,128)(2,1)S(1)}) custom-call(s32[2]{0:T(128)S(1)} %pad_add_fusion.scalar_ref, bf16[256,1024]{1,0:T(8,128)(2,1)S(1)} %shard_map.76.hidden_ref, bf16[1,1024,3584]{2,1,0:T(8,128)(2,1)S(1)} %copy-done.3, f32[16,128]{1,0:T(8,128)S(1)} %shard_map.65.refs_0_), custom_call_target="tpu_custom_call" | custom-call | flops 1 | bytes 1 | tf_op jit(solution)/shard_map/pallas_call | solution.py:92
  65.4 1.8 %shard_map.80 = (bf16[2,128,896]{2,1,0:T(8,128)(2,1)S(1)}, bf16[2,128,896]{2,1,0:T(8,128)(2,1)S(1)}) custom-call(s32[2]{0:T(128)S(1)} %pad_add_fusion.scalar_ref, bf16[256,1024]{1,0:T(8,128)(2,1)S(1)} %shard_map.76.hidden_ref, bf16[1,1024,3584]{2,1,0:T(8,128)(2,1)S(1)} %copy-done.3), custom_call_target="tpu_custom_call" | custom-call | flops 1 | bytes 1 | tf_op jit(solution)/shard_map/pallas_call | solution.py:92
  72.5 3.3 %collective-permute-done.20 = bf16[2,64,896]{2,1,0:T(8,128)(2,1)S(1)} collective-permute-done((bf16[2,64,896]{2,1,0:T(8,128)(2,1)S(1)}, bf16[2,64,896]{2,1,0:T(8,128)(2,1)S(1)}, u32[]{:S(2)}, u32[]{:S(2)}) %collective-permute-start.20) | collective-permute-done | bytes 229408 | tf_op jit(solution)/shard_map/a3/ppermute | solution.py:81
  75.8 2.3 %collective-permute-done.21 = bf16[2,64,896]{2,1,0:T(8,128)(2,1)S(1)} collective-permute-done((bf16[2,64,896]{2,1,0:T(8,128)(2,1)S(1)}, bf16[2,64,896]{2,1,0:T(8,128)(2,1)S(1)}, u32[]{:S(2)}, u32[]{:S(2)}) %collective-permute-start.21) | collective-permute-done | bytes 229408 | tf_op jit(solution)/shard_map/b3/ppermute | solution.py:64
  78.2 1.6 %collective-permute-start.25 = (bf16[64,896]{1,0:T(8,128)(2,1)S(1)}, bf16[64,896]{1,0:T(8,128)(2,1)S(1)}, u32[]{:S(2)}, u32[]{:S(2)}) collective-permute-start(bf16[64,896]{1,0:T(8,128)(2,1)S(1)} %slice_bitcast_fusion.14), channel_id=1, source_target_pairs={{0,16},{16,0},{1,17},{17,1},{2,18},{18,2},{3,19},{19,3},{4,20},{20... | collective-permute-start | bytes 344072 | tf_op jit(solution)/shard_map/q3/ppermute | solution.py:81
  81.6 2.7 %collective-permute-done.25 = bf16[64,896]{1,0:T(8,128)(2,1)S(1)} collective-permute-done((bf16[64,896]{1,0:T(8,128)(2,1)S(1)}, bf16[64,896]{1,0:T(8,128)(2,1)S(1)}, u32[]{:S(2)}, u32[]{:S(2)}) %collective-permute-start.25) | collective-permute-done | bytes 114720 | tf_op jit(solution)/shard_map/q3/ppermute | solution.py:81
  87.2 4.9 %collective-permute-done.17 = bf16[2,2,64,896]{3,2,1,0:T(8,128)(2,1)S(1)} collective-permute-done((bf16[2,2,64,896]{3,2,1,0:T(8,128)(2,1)S(1)}, bf16[2,2,64,896]{3,2,1,0:T(8,128)(2,1)S(1)}, u32[]{:S(2)}, u32[]{:S(2)}) %collective-permute-start.17) | collective-permute-done | bytes 458784 | tf_op jit(solution)/shard_map/n0/ppermute | solution.py:64
  92.6 1.5 %collective-permute-start.31 = (bf16[64,896]{1,0:T(8,128)(2,1)S(1)}, bf16[64,896]{1,0:T(8,128)(2,1)S(1)}, u32[]{:S(2)}, u32[]{:S(2)}) collective-permute-start(bf16[64,896]{1,0:T(8,128)(2,1)S(1)} %slice_bitcast_fusion.11), channel_id=1, source_target_pairs={{0,16},{16,0},{1,17},{17,1},{2,18},{18,2},{3,19},{19,3},{4,20},{20... | collective-permute-start | bytes 344072 | tf_op jit(solution)/shard_map/q2/ppermute | solution.py:81
  103.0 1.6 %collective-permute-start.32 = (bf16[64,896]{1,0:T(8,128)(2,1)S(1)}, bf16[64,896]{1,0:T(8,128)(2,1)S(1)}, u32[]{:S(2)}, u32[]{:S(2)}) collective-permute-start(bf16[64,896]{1,0:T(8,128)(2,1)S(1)} %slice_bitcast_fusion.8), channel_id=1, source_target_pairs={{0,2},{1,3},{2,0},{3,1},{4,6},{5,7},{6,4},{7,5},{8,10},{9,11},{10,... | collective-permute-start | bytes 344072 | tf_op jit(solution)/shard_map/np/ppermute | solution.py:64
  104.6 2.4 %collective-permute-done.33 = bf16[64,896]{1,0:T(8,128)(2,1)S(1)} collective-permute-done((bf16[64,896]{1,0:T(8,128)(2,1)S(1)}, bf16[64,896]{1,0:T(8,128)(2,1)S(1)}, u32[]{:S(2)}, u32[]{:S(2)}) %collective-permute-start.33) | collective-permute-done | bytes 114720 | tf_op jit(solution)/shard_map/nq/ppermute | solution.py:81
  (100 shorter events, 31.6 us)
Async XLA Ops:
  2.0 20.0 %collective-permute-start.1 = (bf16[64,3712]{1,0:T(8,128)(2,1)}, bf16[64,3712]{1,0:T(8,128)(2,1)}, u32[]{:S(2)}, u32[]{:S(2)}) collective-permute-start(bf16[64,3712]{1,0:T(8,128)(2,1)} %get-tuple-element.69.refs_0_), channel_id=1, source_target_pairs={{0,2},{1,3},{2,0},{3,1},{4,6},{5,7},{6,4},{7,5},{8,10},{9,11},{10,... | collective-permute-start | bytes 1425416 | tf_op jit(solution)/shard_map/w0y/ppermute | solution.py:64
  5.0 22.4 %collective-permute-start = (bf16[64,3712]{1,0:T(8,128)(2,1)}, bf16[64,3712]{1,0:T(8,128)(2,1)}, u32[]{:S(2)}, u32[]{:S(2)}) collective-permute-start(bf16[64,3712]{1,0:T(8,128)(2,1)} %get-tuple-element.69.refs_0_), channel_id=1, source_target_pairs={{0,4},{1,5},{2,6},{3,7},{4,0},{5,1},{6,2},{7,3},{8,12},{9,13},{10,... | collective-permute-start | bytes 1425416 | tf_op jit(solution)/shard_map/w1/ppermute | solution.py:64
  6.6 15.4 %collective-permute-start.2 = (bf16[64,1920]{1,0:T(8,128)(2,1)}, bf16[64,1920]{1,0:T(8,128)(2,1)S(1)}, u32[]{:S(2)}, u32[]{:S(2)}) collective-permute-start(bf16[64,1920]{1,0:T(8,128)(2,1)} %get-tuple-element.70), channel_id=1, source_target_pairs={{0,8},{1,9},{2,10},{3,11},{4,12},{5,13},{6,14},{7,15},{8,0},{9,1},... | collective-permute-start | bytes 737288 | tf_op jit(solution)/shard_map/m2/ppermute | solution.py:64
  22.0 8.4 %collective-permute-start.5 = (bf16[64,1920]{1,0:T(8,128)(2,1)S(1)}, bf16[64,1920]{1,0:T(8,128)(2,1)S(1)}, u32[]{:S(2)}, u32[]{:S(2)}) collective-permute-start(bf16[64,1920]{1,0:T(8,128)(2,1)S(1)} %collective-permute-done.2.refs_0_), channel_id=1, source_target_pairs={{0,16},{16,0},{1,17},{17,1},{2,18},{18,2},{3,19},{19,3},{4,20},{20... | collective-permute-start | bytes 737288 | tf_op jit(solution)/shard_map/f2/ppermute | solution.py:81
  23.5 7.0 %collective-permute-start.4 = (bf16[64,1920]{1,0:T(8,128)(2,1)S(1)}, bf16[64,1920]{1,0:T(8,128)(2,1)S(1)}, u32[]{:S(2)}, u32[]{:S(2)}) collective-permute-start(bf16[64,1920]{1,0:T(8,128)(2,1)S(1)} %collective-permute-done.2.refs_0_), channel_id=1, source_target_pairs={{0,2},{1,3},{2,0},{3,1},{4,6},{5,7},{6,4},{7,5},{8,10},{9,11},{10,... | collective-permute-start | bytes 737288 | tf_op jit(solution)/shard_map/m2y/ppermute | solution.py:64
  24.0 7.6 %collective-permute-start.3 = (bf16[64,1920]{1,0:T(8,128)(2,1)S(1)}, bf16[64,1920]{1,0:T(8,128)(2,1)S(1)}, u32[]{:S(2)}, u32[]{:S(2)}) collective-permute-start(bf16[64,1920]{1,0:T(8,128)(2,1)S(1)} %collective-permute-done.2.refs_0_), channel_id=1, source_target_pairs={{0,4},{1,5},{2,6},{3,7},{4,0},{5,1},{6,2},{7,3},{8,12},{9,13},{10,... | collective-permute-start | bytes 737288 | tf_op jit(solution)/shard_map/m3/ppermute | solution.py:64
  30.4 6.8 %collective-permute-start.6 = (bf16[64,3712]{1,0:T(8,128)(2,1)S(1)}, bf16[64,3712]{1,0:T(8,128)(2,1)S(1)}, u32[]{:S(2)}, u32[]{:S(2)}) collective-permute-start(bf16[64,3712]{1,0:T(8,128)(2,1)S(1)} %get-tuple-element.81), channel_id=1, source_target_pairs={{0,1},{1,0},{2,3},{3,2},{4,5},{5,4},{6,7},{7,6},{8,9},{9,8},{10,11... | collective-permute-start | bytes 1425416 | tf_op jit(solution)/shard_map/rows_0/ppermute | solution.py:64
  31.6 10.6 %collective-permute-start.8 = (bf16[64,1920]{1,0:T(8,128)(2,1)S(1)}, bf16[64,1920]{1,0:T(8,128)(2,1)S(1)}, u32[]{:S(2)}, u32[]{:S(2)}) collective-permute-start(bf16[64,1920]{1,0:T(8,128)(2,1)S(1)} %collective-permute-done.4.refs_1_), channel_id=1, source_target_pairs={{0,16},{16,0},{1,17},{17,1},{2,18},{18,2},{3,19},{19,3},{4,20},{20... | collective-permute-start | bytes 737288 | tf_op jit(solution)/shard_map/f2y/ppermute | solution.py:81
  32.1 10.0 %collective-permute-start.9 = (bf16[64,1920]{1,0:T(8,128)(2,1)S(1)}, bf16[64,1920]{1,0:T(8,128)(2,1)S(1)}, u32[]{:S(2)}, u32[]{:S(2)}) collective-permute-start(bf16[64,1920]{1,0:T(8,128)(2,1)S(1)} %collective-permute-done.3.refs_2_), channel_id=1, source_target_pairs={{0,2},{1,3},{2,0},{3,1},{4,6},{5,7},{6,4},{7,5},{8,10},{9,11},{10,... | collective-permute-start | bytes 737288 | tf_op jit(solution)/shard_map/m3y/ppermute | solution.py:64
  33.7 10.5 %collective-permute-start.7 = (bf16[64,1920]{1,0:T(8,128)(2,1)S(1)}, bf16[64,1920]{1,0:T(8,128)(2,1)S(1)}, u32[]{:S(2)}, u32[]{:S(2)}) collective-permute-start(bf16[64,1920]{1,0:T(8,128)(2,1)S(1)} %collective-permute-done.3.refs_2_), channel_id=1, source_target_pairs={{0,16},{16,0},{1,17},{17,1},{2,18},{18,2},{3,19},{19,3},{4,20},{20... | collective-permute-start | bytes 737288 | tf_op jit(solution)/shard_map/f3/ppermute | solution.py:81
  35.2 11.5 %collective-permute-start.10 = (bf16[64,3712]{1,0:T(8,128)(2,1)}, bf16[64,3712]{1,0:T(8,128)(2,1)S(1)}, u32[]{:S(2)}, u32[]{:S(2)}) collective-permute-start(bf16[64,3712]{1,0:T(8,128)(2,1)} %collective-permute-done.1.refs_1_), channel_id=1, source_target_pairs={{0,4},{1,5},{2,6},{3,7},{4,0},{5,1},{6,2},{7,3},{8,12},{9,13},{10,... | collective-permute-start | bytes 1425416 | tf_op jit(solution)/shard_map/w1y/ppermute | solution.py:64
  45.1 6.4 %collective-permute-start.12 = (bf16[128,1920]{1,0:T(8,128)(2,1)S(1)}, bf16[128,1920]{1,0:T(8,128)(2,1)S(1)}, u32[]{:S(2)}, u32[]{:S(2)}) collective-permute-start(bf16[128,1920]{1,0:T(8,128)(2,1)S(1)} %get-tuple-element.93), channel_id=1, source_target_pairs={{0,1},{1,0},{2,3},{3,2},{4,5},{5,4},{6,7},{7,6},{8,9},{9,8},{10,11... | collective-permute-start | bytes 1474568 | tf_op jit(solution)/shard_map/rows_m/ppermute | solution.py:64
  48.6 5.6 %collective-permute-start.13 = (bf16[64,3712]{1,0:T(8,128)(2,1)S(1)}, bf16[64,3712]{1,0:T(8,128)(2,1)S(1)}, u32[]{:S(2)}, u32[]{:S(2)}) collective-permute-start(bf16[64,3712]{1,0:T(8,128)(2,1)S(1)} %get-tuple-element.96), channel_id=1, source_target_pairs={{0,1},{1,0},{2,3},{3,2},{4,5},{5,4},{6,7},{7,6},{8,9},{9,8},{10,11... | collective-permute-start | bytes 1425416 | tf_op jit(solution)/shard_map/rows_1/ppermute | solution.py:64
  49.2 7.9 %collective-permute-start.14 = (bf16[64,1920]{1,0:T(8,128)(2,1)S(1)}, bf16[64,1920]{1,0:T(8,128)(2,1)S(1)}, u32[]{:S(2)}, u32[]{:S(2)}) collective-permute-start(bf16[64,1920]{1,0:T(8,128)(2,1)S(1)} %collective-permute-done.9.refs_3_), channel_id=1, source_target_pairs={{0,16},{16,0},{1,17},{17,1},{2,18},{18,2},{3,19},{19,3},{4,20},{20... | collective-permute-start | bytes 737288 | tf_op jit(solution)/shard_map/f3y/ppermute | solution.py:81
  59.6 5.4 %collective-permute-start.16 = (bf16[4,64,896]{2,1,0:T(8,128)(2,1)S(1)}, bf16[4,64,896]{2,1,0:T(8,128)(2,1)S(1)}, u32[]{:S(2)}, u32[]{:S(2)}) collective-permute-start(bf16[4,64,896]{2,1,0:T(8,128)(2,1)S(1)} %get-tuple-element.106), channel_id=1, source_target_pairs={{0,1},{1,0},{2,3},{3,2},{4,5},{5,4},{6,7},{7,6},{8,9},{9,8},{10,11... | collective-permute-start | bytes 1376264 | tf_op jit(solution)/shard_map/back_1/ppermute | solution.py:64
  67.2 3.7 %collective-permute-start.19 = (bf16[2,128,896]{2,1,0:T(8,128)(2,1)S(1)}, bf16[2,128,896]{2,1,0:T(8,128)(2,1)S(1)}, u32[]{:S(2)}, u32[]{:S(2)}) collective-permute-start(bf16[2,128,896]{2,1,0:T(8,128)(2,1)S(1)} %get-tuple-element.113), channel_id=1, source_target_pairs={{0,1},{1,0},{2,3},{3,2},{4,5},{5,4},{6,7},{7,6},{8,9},{9,8},{10,11... | collective-permute-start | bytes 1376264 | tf_op jit(solution)/shard_map/back_b/ppermute | solution.py:64
  68.0 7.7 %collective-permute-start.20 = (bf16[2,64,896]{2,1,0:T(8,128)(2,1)S(1)}, bf16[2,64,896]{2,1,0:T(8,128)(2,1)S(1)}, u32[]{:S(2)}, u32[]{:S(2)}) collective-permute-start(bf16[2,64,896]{2,1,0:T(8,128)(2,1)S(1)} %get-tuple-element.115), channel_id=1, source_target_pairs={{0,16},{16,0},{1,17},{17,1},{2,18},{18,2},{3,19},{19,3},{4,20},{20... | collective-permute-start | bytes 688136 | tf_op jit(solution)/shard_map/a3/ppermute | solution.py:81
  68.8 23.6 %collective-permute-start.27 = (bf16[2,2,64,896]{3,2,0,1:T(8,128)(2,1)S(1)}, bf16[2,2,64,896]{3,2,0,1:T(8,128)(2,1)S(1)}, u32[]{:S(2)}, u32[]{:S(2)}) collective-permute-start(bf16[2,2,64,896]{3,2,0,1:T(8,128)(2,1)S(1)} %copy.10), channel_id=1, source_target_pairs={{0,4},{1,5},{2,6},{3,7},{4,0},{5,1},{6,2},{7,3},{8,12},{9,13},{10,... | collective-permute-start | bytes 1376264 | tf_op jit(solution)/shard_map/n1/ppermute | solution.py:64
  70.2 21.9 %collective-permute-start.17 = (bf16[2,2,64,896]{3,2,1,0:T(8,128)(2,1)S(1)}, bf16[2,2,64,896]{3,2,1,0:T(8,128)(2,1)S(1)}, u32[]{:S(2)}, u32[]{:S(2)}) collective-permute-start(bf16[2,2,64,896]{3,2,1,0:T(8,128)(2,1)S(1)} %get-tuple-element.134), channel_id=1, source_target_pairs={{0,4},{1,5},{2,6},{3,7},{4,0},{5,1},{6,2},{7,3},{8,12},{9,13},{10,... | collective-permute-start | bytes 1376264 | tf_op jit(solution)/shard_map/n0/ppermute | solution.py:64
  71.3 6.8 %collective-permute-start.21 = (bf16[2,64,896]{2,1,0:T(8,128)(2,1)S(1)}, bf16[2,64,896]{2,1,0:T(8,128)(2,1)S(1)}, u32[]{:S(2)}, u32[]{:S(2)}) collective-permute-start(bf16[2,64,896]{2,1,0:T(8,128)(2,1)S(1)} %get-tuple-element.117), channel_id=1, source_target_pairs={{0,2},{1,3},{2,0},{3,1},{4,6},{5,7},{6,4},{7,5},{8,10},{9,11},{10,... | collective-permute-start | bytes 688136 | tf_op jit(solution)/shard_map/b3/ppermute | solution.py:64
  78.2 6.1 %collective-permute-start.25 = (bf16[64,896]{1,0:T(8,128)(2,1)S(1)}, bf16[64,896]{1,0:T(8,128)(2,1)S(1)}, u32[]{:S(2)}, u32[]{:S(2)}) collective-permute-start(bf16[64,896]{1,0:T(8,128)(2,1)S(1)} %slice_bitcast_fusion.14), channel_id=1, source_target_pairs={{0,16},{16,0},{1,17},{17,1},{2,18},{18,2},{3,19},{19,3},{4,20},{20... | collective-permute-start | bytes 344072 | tf_op jit(solution)/shard_map/q3/ppermute | solution.py:81
  79.8 6.1 %collective-permute-start.24 = (bf16[64,896]{1,0:T(8,128)(2,1)S(1)}, bf16[64,896]{1,0:T(8,128)(2,1)S(1)}, u32[]{:S(2)}, u32[]{:S(2)}) collective-permute-start(bf16[64,896]{1,0:T(8,128)(2,1)S(1)} %slice_bitcast_fusion.15), channel_id=1, source_target_pairs={{0,2},{1,3},{2,0},{3,1},{4,6},{5,7},{6,4},{7,5},{8,10},{9,11},{10,... | collective-permute-start | bytes 344072 | tf_op jit(solution)/shard_map/p3/ppermute | solution.py:64
  80.4 11.8 %collective-permute-start.22 = (bf16[2,64,896]{2,1,0:T(8,128)(2,1)S(1)}, bf16[2,64,896]{2,1,0:T(8,128)(2,1)S(1)}, u32[]{:S(2)}, u32[]{:S(2)}) collective-permute-start(bf16[2,64,896]{2,1,0:T(8,128)(2,1)S(1)} %get-tuple-element.118), channel_id=1, source_target_pairs={{0,16},{16,0},{1,17},{17,1},{2,18},{18,2},{3,19},{19,3},{4,20},{20... | collective-permute-start | bytes 688136 | tf_op jit(solution)/shard_map/a2/ppermute | solution.py:81
  84.3 7.8 %collective-permute-start.23 = (bf16[2,64,896]{2,1,0:T(8,128)(2,1)S(1)}, bf16[2,64,896]{2,1,0:T(8,128)(2,1)S(1)}, u32[]{:S(2)}, u32[]{:S(2)}) collective-permute-start(bf16[2,64,896]{2,1,0:T(8,128)(2,1)S(1)} %get-tuple-element.119), channel_id=1, source_target_pairs={{0,2},{1,3},{2,0},{3,1},{4,6},{5,7},{6,4},{7,5},{8,10},{9,11},{10,... | collective-permute-start | bytes 688136 | tf_op jit(solution)/shard_map/b2/ppermute | solution.py:64
  86.0 10.8 %collective-permute-start.29 = (bf16[2,64,896]{2,1,0:T(8,128)(2,1)S(1)}, bf16[2,64,896]{2,1,0:T(8,128)(2,1)S(1)}, u32[]{:S(2)}, u32[]{:S(2)}) collective-permute-start(bf16[2,64,896]{2,1,0:T(8,128)(2,1)S(1)} %pad_maximum_fusion), channel_id=1, source_target_pairs={{0,4},{1,5},{2,6},{3,7},{4,0},{5,1},{6,2},{7,3},{8,12},{9,13},{10,... | collective-permute-start | bytes 688136 | tf_op jit(solution)/shard_map/s3/ppermute | solution.py:64
  92.6 5.7 %collective-permute-start.31 = (bf16[64,896]{1,0:T(8,128)(2,1)S(1)}, bf16[64,896]{1,0:T(8,128)(2,1)S(1)}, u32[]{:S(2)}, u32[]{:S(2)}) collective-permute-start(bf16[64,896]{1,0:T(8,128)(2,1)S(1)} %slice_bitcast_fusion.11), channel_id=1, source_target_pairs={{0,16},{16,0},{1,17},{17,1},{2,18},{18,2},{3,19},{19,3},{4,20},{20... | collective-permute-start | bytes 344072 | tf_op jit(solution)/shard_map/q2/ppermute | solution.py:81
  94.1 5.1 %collective-permute-start.30 = (bf16[64,896]{1,0:T(8,128)(2,1)S(1)}, bf16[64,896]{1,0:T(8,128)(2,1)S(1)}, u32[]{:S(2)}, u32[]{:S(2)}) collective-permute-start(bf16[64,896]{1,0:T(8,128)(2,1)S(1)} %slice_bitcast_fusion.12), channel_id=1, source_target_pairs={{0,2},{1,3},{2,0},{3,1},{4,6},{5,7},{6,4},{7,5},{8,10},{9,11},{10,... | collective-permute-start | bytes 344072 | tf_op jit(solution)/shard_map/p2/ppermute | solution.py:64
  94.7 6.1 %collective-permute-start.26 = (bf16[2,64,896]{2,1,0:T(8,128)(2,1)S(1)}, bf16[2,64,896]{2,1,0:T(8,128)(2,1)S(1)}, u32[]{:S(2)}, u32[]{:S(2)}) collective-permute-start(bf16[2,64,896]{2,1,0:T(8,128)(2,1)S(1)} %slice_bitcast_fusion.2), channel_id=1, source_target_pairs={{0,16},{16,0},{1,17},{17,1},{2,18},{18,2},{3,19},{19,3},{4,20},{20... | collective-permute-start | bytes 688136 | tf_op jit(solution)/shard_map/n/ppermute | solution.py:81
  95.9 6.0 %collective-permute-start.28 = (bf16[2,64,896]{2,1,0:T(8,128)(2,1)S(1)}, bf16[2,64,896]{2,1,0:T(8,128)(2,1)S(1)}, u32[]{:S(2)}, u32[]{:S(2)}) collective-permute-start(bf16[2,64,896]{2,1,0:T(8,128)(2,1)S(1)} %slice_bitcast_fusion.1), channel_id=1, source_target_pairs={{0,2},{1,3},{2,0},{3,1},{4,6},{5,7},{6,4},{7,5},{8,10},{9,11},{10,... | collective-permute-start | bytes 688136 | tf_op jit(solution)/shard_map/o/ppermute | solution.py:64
  99.4 9.8 %collective-permute-start.34 = (bf16[2,64,896]{2,1,0:T(8,128)(2,1)S(1)}, bf16[2,64,896]{2,1,0:T(8,128)(2,1)S(1)}, u32[]{:S(2)}, u32[]{:S(2)}) collective-permute-start(bf16[2,64,896]{2,1,0:T(8,128)(2,1)S(1)} %pad_maximum_fusion.1), channel_id=1, source_target_pairs={{0,8},{1,9},{2,10},{3,11},{4,12},{5,13},{6,14},{7,15},{8,0},{9,1},... | collective-permute-start | bytes 688136 | tf_op jit(solution)/shard_map/s2/ppermute | solution.py:64
  102.1 4.9 %collective-permute-start.33 = (bf16[64,896]{1,0:T(8,128)(2,1)S(1)}, bf16[64,896]{1,0:T(8,128)(2,1)S(1)}, u32[]{:S(2)}, u32[]{:S(2)}) collective-permute-start(bf16[64,896]{1,0:T(8,128)(2,1)S(1)} %slice_bitcast_fusion.6), channel_id=1, source_target_pairs={{0,16},{16,0},{1,17},{17,1},{2,18},{18,2},{3,19},{19,3},{4,20},{20... | collective-permute-start | bytes 344072 | tf_op jit(solution)/shard_map/nq/ppermute | solution.py:81
  103.0 4.9 %collective-permute-start.32 = (bf16[64,896]{1,0:T(8,128)(2,1)S(1)}, bf16[64,896]{1,0:T(8,128)(2,1)S(1)}, u32[]{:S(2)}, u32[]{:S(2)}) collective-permute-start(bf16[64,896]{1,0:T(8,128)(2,1)S(1)} %slice_bitcast_fusion.8), channel_id=1, source_target_pairs={{0,2},{1,3},{2,0},{3,1},{4,6},{5,7},{6,4},{7,5},{8,10},{9,11},{10,... | collective-permute-start | bytes 344072 | tf_op jit(solution)/shard_map/np/ppermute | solution.py:64
  (10 other events, 57.6 us)

commit v4 on v3

--- a/solution.py
+++ b/solution.py
@@ -81,6 +81,17 @@
         return lax.ppermute(value, "dp", [(0, 1), (1, 0)])
 
 
+def swap_xy(value, first, name):
+    pairs = []
+    experts = NZ * NY * NC
+    for x in range(2):
+        for e in range(experts):
+            along_x = (e % NC == 0) == first
+            pairs.append((x * experts + e, (1 - x) * experts + e if along_x else x * experts + (e ^ NC)))
+    with jax.named_scope(name):
+        return lax.ppermute(value, ("dp", "expert"), pairs)
+
+
 COST = pl.CostEstimate(flops=1, bytes_accessed=1, transcendentals=0)
 MUCH = pl.CostEstimate(flops=1 << 35, bytes_accessed=1, transcendentals=0)
 
@@ -103,12 +114,10 @@
     rows, width = tokens.shape
     half = width // 2
 
-    def kernel(x_ref, tokens_ref, ids_ref, numerators_ref, mine, whole):
+    def kernel(x_ref, tokens_ref, ids_ref, numerators_ref, mine, far):
         side = x_ref[0]
-        near = tokens_ref[:, pl.ds(pl.multiple_of(side * half, 128), half)]
-        mine[:, :half] = near
-        whole[:, :half] = near
-        whole[:, half + TABLE :] = tokens_ref[:, pl.ds(pl.multiple_of((1 - side) * half, 128), half)]
+        mine[:, :half] = tokens_ref[:, pl.ds(pl.multiple_of(side * half, 128), half)]
+        far[...] = tokens_ref[:, pl.ds(pl.multiple_of((1 - side) * half, 128), half)]
         column = lax.broadcasted_iota(jnp.int32, (TABLE, rows), 0)
         expert = jnp.where(column < TABLE // 2, column, column - TABLE // 2)
         total = jnp.zeros((TABLE, rows), jnp.int32)
@@ -116,13 +125,11 @@
             total += jnp.where(expert == ids_ref[pl.ds(k, 1)], numerators_ref[pl.ds(k, 1)], 0)
         high = lax.shift_right_logical(total, 5)
         code = jnp.where(column < TABLE // 2, high, total - high * 32)
-        table = code.astype(F32).T.astype(BF)
-        mine[:, half:] = table
-        whole[:, half : half + TABLE] = table
+        mine[:, half:] = code.astype(F32).T.astype(BF)
 
     out = (
         jax.ShapeDtypeStruct((rows, half + TABLE), BF),
-        jax.ShapeDtypeStruct((rows, width + TABLE), BF),
+        jax.ShapeDtypeStruct((rows, half), BF),
     )
     vmem = pl.BlockSpec(memory_space=pltpu.VMEM)
     return pl.pallas_call(
@@ -141,20 +148,51 @@
     return jnp.dot(table, code.astype(BF), preferred_element_type=F32)
 
 
-def select(me, room, half, blocks, cost=COST):
-    rows, full = blocks[0].shape
+def chooser(refs, layout, core):
+    def read(n, columns=slice(None)):
+        piece = layout[n]
+        if isinstance(piece, tuple):
+            return jnp.where(core == 0, refs[piece[0]][:, columns], refs[piece[1]][:, columns])
+        return refs[piece][:, columns]
+
+    return read
+
+
+def flatten(pieces):
+    arrays, layout = [], []
+
+    def number(array):
+        for n, other in enumerate(arrays):
+            if other is array:
+                return n
+        arrays.append(array)
+        return len(arrays) - 1
+
+    for piece in pieces:
+        layout.append(tuple(number(p) for p in piece) if isinstance(piece, tuple) else number(piece))
+    return arrays, layout
+
+
+def select(me, room, half, blocks, join=False, cost=COST):
     count = len(blocks)
+    rows = blocks[0][0].shape[0]
+    arrays, layout = flatten([piece for block in blocks for piece in block])
+    widths = [arrays[n[0] if isinstance(n, tuple) else n].shape[1] for n in layout]
+    start_of = [sum(len(block) for block in blocks[:b]) for b in range(count)]
+    full = sum(widths[: len(blocks[0])])
 
     def kernel(me_ref, *refs):
-        keep, give, put_ref = refs[-3:]
+        keep, give, put_ref = refs[-4:-1] if join else refs[-3:]
         mine = me_ref[0]
+        read = chooser(refs, layout, mine % NC)
         before = lax.broadcasted_iota(jnp.int32, (rows, rows), 1) < lax.broadcasted_iota(
             jnp.int32, (rows, rows), 0
         )
         before = jnp.where(before, 1.0, 0.0).astype(BF)
         slot = lax.broadcasted_iota(jnp.int32, (rows, 2 * room), 1)
         first = slot < room
-        chosen = [jnp.where(lookup(ref[:, half : half + TABLE], mine) > 0, 1.0, 0.0) for ref in refs[:count]]
+        tables = [read(n, slice(half, half + TABLE)) for n in start_of]
+        chosen = [jnp.where(lookup(table, mine) > 0, 1.0, 0.0) for table in tables]
         place = [jnp.dot(before, c.astype(BF), preferred_element_type=F32) for c in chosen]
         put = []
         for c, p in zip(chosen, place, strict=True):
@@ -164,28 +202,39 @@
         pick = [p.T.astype(BF) for p in put]
         for b in range(count):
             put_ref[b] = put[b].astype(BF)
-            got = jnp.dot(pick[b], refs[b][...], preferred_element_type=F32).astype(BF)
+            start = 0
+            for n in range(start_of[b], start_of[b] + len(blocks[b])):
+                columns = slice(start, start + widths[n])
+                value = read(n)
+                got = jnp.dot(pick[b], value, preferred_element_type=F32).astype(BF)
+                keep[pl.ds(b * room, room), columns] = got[:room]
+                give[pl.ds(b * room, room), columns] = got[room:]
+                if join and b == count - 1:
+                    refs[-1][:, columns] = value
+                start += widths[n]
+
+    out = jax.ShapeDtypeStruct((count * room, full), BF)
+    put = jax.ShapeDtypeStruct((count, rows, 2 * room), BF)
+    last = (jax.ShapeDtypeStruct((rows, full), BF),) if join else ()
+    return call(kernel, (out, out, put, *last), [me.reshape(1), *arrays], cost)
+
+
+def select_far(me, put, half, pieces):
+    rows = put.shape[1]
+    room = put.shape[2] // 2
+    arrays, layout = flatten(pieces)
+
+    def kernel(me_ref, put_ref, *refs):
+        keep, give = refs[-2:]
+        read = chooser(refs, layout, me_ref[0] % NC)
+        for b in range(len(pieces)):
+            pick = put_ref[b].astype(F32).T.astype(BF)
+            got = jnp.dot(pick, read(b, slice(0, half)), preferred_element_type=F32).astype(BF)
             keep[pl.ds(b * room, room)] = got[:room]
             give[pl.ds(b * room, room)] = got[room:]
 
-    out = jax.ShapeDtypeStruct((count * room, full), BF)
-    put = jax.ShapeDtypeStruct((count, rows, 2 * room), BF)
-    return call(kernel, (out, out, put), [me.reshape(1), *blocks], cost)
-
-
-def select_far(put, half, blocks):
-    room = put.shape[2] // 2
-
-    def kernel(put_ref, *refs):
-        keep, give = refs[-2:]
-        for b, ref in enumerate(refs[:-2]):
-            pick = put_ref[b].astype(F32).T.astype(BF)
-            got = jnp.dot(pick, ref[:, :half], preferred_element_type=F32).astype(BF)
-            keep[pl.ds(b * room, room)] = got[:room]
-            give[pl.ds(b * room, room)] = got[room:]
-
-    out = jax.ShapeDtypeStruct((len(blocks) * room, half), BF)
-    return call(kernel, (out, out), [put, *blocks])
+    out = jax.ShapeDtypeStruct((len(pieces) * room, half), BF)
+    return call(kernel, (out, out), [me.reshape(1), put, *arrays])
 
 
 def touch(*weights):
@@ -245,60 +294,48 @@
     return call(kernel, out, [scalars, keep, got, gate, up, *first, *tokens])
 
 
-def down(scalars, hidden, weights, quarters, *tokens):
+def down(scalars, hidden, weights, part, parts, *tokens):
     rows, depth = hidden.shape
-    tile = weights.shape[2] // 4
+    size = rows // 2 // parts
+    tile = weights.shape[2] // 2
 
     def kernel(scalar_ref, hidden_ref, down_ref, *refs):
         near, away = refs[-2:]
         x = scalar_ref[0]
-        for n in range(2 * len(quarters)):
-            side = x if n % 2 else 1 - x
-            start = (2 * side + quarters[n // 2]) * tile
-            weight = down_ref[0, :, pl.ds(pl.multiple_of(start, 128), tile)]
-            value = jnp.dot(hidden_ref[...], weight, preferred_element_type=F32).astype(BF)
-            near[n] = value[: rows // 2]
-            away[n] = value[rows // 2 :]
-
-    out = jax.ShapeDtypeStruct((2 * len(quarters), rows // 2, tile), BF)
+        value = jnp.concatenate(
+            [hidden_ref[start : start + size] for start in (part * size, rows // 2 + part * size)], axis=0
+        )
+        for n in range(2):
+            side = x if n else 1 - x
+            weight = down_ref[0, :, pl.ds(pl.multiple_of(side * tile, 128), tile)]
+            got = jnp.dot(value, weight, preferred_element_type=F32).astype(BF)
+            near[n] = got[:size]
+            away[n] = got[size:]
+
+    out = jax.ShapeDtypeStruct((2, size, tile), BF)
     return call(kernel, (out, out), [scalars, hidden, weights, *tokens])
 
 
-def placed(put_ref, near_ref, back_ref, h, b):
-    room = put_ref.shape[2] // 2
-    part = pl.ds(b * room, room)
-    value = jnp.concatenate([near_ref[h, part], back_ref[h, part]], axis=0)
-    return jnp.dot(put_ref[b], value, preferred_element_type=F32).astype(BF)
-
-
-def spread(put, near, back, quarter):
-    rows, width = put.shape[1], near.shape[2]
-    part = jax.ShapeDtypeStruct((2, rows, width), BF)
-    whole = jax.ShapeDtypeStruct((2, 2, rows, width), BF)
-
-    def kernel(put_ref, near_ref, back_ref, *refs):
-        give, keep = refs[:2], refs[2]
+def spread(me, put, near, back, first, apart):
+    rows, room = put.shape[1], put.shape[2] // 2
+    width = near.shape[2]
+    shape = lambda count: jax.ShapeDtypeStruct((count, rows, width), BF)
+
+    def kernel(me_ref, put_ref, near_ref, back_ref, *outs):
+        give, keep = (outs[0], outs[1]) if apart else (outs[0].at[0:2], outs[0].at[2:4])
+        core = me_ref[0] % NC
+        got = {}
         for h in range(2):
-            for b, (k, j) in enumerate(KJ[:4]):
-                got = placed(put_ref, near_ref, back_ref, h, b)
-                stays, index = (h == 1, j) if quarter == 0 else (j == 0, h)
-                if stays:
-                    keep[k, index] = got
-                else:
-                    give[k][index] = got
-
-    return call(kernel, (part, part, whole), [put, near, back])
-
-
-def spread_own(put, near, back):
-    rows, width = put.shape[1], near.shape[2]
-
-    def kernel(put_ref, near_ref, back_ref, out):
-        for h in range(near.shape[0]):
             for j in range(NY):
-                out[h, j] = placed(put_ref, near_ref, back_ref, h, j)
-
-    return call(kernel, jax.ShapeDtypeStruct((near.shape[0], NY, rows, width), BF), [put, near, back])
+                part = pl.ds(j * room, room)
+                value = jnp.concatenate([near_ref[h, part], back_ref[h, part]], axis=0)
+                got[h, j] = jnp.dot(put_ref[first + j], value, preferred_element_type=F32).astype(BF)
+        give[0] = jnp.where(core == 0, got[0, 0], got[1, 1])
+        give[1] = got[0, 1]
+        keep[0] = got[1, 0]
+        keep[1] = jnp.where(core == 0, got[1, 1], got[0, 0])
+
+    return call(kernel, (shape(2), shape(2)) if apart else shape(4), [me.reshape(1), put, near, back])
 
 
 def in_order(values, earlier):
@@ -325,72 +362,67 @@
 
     scalars = jnp.stack([x, me])
 
-    mine, whole = prepare(x, tokens, expert_ids, weight_num)
-    w1 = swap_z(whole, 1, "w1")
-    w0y = swap_y(whole, "w0y")
+    mine, far = prepare(x, tokens, expert_ids, weight_num)
+    f1 = swap_z(far, 1, "f1")
+    f0y = swap_y(far, "f0y")
+    m1 = swap_z(mine, 1, "m1")
+    m0y = swap_y(mine, "m0y")
     m2 = swap_z(mine, 2, "m2")
     touched = touch(*in_order((gate_proj, up_proj), (mine,)))
-    w0y, m2, _ = lax.optimization_barrier((w0y, m2, touched))
+    f0y, m0y, m2, _ = lax.optimization_barrier((f0y, m0y, m2, touched))
+    r2 = swap_xy(m2, False, "r2")
+    q2 = swap_xy(m2, True, "q2")
+    m3 = swap_z(m2, 1, "m3")
+    keep_0, give, put_0, w0y = select(after(me, m2), room, half, [(mine, far), (m0y, f0y)], True, MUCH)
+    got_0 = swap_core(after(give, q2, f1, m1), "rows_0")
     w1y = swap_z(w0y, 1, "w1y")
-    f2 = swap_x(m2, "f2")
-    m2y = swap_y(m2, "m2y")
-    m3 = swap_z(m2, 1, "m3")
-    keep_0, give, put_0 = select(after(me, w1, m2), room, half, [whole, w0y], MUCH)
-    got_0 = swap_core(after(give, f2), "rows_0")
-    m3 = after(m3, m2y, f2)
-    f3 = swap_x(m3, "f3")
-    f2y = swap_x(after(m2y, m3), "f2y")
-    m3y = swap_y(m3, "m3y")
-    f3y = swap_x(m3y, "f3y")
+    q2, r2, m3 = lax.optimization_barrier((q2, r2, m3))
+    t2 = swap_xy(q2, False, "t2")
+    r3 = swap_xy(m3, False, "r3")
+    q3 = swap_xy(m3, True, "q3")
+    t3 = swap_xy(q3, False, "t3")
     hidden_0 = gate_up(after(scalars, m3), keep_0, got_0, gate_proj, up_proj, 0)
-    near_0, away = down(scalars, hidden_0, down_proj, (0, 1))
+    near_0, away = down(scalars, hidden_0, down_proj, 0, 1)
     back_0 = swap_core(away, "back_0")
 
-    keep, give, put = select(after(me, near_0, f3, f2y, m3y), room, half, [m2, m2y, m3, m3y], MUCH)
+    blocks = [(m2,), ((r2, q2),), (m3,), ((r3, q3),)]
+    keep, give, put = select(after(me, near_0, w1y, t2, r3, q3), room, half, blocks, False, MUCH)
     got = swap_core(give, "rows_m")
-    keep_1, give, put_1 = select(after(me, keep), room, half, [w1, w1y])
+    keep_1, give, put_1 = select(after(me, keep), room, half, [(m1, f1), (w1y,)])
     got_1 = swap_core(give, "rows_1")
-    own = spread_own(after(put_0, keep_1), near_0, back_0)
-    first = gate_up(after(scalars, own), keep, got, gate_proj, up_proj, 1)
-    hidden_1 = gate_up(after(scalars, first[0]), keep_1, got_1, gate_proj, up_proj, 0)
-    keep_f, give_f = select_far(after(put, hidden_1), half, [f2, f2y, f3, f3y])
+    first = gate_up(after(scalars, keep_1), keep, got, gate_proj, up_proj, 1)
+    keep_f, give_f = select_far(me, after(put, first[0]), half, [(q2, r2), t2, (q3, r3), t3])
     got_f = swap_core(give_f, "rows_f")
-    near_1, away = down(after(scalars, keep_f), hidden_1, down_proj, (0, 1))
+    hidden_1 = gate_up(after(scalars, keep_f), keep_1, got_1, gate_proj, up_proj, 0)
+    near_1, away = down(scalars, hidden_1, down_proj, 0, 1)
     back_1 = swap_core(away, "back_1")
     hidden = gate_up(after(scalars, near_1), keep_f, got_f, gate_proj, up_proj, 2, [*first, keep, got])
-    near_a, away = down(scalars, hidden, down_proj, (0,), touched)
-    back = swap_core(away, "back_a")
-    n = spread_own(after(put_1, near_a), near_1, back_1)
-    n0, n1 = swap_z(n[:2], 1, "n0"), swap_z(n[2:], 1, "n1")
-    near_b, away = down(after(scalars, n), hidden, down_proj, (1,))
-    a2, a3, keep_a = spread(put, near_a, back, 0)
-    back = swap_core(away, "back_b")
-    b2, b3, keep_b = spread(after(put, keep_a), near_b, back, 1)
-
-    b3, a3 = swap_y(b3, "b3"), swap_x(a3, "a3")
-    a3, b3 = add(keep_a[1], a3), add(keep_b[1], b3)
-    a2, b2, a3, b3 = lax.optimization_barrier((a2, b2, a3, b3))
-    b2, a2 = swap_y(b2, "b2"), swap_x(a2, "a2")
-    p3, q3 = swap_y(a3[1], "p3"), swap_x(b3[0], "q3")
-    s3 = jnp.stack([add(a3[0], p3), add(b3[1], q3)])
-    n0, a2, b2 = in_order((n0, a2, b2), (s3,))
+    near_3, away = down(scalars, hidden, down_proj, 1, 2, touched)
+    back_3 = swap_core(away, "back_3")
+    k1 = spread(me, after(put_1, near_3), near_1, back_1, 0, False)
+    near_2, away = down(after(scalars, k1), hidden, down_proj, 0, 2)
+    back_2 = swap_core(away, "back_2")
+    give_3, keep_3 = spread(me, after(put, near_2), near_3, back_3, 2, True)
+    give_2, keep_2 = spread(me, after(put, keep_3), near_2, back_2, 0, True)
+    own = spread(me, after(put_0, keep_2), near_0, back_0, 0, False)
+
+    n = swap_z(k1, 1, "n")
+    u3 = swap_xy(give_3, True, "u3")
+    u3 = add(keep_3, after(u3, keep_2))
+    u2 = swap_xy(after(give_2, u3), True, "u2")
+    v3 = swap_xy(u3[1], False, "v3")
+    s3 = add(u3[0], v3)
+    n = add(own, after(n, s3))
+    u2 = after(u2, s3)
     s3 = swap_z(s3, 1, "s3")
-    n0 = add(own[:2], n0)
-    a2, b2 = in_order((a2, b2), (n0,))
-    n, n0 = swap_x(n0[0], "n"), n0[1]
-    a2, b2 = add(keep_a[0], a2), add(keep_b[0], b2)
-    p2, q2 = swap_y(a2[1], "p2"), swap_x(b2[0], "q2")
-    n1 = add(own[2:], after(n1, a2, b2))
-    o, n1 = swap_y(n1[:, 1], "o"), n1[:, 0]
-    s3, p2, q2 = in_order((s3, p2, q2), (n1,))
-    s2 = jnp.stack([add(a2[0], p2, s3[0]), add(b2[1], q2, s3[1])])
-    n, o = in_order((n, o), (s2,))
+    u2 = add(keep_2, u2)
+    v2 = swap_xy(u2[1], False, "v2")
+    s2 = add(u2[0], v2, s3)
+    u0 = swap_xy(n[:2], True, "u0")
     s2 = swap_z(s2, 2, "s2")
-    n, o = add(n0, n), add(n1, o)
-    np, nq = swap_y(n[1], "np"), swap_x(o[0], "nq")
-    n = jnp.stack([add(n[0], np), add(o[1], nq)])
-    total = add(n, s2)
-    return jnp.concatenate([total[0], total[1]], axis=1)
+    u0 = add(n[2:], u0)
+    v0 = swap_xy(u0[1], False, "v0")
+    return add(u0[0], v0, s2)
 
 
 def solution(mesh):

time: 110 us -> 107 us (0.973)
  starting transfers between devices: 38.2 us -> 29.4 us
  waiting for transfers between devices: 34.7 us -> 39.5 us
    ppermute x25 -> x18, starting transfers between devices: 27 us -> 15.6 us  [swap_expert(): return lax.ppermute(value, 'expert', pairs)]
    ppermute x10 -> x12, waiting for transfers between devices: 11.9 us -> 17.4 us  [swap_xy(): return lax.ppermute(value, ('dp', 'expert'), pairs)]
    ppermute x10 -> x12, starting transfers between devices: 11.2 us -> 13.8 us  [swap_xy(): return lax.ppermute(value, ('dp', 'expert'), pairs)]
    unnamed x15 -> x16, local copies, waits for them, and re-layouts: 7.47 us -> 8.29 us
    ppermute x25 -> x18, waiting for transfers between devices: 22.7 us -> 22.1 us  [swap_expert(): return lax.ppermute(value, 'expert', pairs)]
  transfers between devices with their start and end apart: 35 -> 30, of which waited for: 17 -> 11; matrix products, arithmetic and copies ran while one was open for 1% -> 1% of each run, Pallas kernels for 23% -> 22%
where the time goes in v4:
time: 107 us
  waiting for transfers between devices  39.5 us (37%)
  starting transfers between devices  29.4 us (27%)
  Pallas kernels  27.6 us (26%)
  local copies, waits for them, and re-layouts  8.37 us (8%)
  other arithmetic  1.54 us (1%)
    pallas_call x17, Pallas kernels, call(): pl.pallas_call(kernel, out_shape=out, in_specs=spec, out_specs=jax.tree.m...  25.7 us
    ppermute x18, waiting for transfers between devices, swap_expert(): return lax.ppermute(value, 'expert', pairs)  22.1 us
    ppermute x12, waiting for transfers between devices, swap_xy(): return lax.ppermute(value, ('dp', 'expert'), pairs)  17.4 us
    ppermute x18, starting transfers between devices, swap_expert(): return lax.ppermute(value, 'expert', pairs)  15.6 us
    ppermute x12, starting transfers between devices, swap_xy(): return lax.ppermute(value, ('dp', 'expert'), pairs)  13.8 us
    unnamed x16, local copies, waits for them, and re-layouts  8.29 us
  transfers between devices with their start and end apart: 30, of which 11 were waited for; matrix products, arithmetic and copies ran while one was open for 1% of the time, Pallas kernels for 22%

profile of v4, /device:TPU:0, one launch (start us, length us, event | category | flops | bytes accessed | tf_op | source)
XLA Modules:
  0.0 106.6 jit_solution(3937023187360454517)
XLA Ops:
  0.0 1.9 %shard_map.64 = (bf16[64,1920]{1,0:T(8,128)(2,1)}, bf16[64,1792]{1,0:T(8,128)(2,1)}) custom-call(s32[1]{0:T(128)} %bitcast.1.x_ref, bf16[64,3584]{1,0:T(8,128)(2,1)} %tokens_ref.1, s32[8,64]{1,0:T(8,128)} %bitcast.30, s32[8,64]{1,0:T(8,128)} %bitcast.31), custom_call_target="tpu_custom_call" | custom-call | flops 1 | bytes 1 | tf_op jit(solution)/shard_map/pallas_call | solution.py:135
  1.9 4.0 %collective-permute-start.2 = (bf16[64,1920]{1,0:T(8,128)(2,1)}, bf16[64,1920]{1,0:T(8,128)(2,1)}, u32[]{:S(2)}, u32[]{:S(2)}) collective-permute-start(bf16[64,1920]{1,0:T(8,128)(2,1)} %get-tuple-element.60.refs_0_), channel_id=1, source_target_pairs={{0,8},{1,9},{2,10},{3,11},{4,12},{5,13},{6,14},{7,15},{8,0},{9,1},... | collective-permute-start | bytes 737288 | tf_op jit(solution)/shard_map/m2/ppermute | solution.py:64
  5.9 1.5 %collective-permute-start.1 = (bf16[64,1920]{1,0:T(8,128)(2,1)}, bf16[64,1920]{1,0:T(8,128)(2,1)}, u32[]{:S(2)}, u32[]{:S(2)}) collective-permute-start(bf16[64,1920]{1,0:T(8,128)(2,1)} %get-tuple-element.60.refs_0_), channel_id=1, source_target_pairs={{0,2},{1,3},{2,0},{3,1},{4,6},{5,7},{6,4},{7,5},{8,10},{9,11},{10,... | collective-permute-start | bytes 737288 | tf_op jit(solution)/shard_map/m0y/ppermute | solution.py:64
  8.0 1.6 %collective-permute-start.6 = (bf16[64,1792]{1,0:T(8,128)(2,1)}, bf16[64,1792]{1,0:T(8,128)(2,1)}, u32[]{:S(2)}, u32[]{:S(2)}) collective-permute-start(bf16[64,1792]{1,0:T(8,128)(2,1)} %get-tuple-element.59.refs_1_), channel_id=1, source_target_pairs={{0,4},{1,5},{2,6},{3,7},{4,0},{5,1},{6,2},{7,3},{8,12},{9,13},{10,... | collective-permute-start | bytes 688136 | tf_op jit(solution)/shard_map/f1/ppermute | solution.py:64
  10.0 3.1 %copy-done = bf16[1,3584,1024]{2,1,0:T(8,128)(2,1)S(1)} copy-done((bf16[1,3584,1024]{2,1,0:T(8,128)(2,1)S(1)}, bf16[1,3584,1024]{2,1,0:T(8,128)(2,1)}, u32[]{:S(2)}) %copy-start) | copy-done | bytes 7340056
  13.1 3.1 %copy-done.1 = bf16[1,3584,1024]{2,1,0:T(8,128)(2,1)S(1)} copy-done((bf16[1,3584,1024]{2,1,0:T(8,128)(2,1)S(1)}, bf16[1,3584,1024]{2,1,0:T(8,128)(2,1)}, u32[]{:S(2)}) %copy-start.1) | copy-done | bytes 7340056
  16.2 2.4 %collective-permute-done.refs_3_ = bf16[64,1792]{1,0:T(8,128)(2,1)} collective-permute-done((bf16[64,1792]{1,0:T(8,128)(2,1)}, bf16[64,1792]{1,0:T(8,128)(2,1)}, u32[]{:S(2)}, u32[]{:S(2)}) %collective-permute-start) | collective-permute-done | bytes 229408 | tf_op jit(solution)/shard_map/f0y/ppermute | solution.py:64
  18.6 1.6 %collective-permute-start.5 = (bf16[64,1920]{1,0:T(8,128)(2,1)}, bf16[64,1920]{1,0:T(8,128)(2,1)S(1)}, u32[]{:S(2)}, u32[]{:S(2)}) collective-permute-start(bf16[64,1920]{1,0:T(8,128)(2,1)} %collective-permute-done.2.refs_0_), channel_id=1, source_target_pairs={{0,4},{1,5},{2,6},{3,7},{4,0},{5,1},{6,2},{7,3},{8,12},{9,13},{10,... | collective-permute-start | bytes 737288 | tf_op jit(solution)/shard_map/m3/ppermute | solution.py:64
  20.2 1.5 %collective-permute-start.4 = (bf16[64,1920]{1,0:T(8,128)(2,1)}, bf16[64,1920]{1,0:T(8,128)(2,1)S(1)}, u32[]{:S(2)}, u32[]{:S(2)}) collective-permute-start(bf16[64,1920]{1,0:T(8,128)(2,1)} %collective-permute-done.2.refs_0_), channel_id=1, source_target_pairs={{0,2},{1,17},{2,0},{3,19},{4,6},{5,21},{6,4},{7,23},{8,10},{9,25},... | collective-permute-start | bytes 737288 | tf_op jit(solution)/shard_map/r2/ppermute | solution.py:92
  21.7 1.5 %collective-permute-start.3 = (bf16[64,1920]{1,0:T(8,128)(2,1)}, bf16[64,1920]{1,0:T(8,128)(2,1)S(1)}, u32[]{:S(2)}, u32[]{:S(2)}) collective-permute-start(bf16[64,1920]{1,0:T(8,128)(2,1)} %collective-permute-done.2.refs_0_), channel_id=1, source_target_pairs={{0,16},{1,3},{2,18},{3,1},{4,20},{5,7},{6,22},{7,5},{8,24},{9,11},... | collective-permute-start | bytes 737288 | tf_op jit(solution)/shard_map/q2/ppermute | solution.py:92
  25.1 2.0 %shard_map.66 = (bf16[64,3712]{1,0:T(8,128)(2,1)S(1)}, bf16[64,3712]{1,0:T(8,128)(2,1)S(1)}, bf16[2,64,64]{2,1,0:T(8,128)(2,1)S(1)}, bf16[64,3712]{1,0:T(8,128)(2,1)S(1)}) custom-call(s32[1]{0:T(128)} %bitcast.4.me_ref, bf16[64,1920]{1,0:T(8,128)(2,1)S(1)} %copy-done.4, bf16[64,1792]{1,0:T(8,128)(2,1)S(1)} %copy-done.5, ...), custom_call_target="tpu_custom_call" | custom-call | flops 34359738368 | bytes 1 | tf_op jit(solution)/shard_map/pallas_call | solution.py:103
  29.3 1.6 %collective-permute-start.10 = (bf16[64,1920]{1,0:T(8,128)(2,1)S(1)}, bf16[64,1920]{1,0:T(8,128)(2,1)S(1)}, u32[]{:S(2)}, u32[]{:S(2)}) collective-permute-start(bf16[64,1920]{1,0:T(8,128)(2,1)S(1)} %collective-permute-done.3.refs_2_.refs_0_), channel_id=1, source_target_pairs={{0,2},{1,17},{2,0},{3,19},{4,6},{5,21},{6,4},{7,23},{8,10},{9,25},... | collective-permute-start | bytes 737288 | tf_op jit(solution)/shard_map/t2/ppermute | solution.py:92
  33.0 2.8 %shard_map.67.hidden_ref = bf16[128,1024]{1,0:T(8,128)(2,1)S(1)} custom-call(s32[2]{0:T(128)S(1)} %pad_add_fusion.scalar_ref, bf16[64,3712]{1,0:T(8,128)(2,1)S(1)} %get-tuple-element.70.keep_ref, bf16[64,3712]{1,0:T(8,128)(2,1)S(1)} %collective-permute-done.8.got_ref, bf16[1,3584,1024]{2,1,0:T(8,128)(2,1)S(1)} %bitcast.29, bf16[1,3584,1024]{2,1,0:T(8,128)(2,1)S(1)} %copy-done.2), custom_call_target="tpu_custom_call" | custom-call | flops 1 | bytes 1 | tf_op jit(solution)/shard_map/pallas_call | solution.py:103
  36.1 1.7 %shard_map.68 = (bf16[2,64,1792]{2,1,0:T(8,128)(2,1)S(1)}, bf16[2,64,1792]{2,1,0:T(8,128)(2,1)S(1)}) custom-call(s32[2]{0:T(128)S(1)} %pad_add_fusion.scalar_ref, bf16[128,1024]{1,0:T(8,128)(2,1)S(1)} %shard_map.67.hidden_ref, bf16[1,1024,3584]{2,1,0:T(8,128)(2,1)S(1)} %copy-done.3), custom_call_target="tpu_custom_call" | custom-call | flops 1 | bytes 1 | tf_op jit(solution)/shard_map/pallas_call | solution.py:103
  37.8 3.6 %collective-permute-done.9.refs_2_ = bf16[64,3712]{1,0:T(8,128)(2,1)S(1)} collective-permute-done((bf16[64,3712]{1,0:T(8,128)(2,1)S(1)}, bf16[64,3712]{1,0:T(8,128)(2,1)S(1)}, u32[]{:S(2)}, u32[]{:S(2)}) %collective-permute-start.9) | collective-permute-done | bytes 475168 | tf_op jit(solution)/shard_map/w1y/ppermute | solution.py:64
  41.4 1.9 %shard_map.69 = (bf16[128,1920]{1,0:T(8,128)(2,1)S(1)}, bf16[128,1920]{1,0:T(8,128)(2,1)S(1)}, bf16[4,64,64]{2,1,0:T(8,128)(2,1)S(1)}) custom-call(s32[1]{0:T(128)} %bitcast.5.me_ref, bf16[64,1920]{1,0:T(8,128)(2,1)} %collective-permute-done.2.refs_0_, bf16[64,1920]{1,0:T(8,128)(2,1)S(1)} %collective-permute-done.4.refs_1_, ...), custom_call_target="tpu_custom_call" | custom-call | flops 34359738368 | bytes 1 | tf_op jit(solution)/shard_map/pallas_call | solution.py:103
  44.0 1.7 %shard_map.70 = (bf16[64,3712]{1,0:T(8,128)(2,1)S(1)}, bf16[64,3712]{1,0:T(8,128)(2,1)S(1)}, bf16[2,64,64]{2,1,0:T(8,128)(2,1)S(1)}) custom-call(s32[1]{0:T(128)} %bitcast.6.me_ref, bf16[64,1920]{1,0:T(8,128)(2,1)S(1)} %collective-permute-done.7.refs_0_, bf16[64,1792]{1,0:T(8,128)(2,1)} %collective-permute-done.6.refs_1_, ...), custom_call_target="tpu_custom_call" | custom-call | flops 1 | bytes 1 | tf_op jit(solution)/shard_map/pallas_call | solution.py:103
  46.9 2.6 %shard_map.71 = (f32[256,1024]{1,0:T(8,128)S(1)}, f32[256,1024]{1,0:T(8,128)S(1)}) custom-call(s32[2]{0:T(128)S(1)} %pad_add_fusion.scalar_ref, bf16[128,1920]{1,0:T(8,128)(2,1)S(1)} %get-tuple-element.79.keep_ref.refs_2_, bf16[128,1920]{1,0:T(8,128)(2,1)S(1)} %collective-permute-done.13.got_ref.refs_3_, bf16[1,3584,1024]{2,1,0:T(8,128)(2,1)S(1)} %bitcast.29, ...), custom_call_target="tpu_custom_call" | custom-call | flops 1 | bytes 1 | tf_op jit(solution)/shard_map/pallas_call | solution.py:103
  50.2 2.8 %shard_map.73.hidden_ref = bf16[128,1024]{1,0:T(8,128)(2,1)S(1)} custom-call(s32[2]{0:T(128)S(1)} %pad_add_fusion.scalar_ref, bf16[64,3712]{1,0:T(8,128)(2,1)S(1)} %get-tuple-element.82.keep_ref, bf16[64,3712]{1,0:T(8,128)(2,1)S(1)} %collective-permute-done.15.got_ref, bf16[1,3584,1024]{2,1,0:T(8,128)(2,1)S(1)} %bitcast.29, bf16[1,3584,1024]{2,1,0:T(8,128)(2,1)S(1)} %copy-done.2), custom_call_target="tpu_custom_call" | custom-call | flops 1 | bytes 1 | tf_op jit(solution)/shard_map/pallas_call | solution.py:103
  53.0 1.7 %shard_map.74 = (bf16[2,64,1792]{2,1,0:T(8,128)(2,1)S(1)}, bf16[2,64,1792]{2,1,0:T(8,128)(2,1)S(1)}) custom-call(s32[2]{0:T(128)S(1)} %pad_add_fusion.scalar_ref, bf16[128,1024]{1,0:T(8,128)(2,1)S(1)} %shard_map.73.hidden_ref, bf16[1,1024,3584]{2,1,0:T(8,128)(2,1)S(1)} %copy-done.3), custom_call_target="tpu_custom_call" | custom-call | flops 1 | bytes 1 | tf_op jit(solution)/shard_map/pallas_call | solution.py:103
  55.3 3.0 %shard_map.75.hidden_ref = bf16[256,1024]{1,0:T(8,128)(2,1)S(1)} custom-call(s32[2]{0:T(128)S(1)} %pad_add_fusion.scalar_ref, bf16[128,1792]{1,0:T(8,128)(2,1)S(1)} %get-tuple-element.87.keep_ref, bf16[128,1792]{1,0:T(8,128)(2,1)S(1)} %collective-permute-done.16.got_ref, bf16[1,3584,1024]{2,1,0:T(8,128)(2,1)S(1)} %bitcast.29, ...), custom_call_target="tpu_custom_call" | custom-call | flops 1 | bytes 1 | tf_op jit(solution)/shard_map/pallas_call | solution.py:103
  58.3 1.7 %shard_map.76 = (bf16[2,64,1792]{2,1,0:T(8,128)(2,1)S(1)}, bf16[2,64,1792]{2,1,0:T(8,128)(2,1)S(1)}) custom-call(s32[2]{0:T(128)S(1)} %pad_add_fusion.scalar_ref, bf16[256,1024]{1,0:T(8,128)(2,1)S(1)} %shard_map.75.hidden_ref, bf16[1,1024,3584]{2,1,0:T(8,128)(2,1)S(1)} %copy-done.3, f32[16,128]{1,0:T(8,128)S(1)} %shard_map.65.refs_0_), custom_call_target="tpu_custom_call" | custom-call | flops 1 | bytes 1 | tf_op jit(solution)/shard_map/pallas_call | solution.py:103
  60.4 1.7 %shard_map.78 = (bf16[2,64,1792]{2,1,0:T(8,128)(2,1)S(1)}, bf16[2,64,1792]{2,1,0:T(8,128)(2,1)S(1)}) custom-call(s32[2]{0:T(128)S(1)} %pad_add_fusion.scalar_ref, bf16[256,1024]{1,0:T(8,128)(2,1)S(1)} %shard_map.75.hidden_ref, bf16[1,1024,3584]{2,1,0:T(8,128)(2,1)S(1)} %copy-done.3), custom_call_target="tpu_custom_call" | custom-call | flops 1 | bytes 1 | tf_op jit(solution)/shard_map/pallas_call | solution.py:103
  63.1 1.5 %collective-permute-start.22 = (bf16[2,64,1792]{2,1,0:T(8,128)(2,1)S(1)}, bf16[2,64,1792]{2,1,0:T(8,128)(2,1)S(1)}, u32[]{:S(2)}, u32[]{:S(2)}) collective-permute-start(bf16[2,64,1792]{2,1,0:T(8,128)(2,1)S(1)} %get-tuple-element.107), channel_id=1, source_target_pairs={{0,16},{1,3},{2,18},{3,1},{4,20},{5,7},{6,22},{7,5},{8,24},{9,11},... | collective-permute-start | bytes 1376264 | tf_op jit(solution)/shard_map/u3/ppermute | solution.py:92
  65.5 6.2 %collective-permute-done.22 = bf16[2,64,1792]{2,1,0:T(8,128)(2,1)S(1)} collective-permute-done((bf16[2,64,1792]{2,1,0:T(8,128)(2,1)S(1)}, bf16[2,64,1792]{2,1,0:T(8,128)(2,1)S(1)}, u32[]{:S(2)}, u32[]{:S(2)}) %collective-permute-start.22) | collective-permute-done | bytes 458784 | tf_op jit(solution)/shard_map/u3/ppermute | solution.py:92
  72.7 1.5 %collective-permute-start.26 = (bf16[2,64,1792]{2,1,0:T(8,128)(2,1)S(1)}, bf16[2,64,1792]{2,1,0:T(8,128)(2,1)S(1)}, u32[]{:S(2)}, u32[]{:S(2)}) collective-permute-start(bf16[2,64,1792]{2,1,0:T(8,128)(2,1)S(1)} %get-tuple-element.111), channel_id=1, source_target_pairs={{0,16},{1,3},{2,18},{3,1},{4,20},{5,7},{6,22},{7,5},{8,24},{9,11},... | collective-permute-start | bytes 1376264 | tf_op jit(solution)/shard_map/u2/ppermute | solution.py:92
  74.2 6.0 %collective-permute-done.23 = bf16[64,1792]{1,0:T(8,128)(2,1)S(1)} collective-permute-done((bf16[64,1792]{1,0:T(8,128)(2,1)S(1)}, bf16[64,1792]{1,0:T(8,128)(2,1)S(1)}, u32[]{:S(2)}, u32[]{:S(2)}) %collective-permute-start.23) | collective-permute-done | bytes 229408 | tf_op jit(solution)/shard_map/v3/ppermute | solution.py:92
  80.9 6.9 %collective-permute-done.21 = bf16[4,64,1792]{2,1,0:T(8,128)(2,1)S(1)} collective-permute-done((bf16[4,64,1792]{2,1,0:T(8,128)(2,1)S(1)}, bf16[4,64,1792]{2,1,0:T(8,128)(2,1)S(1)}, u32[]{:S(2)}, u32[]{:S(2)}) %collective-permute-start.21) | collective-permute-done | bytes 917536 | tf_op jit(solution)/shard_map/n/ppermute | solution.py:64
  90.1 2.2 %collective-permute-done.28 = bf16[64,1792]{1,0:T(8,128)(2,1)S(1)} collective-permute-done((bf16[64,1792]{1,0:T(8,128)(2,1)S(1)}, bf16[64,1792]{1,0:T(8,128)(2,1)S(1)}, u32[]{:S(2)}, u32[]{:S(2)}) %collective-permute-start.28) | collective-permute-done | bytes 229408 | tf_op jit(solution)/shard_map/s3/ppermute | solution.py:64
  92.3 4.1 %collective-permute-done.27 = bf16[64,1792]{1,0:T(8,128)(2,1)S(1)} collective-permute-done((bf16[64,1792]{1,0:T(8,128)(2,1)S(1)}, bf16[64,1792]{1,0:T(8,128)(2,1)S(1)}, u32[]{:S(2)}, u32[]{:S(2)}) %collective-permute-start.27) | collective-permute-done | bytes 229408 | tf_op jit(solution)/shard_map/v2/ppermute | solution.py:92
  96.5 2.0 %collective-permute-start.29 = (bf16[64,1792]{1,0:T(8,128)(2,1)S(1)}, bf16[64,1792]{1,0:T(8,128)(2,1)S(1)}, u32[]{:S(2)}, u32[]{:S(2)}) collective-permute-start(bf16[64,1792]{1,0:T(8,128)(2,1)S(1)} %fusion.1), channel_id=1, source_target_pairs={{0,8},{1,9},{2,10},{3,11},{4,12},{5,13},{6,14},{7,15},{8,0},{9,1},... | collective-permute-start | bytes 688136 | tf_op jit(solution)/shard_map/s2/ppermute | solution.py:64
  99.7 6.2 %collective-permute-done.29 = bf16[64,1792]{1,0:T(8,128)(2,1)S(1)} collective-permute-done((bf16[64,1792]{1,0:T(8,128)(2,1)S(1)}, bf16[64,1792]{1,0:T(8,128)(2,1)S(1)}, u32[]{:S(2)}, u32[]{:S(2)}) %collective-permute-start.29) | collective-permute-done | bytes 229408 | tf_op jit(solution)/shard_map/s2/ppermute | solution.py:64
  (75 shorter events, 18.7 us)
Async XLA Ops:
  1.9 16.7 %collective-permute-start.2 = (bf16[64,1920]{1,0:T(8,128)(2,1)}, bf16[64,1920]{1,0:T(8,128)(2,1)}, u32[]{:S(2)}, u32[]{:S(2)}) collective-permute-start(bf16[64,1920]{1,0:T(8,128)(2,1)} %get-tuple-element.60.refs_0_), channel_id=1, source_target_pairs={{0,8},{1,9},{2,10},{3,11},{4,12},{5,13},{6,14},{7,15},{8,0},{9,1},... | collective-permute-start | bytes 737288 | tf_op jit(solution)/shard_map/m2/ppermute | solution.py:64
  5.9 12.7 %collective-permute-start.1 = (bf16[64,1920]{1,0:T(8,128)(2,1)}, bf16[64,1920]{1,0:T(8,128)(2,1)}, u32[]{:S(2)}, u32[]{:S(2)}) collective-permute-start(bf16[64,1920]{1,0:T(8,128)(2,1)} %get-tuple-element.60.refs_0_), channel_id=1, source_target_pairs={{0,2},{1,3},{2,0},{3,1},{4,6},{5,7},{6,4},{7,5},{8,10},{9,11},{10,... | collective-permute-start | bytes 737288 | tf_op jit(solution)/shard_map/m0y/ppermute | solution.py:64
  7.4 11.1 %collective-permute-start = (bf16[64,1792]{1,0:T(8,128)(2,1)}, bf16[64,1792]{1,0:T(8,128)(2,1)}, u32[]{:S(2)}, u32[]{:S(2)}) collective-permute-start(bf16[64,1792]{1,0:T(8,128)(2,1)} %get-tuple-element.59.refs_1_), channel_id=1, source_target_pairs={{0,2},{1,3},{2,0},{3,1},{4,6},{5,7},{6,4},{7,5},{8,10},{9,11},{10,... | collective-permute-start | bytes 688136 | tf_op jit(solution)/shard_map/f0y/ppermute | solution.py:64
  8.0 19.1 %collective-permute-start.6 = (bf16[64,1792]{1,0:T(8,128)(2,1)}, bf16[64,1792]{1,0:T(8,128)(2,1)}, u32[]{:S(2)}, u32[]{:S(2)}) collective-permute-start(bf16[64,1792]{1,0:T(8,128)(2,1)} %get-tuple-element.59.refs_1_), channel_id=1, source_target_pairs={{0,4},{1,5},{2,6},{3,7},{4,0},{5,1},{6,2},{7,3},{8,12},{9,13},{10,... | collective-permute-start | bytes 688136 | tf_op jit(solution)/shard_map/f1/ppermute | solution.py:64
  9.5 17.6 %collective-permute-start.7 = (bf16[64,1920]{1,0:T(8,128)(2,1)}, bf16[64,1920]{1,0:T(8,128)(2,1)S(1)}, u32[]{:S(2)}, u32[]{:S(2)}) collective-permute-start(bf16[64,1920]{1,0:T(8,128)(2,1)} %get-tuple-element.60.refs_0_), channel_id=1, source_target_pairs={{0,4},{1,5},{2,6},{3,7},{4,0},{5,1},{6,2},{7,3},{8,12},{9,13},{10,... | collective-permute-start | bytes 737288 | tf_op jit(solution)/shard_map/m1/ppermute | solution.py:64
  16.1 16.8 %slice-start = ((s8[7340032]{0:T(1024)(128)(4,1)}), s8[3145728]{0:T(1024)(128)(4,1)S(1)}, s32[]{:S(2)}) async-start(s8[7340032]{0:T(1024)(128)(4,1)} %bitcast.28), calls=%async_computation | async-start | bytes 6291456
  18.6 10.7 %collective-permute-start.5 = (bf16[64,1920]{1,0:T(8,128)(2,1)}, bf16[64,1920]{1,0:T(8,128)(2,1)S(1)}, u32[]{:S(2)}, u32[]{:S(2)}) collective-permute-start(bf16[64,1920]{1,0:T(8,128)(2,1)} %collective-permute-done.2.refs_0_), channel_id=1, source_target_pairs={{0,4},{1,5},{2,6},{3,7},{4,0},{5,1},{6,2},{7,3},{8,12},{9,13},{10,... | collective-permute-start | bytes 737288 | tf_op jit(solution)/shard_map/m3/ppermute | solution.py:64
  20.2 9.1 %collective-permute-start.4 = (bf16[64,1920]{1,0:T(8,128)(2,1)}, bf16[64,1920]{1,0:T(8,128)(2,1)S(1)}, u32[]{:S(2)}, u32[]{:S(2)}) collective-permute-start(bf16[64,1920]{1,0:T(8,128)(2,1)} %collective-permute-done.2.refs_0_), channel_id=1, source_target_pairs={{0,2},{1,17},{2,0},{3,19},{4,6},{5,21},{6,4},{7,23},{8,10},{9,25},... | collective-permute-start | bytes 737288 | tf_op jit(solution)/shard_map/r2/ppermute | solution.py:92
  21.7 6.4 %collective-permute-start.3 = (bf16[64,1920]{1,0:T(8,128)(2,1)}, bf16[64,1920]{1,0:T(8,128)(2,1)S(1)}, u32[]{:S(2)}, u32[]{:S(2)}) collective-permute-start(bf16[64,1920]{1,0:T(8,128)(2,1)} %collective-permute-done.2.refs_0_), channel_id=1, source_target_pairs={{0,16},{1,3},{2,18},{3,1},{4,20},{5,7},{6,22},{7,5},{8,24},{9,11},... | collective-permute-start | bytes 737288 | tf_op jit(solution)/shard_map/q2/ppermute | solution.py:92
  25.1 7.9 %copy-start.2 = (bf16[1,3584,1024]{2,1,0:T(8,128)(2,1)S(1)}, bf16[1,3584,1024]{2,1,0:T(8,128)(2,1)}, u32[]{:S(2)}) copy-start(bf16[1,3584,1024]{2,1,0:T(8,128)(2,1)} %up_ref.7) | copy-start | bytes 22020100
  28.1 4.9 %collective-permute-start.8 = (bf16[64,3712]{1,0:T(8,128)(2,1)S(1)}, bf16[64,3712]{1,0:T(8,128)(2,1)S(1)}, u32[]{:S(2)}, u32[]{:S(2)}) collective-permute-start(bf16[64,3712]{1,0:T(8,128)(2,1)S(1)} %get-tuple-element.72), channel_id=1, source_target_pairs={{0,1},{1,0},{2,3},{3,2},{4,5},{5,4},{6,7},{7,6},{8,9},{9,8},{10,11... | collective-permute-start | bytes 1425416 | tf_op jit(solution)/shard_map/rows_0/ppermute | solution.py:64
  28.1 13.3 %collective-permute-start.9 = (bf16[64,3712]{1,0:T(8,128)(2,1)S(1)}, bf16[64,3712]{1,0:T(8,128)(2,1)S(1)}, u32[]{:S(2)}, u32[]{:S(2)}) collective-permute-start(bf16[64,3712]{1,0:T(8,128)(2,1)S(1)} %get-tuple-element.74), channel_id=1, source_target_pairs={{0,4},{1,5},{2,6},{3,7},{4,0},{5,1},{6,2},{7,3},{8,12},{9,13},{10,... | collective-permute-start | bytes 1425416 | tf_op jit(solution)/shard_map/w1y/ppermute | solution.py:64
  29.3 12.1 %collective-permute-start.10 = (bf16[64,1920]{1,0:T(8,128)(2,1)S(1)}, bf16[64,1920]{1,0:T(8,128)(2,1)S(1)}, u32[]{:S(2)}, u32[]{:S(2)}) collective-permute-start(bf16[64,1920]{1,0:T(8,128)(2,1)S(1)} %collective-permute-done.3.refs_2_.refs_0_), channel_id=1, source_target_pairs={{0,2},{1,17},{2,0},{3,19},{4,6},{5,21},{6,4},{7,23},{8,10},{9,25},... | collective-permute-start | bytes 737288 | tf_op jit(solution)/shard_map/t2/ppermute | solution.py:92
  30.9 10.5 %collective-permute-start.12 = (bf16[64,1920]{1,0:T(8,128)(2,1)S(1)}, bf16[64,1920]{1,0:T(8,128)(2,1)S(1)}, u32[]{:S(2)}, u32[]{:S(2)}) collective-permute-start(bf16[64,1920]{1,0:T(8,128)(2,1)S(1)} %collective-permute-done.5.refs_3_), channel_id=1, source_target_pairs={{0,16},{1,3},{2,18},{3,1},{4,20},{5,7},{6,22},{7,5},{8,24},{9,11},... | collective-permute-start | bytes 737288 | tf_op jit(solution)/shard_map/q3/ppermute | solution.py:92
  32.4 9.0 %collective-permute-start.11 = (bf16[64,1920]{1,0:T(8,128)(2,1)S(1)}, bf16[64,1920]{1,0:T(8,128)(2,1)S(1)}, u32[]{:S(2)}, u32[]{:S(2)}) collective-permute-start(bf16[64,1920]{1,0:T(8,128)(2,1)S(1)} %collective-permute-done.5.refs_3_), channel_id=1, source_target_pairs={{0,2},{1,17},{2,0},{3,19},{4,6},{5,21},{6,4},{7,23},{8,10},{9,25},... | collective-permute-start | bytes 737288 | tf_op jit(solution)/shard_map/r3/ppermute | solution.py:92
  43.3 3.6 %collective-permute-start.13 = (bf16[128,1920]{1,0:T(8,128)(2,1)S(1)}, bf16[128,1920]{1,0:T(8,128)(2,1)S(1)}, u32[]{:S(2)}, u32[]{:S(2)}) collective-permute-start(bf16[128,1920]{1,0:T(8,128)(2,1)S(1)} %get-tuple-element.84), channel_id=1, source_target_pairs={{0,1},{1,0},{2,3},{3,2},{4,5},{5,4},{6,7},{7,6},{8,9},{9,8},{10,11... | collective-permute-start | bytes 1474568 | tf_op jit(solution)/shard_map/rows_m/ppermute | solution.py:64
  43.4 6.3 %collective-permute-start.14 = (bf16[64,1920]{1,0:T(8,128)(2,1)S(1)}, bf16[64,1920]{1,0:T(8,128)(2,1)S(1)}, u32[]{:S(2)}, u32[]{:S(2)}) collective-permute-start(bf16[64,1920]{1,0:T(8,128)(2,1)S(1)} %collective-permute-done.12.refs_5_.refs_3_), channel_id=1, source_target_pairs={{0,2},{1,17},{2,0},{3,19},{4,6},{5,21},{6,4},{7,23},{8,10},{9,25},... | collective-permute-start | bytes 737288 | tf_op jit(solution)/shard_map/t3/ppermute | solution.py:92
  45.7 4.5 %collective-permute-start.15 = (bf16[64,3712]{1,0:T(8,128)(2,1)S(1)}, bf16[64,3712]{1,0:T(8,128)(2,1)S(1)}, u32[]{:S(2)}, u32[]{:S(2)}) collective-permute-start(bf16[64,3712]{1,0:T(8,128)(2,1)S(1)} %get-tuple-element.89), channel_id=1, source_target_pairs={{0,1},{1,0},{2,3},{3,2},{4,5},{5,4},{6,7},{7,6},{8,9},{9,8},{10,11... | collective-permute-start | bytes 1425416 | tf_op jit(solution)/shard_map/rows_1/ppermute | solution.py:64
  50.1 5.2 %collective-permute-start.16 = (bf16[128,1792]{1,0:T(8,128)(2,1)S(1)}, bf16[128,1792]{1,0:T(8,128)(2,1)S(1)}, u32[]{:S(2)}, u32[]{:S(2)}) collective-permute-start(bf16[128,1792]{1,0:T(8,128)(2,1)S(1)} %get-tuple-element.92), channel_id=1, source_target_pairs={{0,1},{1,0},{2,3},{3,2},{4,5},{5,4},{6,7},{7,6},{8,9},{9,8},{10,11... | collective-permute-start | bytes 1376264 | tf_op jit(solution)/shard_map/rows_f/ppermute | solution.py:64
  54.7 5.3 %collective-permute-start.17 = (bf16[2,64,1792]{2,1,0:T(8,128)(2,1)S(1)}, bf16[2,64,1792]{2,1,0:T(8,128)(2,1)S(1)}, u32[]{:S(2)}, u32[]{:S(2)}) collective-permute-start(bf16[2,64,1792]{2,1,0:T(8,128)(2,1)S(1)} %get-tuple-element.96), channel_id=1, source_target_pairs={{0,1},{1,0},{2,3},{3,2},{4,5},{5,4},{6,7},{7,6},{8,9},{9,8},{10,11... | collective-permute-start | bytes 1376264 | tf_op jit(solution)/shard_map/back_1/ppermute | solution.py:64
  60.0 2.7 %collective-permute-start.18 = (bf16[2,64,1792]{2,1,0:T(8,128)(2,1)S(1)}, bf16[2,64,1792]{2,1,0:T(8,128)(2,1)S(1)}, u32[]{:S(2)}, u32[]{:S(2)}) collective-permute-start(bf16[2,64,1792]{2,1,0:T(8,128)(2,1)S(1)} %get-tuple-element.100), channel_id=1, source_target_pairs={{0,1},{1,0},{2,3},{3,2},{4,5},{5,4},{6,7},{7,6},{8,9},{9,8},{10,11... | collective-permute-start | bytes 1376264 | tf_op jit(solution)/shard_map/back_3/ppermute | solution.py:64
  62.1 2.9 %collective-permute-start.19 = (bf16[2,64,1792]{2,1,0:T(8,128)(2,1)S(1)}, bf16[2,64,1792]{2,1,0:T(8,128)(2,1)S(1)}, u32[]{:S(2)}, u32[]{:S(2)}) collective-permute-start(bf16[2,64,1792]{2,1,0:T(8,128)(2,1)S(1)} %get-tuple-element.103), channel_id=1, source_target_pairs={{0,1},{1,0},{2,3},{3,2},{4,5},{5,4},{6,7},{7,6},{8,9},{9,8},{10,11... | collective-permute-start | bytes 1376264 | tf_op jit(solution)/shard_map/back_2/ppermute | solution.py:64
  63.1 8.5 %collective-permute-start.22 = (bf16[2,64,1792]{2,1,0:T(8,128)(2,1)S(1)}, bf16[2,64,1792]{2,1,0:T(8,128)(2,1)S(1)}, u32[]{:S(2)}, u32[]{:S(2)}) collective-permute-start(bf16[2,64,1792]{2,1,0:T(8,128)(2,1)S(1)} %get-tuple-element.107), channel_id=1, source_target_pairs={{0,16},{1,3},{2,18},{3,1},{4,20},{5,7},{6,22},{7,5},{8,24},{9,11},... | collective-permute-start | bytes 1376264 | tf_op jit(solution)/shard_map/u3/ppermute | solution.py:92
  64.6 7.7 %collective-permute-start.20 = (bf16[2,64,1792]{2,1,0:T(8,128)(2,1)S(1)}, bf16[2,64,1792]{2,1,0:T(8,128)(2,1)S(1)}, u32[]{:S(2)}, u32[]{:S(2)}) collective-permute-start(bf16[2,64,1792]{2,1,0:T(8,128)(2,1)S(1)} %get-tuple-element.106), channel_id=1, source_target_pairs={{0,1},{1,0},{2,3},{3,2},{4,5},{5,4},{6,7},{7,6},{8,9},{9,8},{10,11... | collective-permute-start | bytes 1376264 | tf_op jit(solution)/shard_map/back_0/ppermute | solution.py:64
  64.6 23.1 %collective-permute-start.21 = (bf16[4,64,1792]{2,1,0:T(8,128)(2,1)S(1)}, bf16[4,64,1792]{2,1,0:T(8,128)(2,1)S(1)}, u32[]{:S(2)}, u32[]{:S(2)}) collective-permute-start(bf16[4,64,1792]{2,1,0:T(8,128)(2,1)S(1)} %shard_map.77), channel_id=1, source_target_pairs={{0,4},{1,5},{2,6},{3,7},{4,0},{5,1},{6,2},{7,3},{8,12},{9,13},{10,... | collective-permute-start | bytes 2752520 | tf_op jit(solution)/shard_map/n/ppermute | solution.py:64
  71.7 8.5 %collective-permute-start.23 = (bf16[64,1792]{1,0:T(8,128)(2,1)S(1)}, bf16[64,1792]{1,0:T(8,128)(2,1)S(1)}, u32[]{:S(2)}, u32[]{:S(2)}) collective-permute-start(bf16[64,1792]{1,0:T(8,128)(2,1)S(1)} %slice_bitcast_fusion.4), channel_id=1, source_target_pairs={{0,2},{1,17},{2,0},{3,19},{4,6},{5,21},{6,4},{7,23},{8,10},{9,25},... | collective-permute-start | bytes 688136 | tf_op jit(solution)/shard_map/v3/ppermute | solution.py:92
  72.7 15.1 %collective-permute-start.26 = (bf16[2,64,1792]{2,1,0:T(8,128)(2,1)S(1)}, bf16[2,64,1792]{2,1,0:T(8,128)(2,1)S(1)}, u32[]{:S(2)}, u32[]{:S(2)}) collective-permute-start(bf16[2,64,1792]{2,1,0:T(8,128)(2,1)S(1)} %get-tuple-element.111), channel_id=1, source_target_pairs={{0,16},{1,3},{2,18},{3,1},{4,20},{5,7},{6,22},{7,5},{8,24},{9,11},... | collective-permute-start | bytes 1376264 | tf_op jit(solution)/shard_map/u2/ppermute | solution.py:92
  80.3 11.9 %collective-permute-start.28 = (bf16[64,1792]{1,0:T(8,128)(2,1)S(1)}, bf16[64,1792]{1,0:T(8,128)(2,1)S(1)}, u32[]{:S(2)}, u32[]{:S(2)}) collective-permute-start(bf16[64,1792]{1,0:T(8,128)(2,1)S(1)} %fusion.4), channel_id=1, source_target_pairs={{0,4},{1,5},{2,6},{3,7},{4,0},{5,1},{6,2},{7,3},{8,12},{9,13},{10,... | collective-permute-start | bytes 688136 | tf_op jit(solution)/shard_map/s3/ppermute | solution.py:64
  87.9 8.5 %collective-permute-start.27 = (bf16[64,1792]{1,0:T(8,128)(2,1)S(1)}, bf16[64,1792]{1,0:T(8,128)(2,1)S(1)}, u32[]{:S(2)}, u32[]{:S(2)}) collective-permute-start(bf16[64,1792]{1,0:T(8,128)(2,1)S(1)} %slice_bitcast_fusion), channel_id=1, source_target_pairs={{0,2},{1,17},{2,0},{3,19},{4,6},{5,21},{6,4},{7,23},{8,10},{9,25},... | collective-permute-start | bytes 688136 | tf_op jit(solution)/shard_map/v2/ppermute | solution.py:92
  88.7 9.8 %collective-permute-start.24 = (bf16[2,64,1792]{2,1,0:T(8,128)(2,1)S(1)}, bf16[2,64,1792]{2,1,0:T(8,128)(2,1)S(1)}, u32[]{:S(2)}, u32[]{:S(2)}) collective-permute-start(bf16[2,64,1792]{2,1,0:T(8,128)(2,1)S(1)} %slice.35), channel_id=1, source_target_pairs={{0,16},{1,3},{2,18},{3,1},{4,20},{5,7},{6,22},{7,5},{8,24},{9,11},... | collective-permute-start | bytes 1376264 | tf_op jit(solution)/shard_map/u0/ppermute | solution.py:92
  96.5 9.3 %collective-permute-start.29 = (bf16[64,1792]{1,0:T(8,128)(2,1)S(1)}, bf16[64,1792]{1,0:T(8,128)(2,1)S(1)}, u32[]{:S(2)}, u32[]{:S(2)}) collective-permute-start(bf16[64,1792]{1,0:T(8,128)(2,1)S(1)} %fusion.1), channel_id=1, source_target_pairs={{0,8},{1,9},{2,10},{3,11},{4,12},{5,13},{6,14},{7,15},{8,0},{9,1},... | collective-permute-start | bytes 688136 | tf_op jit(solution)/shard_map/s2/ppermute | solution.py:64
  98.6 7.2 %collective-permute-start.25 = (bf16[64,1792]{1,0:T(8,128)(2,1)S(1)}, bf16[64,1792]{1,0:T(8,128)(2,1)S(1)}, u32[]{:S(2)}, u32[]{:S(2)}) collective-permute-start(bf16[64,1792]{1,0:T(8,128)(2,1)S(1)} %slice_bitcast_fusion.2), channel_id=1, source_target_pairs={{0,2},{1,17},{2,0},{3,19},{4,6},{5,21},{6,4},{7,23},{8,10},{9,25},... | collective-permute-start | bytes 688136 | tf_op jit(solution)/shard_map/v0/ppermute | solution.py:92
  (6 other events, 19.0 us)

commit v5 on v4

--- a/solution.py
+++ b/solution.py
@@ -409,14 +409,13 @@
     n = swap_z(k1, 1, "n")
     u3 = swap_xy(give_3, True, "u3")
     u3 = add(keep_3, after(u3, keep_2))
-    u2 = swap_xy(after(give_2, u3), True, "u2")
     v3 = swap_xy(u3[1], False, "v3")
-    s3 = add(u3[0], v3)
+    u2 = swap_xy(give_2, True, "u2")
+    u2 = add(keep_2, after(u2, u3))
+    v2 = swap_xy(u2[1], False, "v2")
+    s3 = add(u3[0], after(v3, u2))
     n = add(own, after(n, s3))
-    u2 = after(u2, s3)
     s3 = swap_z(s3, 1, "s3")
-    u2 = add(keep_2, u2)
-    v2 = swap_xy(u2[1], False, "v2")
     s2 = add(u2[0], v2, s3)
     u0 = swap_xy(n[:2], True, "u0")
     s2 = swap_z(s2, 2, "s2")

time: 107 us -> 106 us (level)
  waiting for transfers between devices: 39.5 us -> 38 us
    ppermute x18, waiting for transfers between devices: 22.1 us -> 20.5 us  [swap_expert(): return lax.ppermute(value, 'expert', pairs)]
    ppermute x18, starting transfers between devices: 15.6 us -> 16.8 us  [swap_expert(): return lax.ppermute(value, 'expert', pairs)]
    ppermute x12, starting transfers between devices: 13.8 us -> 12.7 us  [swap_xy(): return lax.ppermute(value, ('dp', 'expert'), pairs)]
  transfers between devices with their start and end apart: 30 -> 30, of which waited for: 11 -> 12; matrix products, arithmetic and copies ran while one was open for 1% -> 1% of each run, Pallas kernels for 22% -> 23%
where the time goes in v5:
time: 106 us; the launch traced here: 105 us
  waiting for transfers between devices  38 us (36%)
  starting transfers between devices  29.5 us (28%)
  Pallas kernels  27.5 us (26%)
  local copies, waits for them, and re-layouts  8.37 us (8%)
  other arithmetic  1.54 us (1%)
    pallas_call x17, Pallas kernels, call(): pl.pallas_call(kernel, out_shape=out, in_specs=spec, out_specs=jax.tree.m...  25.7 us
    ppermute x18, waiting for transfers between devices, swap_expert(): return lax.ppermute(value, 'expert', pairs)  20.5 us
    ppermute x12, waiting for transfers between devices, swap_xy(): return lax.ppermute(value, ('dp', 'expert'), pairs)  17.5 us
    ppermute x18, starting transfers between devices, swap_expert(): return lax.ppermute(value, 'expert', pairs)  16.8 us
    ppermute x12, starting transfers between devices, swap_xy(): return lax.ppermute(value, ('dp', 'expert'), pairs)  12.7 us
    unnamed x16, local copies, waits for them, and re-layouts  8.29 us
  transfers between devices with their start and end apart: 30, of which 12 were waited for; matrix products, arithmetic and copies ran while one was open for 1% of the time, Pallas kernels for 23%

profile of v5, /device:TPU:0, one launch (start us, length us, event | category | flops | bytes accessed | tf_op | source)
XLA Modules:
  0.0 105.2 jit_solution(4415377640281344294)
XLA Ops:
  0.0 1.9 %shard_map.64 = (bf16[64,1920]{1,0:T(8,128)(2,1)}, bf16[64,1792]{1,0:T(8,128)(2,1)}) custom-call(s32[1]{0:T(128)} %bitcast.1.x_ref, bf16[64,3584]{1,0:T(8,128)(2,1)} %tokens_ref.1, s32[8,64]{1,0:T(8,128)} %bitcast.30, s32[8,64]{1,0:T(8,128)} %bitcast.31), custom_call_target="tpu_custom_call" | custom-call | flops 1 | bytes 1 | tf_op jit(solution)/shard_map/pallas_call | solution.py:135
  1.9 4.0 %collective-permute-start.2 = (bf16[64,1920]{1,0:T(8,128)(2,1)}, bf16[64,1920]{1,0:T(8,128)(2,1)}, u32[]{:S(2)}, u32[]{:S(2)}) collective-permute-start(bf16[64,1920]{1,0:T(8,128)(2,1)} %get-tuple-element.60.refs_0_), channel_id=1, source_target_pairs={{0,8},{1,9},{2,10},{3,11},{4,12},{5,13},{6,14},{7,15},{8,0},{9,1},... | collective-permute-start | bytes 737288 | tf_op jit(solution)/shard_map/m2/ppermute | solution.py:64
  5.9 1.5 %collective-permute-start.1 = (bf16[64,1920]{1,0:T(8,128)(2,1)}, bf16[64,1920]{1,0:T(8,128)(2,1)}, u32[]{:S(2)}, u32[]{:S(2)}) collective-permute-start(bf16[64,1920]{1,0:T(8,128)(2,1)} %get-tuple-element.60.refs_0_), channel_id=1, source_target_pairs={{0,2},{1,3},{2,0},{3,1},{4,6},{5,7},{6,4},{7,5},{8,10},{9,11},{10,... | collective-permute-start | bytes 737288 | tf_op jit(solution)/shard_map/m0y/ppermute | solution.py:64
  8.0 1.6 %collective-permute-start.6 = (bf16[64,1792]{1,0:T(8,128)(2,1)}, bf16[64,1792]{1,0:T(8,128)(2,1)}, u32[]{:S(2)}, u32[]{:S(2)}) collective-permute-start(bf16[64,1792]{1,0:T(8,128)(2,1)} %get-tuple-element.59.refs_1_), channel_id=1, source_target_pairs={{0,4},{1,5},{2,6},{3,7},{4,0},{5,1},{6,2},{7,3},{8,12},{9,13},{10,... | collective-permute-start | bytes 688136 | tf_op jit(solution)/shard_map/f1/ppermute | solution.py:64
  10.0 3.1 %copy-done = bf16[1,3584,1024]{2,1,0:T(8,128)(2,1)S(1)} copy-done((bf16[1,3584,1024]{2,1,0:T(8,128)(2,1)S(1)}, bf16[1,3584,1024]{2,1,0:T(8,128)(2,1)}, u32[]{:S(2)}) %copy-start) | copy-done | bytes 7340056
  13.1 3.1 %copy-done.1 = bf16[1,3584,1024]{2,1,0:T(8,128)(2,1)S(1)} copy-done((bf16[1,3584,1024]{2,1,0:T(8,128)(2,1)S(1)}, bf16[1,3584,1024]{2,1,0:T(8,128)(2,1)}, u32[]{:S(2)}) %copy-start.1) | copy-done | bytes 7340056
  16.2 2.4 %collective-permute-done.refs_3_ = bf16[64,1792]{1,0:T(8,128)(2,1)} collective-permute-done((bf16[64,1792]{1,0:T(8,128)(2,1)}, bf16[64,1792]{1,0:T(8,128)(2,1)}, u32[]{:S(2)}, u32[]{:S(2)}) %collective-permute-start) | collective-permute-done | bytes 229408 | tf_op jit(solution)/shard_map/f0y/ppermute | solution.py:64
  18.6 1.6 %collective-permute-start.5 = (bf16[64,1920]{1,0:T(8,128)(2,1)}, bf16[64,1920]{1,0:T(8,128)(2,1)S(1)}, u32[]{:S(2)}, u32[]{:S(2)}) collective-permute-start(bf16[64,1920]{1,0:T(8,128)(2,1)} %collective-permute-done.2.refs_0_), channel_id=1, source_target_pairs={{0,4},{1,5},{2,6},{3,7},{4,0},{5,1},{6,2},{7,3},{8,12},{9,13},{10,... | collective-permute-start | bytes 737288 | tf_op jit(solution)/shard_map/m3/ppermute | solution.py:64
  20.2 1.5 %collective-permute-start.4 = (bf16[64,1920]{1,0:T(8,128)(2,1)}, bf16[64,1920]{1,0:T(8,128)(2,1)S(1)}, u32[]{:S(2)}, u32[]{:S(2)}) collective-permute-start(bf16[64,1920]{1,0:T(8,128)(2,1)} %collective-permute-done.2.refs_0_), channel_id=1, source_target_pairs={{0,2},{1,17},{2,0},{3,19},{4,6},{5,21},{6,4},{7,23},{8,10},{9,25},... | collective-permute-start | bytes 737288 | tf_op jit(solution)/shard_map/r2/ppermute | solution.py:92
  21.7 1.5 %collective-permute-start.3 = (bf16[64,1920]{1,0:T(8,128)(2,1)}, bf16[64,1920]{1,0:T(8,128)(2,1)S(1)}, u32[]{:S(2)}, u32[]{:S(2)}) collective-permute-start(bf16[64,1920]{1,0:T(8,128)(2,1)} %collective-permute-done.2.refs_0_), channel_id=1, source_target_pairs={{0,16},{1,3},{2,18},{3,1},{4,20},{5,7},{6,22},{7,5},{8,24},{9,11},... | collective-permute-start | bytes 737288 | tf_op jit(solution)/shard_map/q2/ppermute | solution.py:92
  25.1 2.0 %shard_map.66 = (bf16[64,3712]{1,0:T(8,128)(2,1)S(1)}, bf16[64,3712]{1,0:T(8,128)(2,1)S(1)}, bf16[2,64,64]{2,1,0:T(8,128)(2,1)S(1)}, bf16[64,3712]{1,0:T(8,128)(2,1)S(1)}) custom-call(s32[1]{0:T(128)} %bitcast.4.me_ref, bf16[64,1920]{1,0:T(8,128)(2,1)S(1)} %copy-done.4, bf16[64,1792]{1,0:T(8,128)(2,1)S(1)} %copy-done.5, ...), custom_call_target="tpu_custom_call" | custom-call | flops 34359738368 | bytes 1 | tf_op jit(solution)/shard_map/pallas_call | solution.py:103
  29.3 1.6 %collective-permute-start.10 = (bf16[64,1920]{1,0:T(8,128)(2,1)S(1)}, bf16[64,1920]{1,0:T(8,128)(2,1)S(1)}, u32[]{:S(2)}, u32[]{:S(2)}) collective-permute-start(bf16[64,1920]{1,0:T(8,128)(2,1)S(1)} %collective-permute-done.3.refs_2_.refs_0_), channel_id=1, source_target_pairs={{0,2},{1,17},{2,0},{3,19},{4,6},{5,21},{6,4},{7,23},{8,10},{9,25},... | collective-permute-start | bytes 737288 | tf_op jit(solution)/shard_map/t2/ppermute | solution.py:92
  33.0 2.8 %shard_map.67.hidden_ref = bf16[128,1024]{1,0:T(8,128)(2,1)S(1)} custom-call(s32[2]{0:T(128)S(1)} %pad_add_fusion.scalar_ref, bf16[64,3712]{1,0:T(8,128)(2,1)S(1)} %get-tuple-element.70.keep_ref, bf16[64,3712]{1,0:T(8,128)(2,1)S(1)} %collective-permute-done.8.got_ref, bf16[1,3584,1024]{2,1,0:T(8,128)(2,1)S(1)} %bitcast.29, bf16[1,3584,1024]{2,1,0:T(8,128)(2,1)S(1)} %copy-done.2), custom_call_target="tpu_custom_call" | custom-call | flops 1 | bytes 1 | tf_op jit(solution)/shard_map/pallas_call | solution.py:103
  36.1 1.7 %shard_map.68 = (bf16[2,64,1792]{2,1,0:T(8,128)(2,1)S(1)}, bf16[2,64,1792]{2,1,0:T(8,128)(2,1)S(1)}) custom-call(s32[2]{0:T(128)S(1)} %pad_add_fusion.scalar_ref, bf16[128,1024]{1,0:T(8,128)(2,1)S(1)} %shard_map.67.hidden_ref, bf16[1,1024,3584]{2,1,0:T(8,128)(2,1)S(1)} %copy-done.3), custom_call_target="tpu_custom_call" | custom-call | flops 1 | bytes 1 | tf_op jit(solution)/shard_map/pallas_call | solution.py:103
  37.8 3.6 %collective-permute-done.9.refs_2_ = bf16[64,3712]{1,0:T(8,128)(2,1)S(1)} collective-permute-done((bf16[64,3712]{1,0:T(8,128)(2,1)S(1)}, bf16[64,3712]{1,0:T(8,128)(2,1)S(1)}, u32[]{:S(2)}, u32[]{:S(2)}) %collective-permute-start.9) | collective-permute-done | bytes 475168 | tf_op jit(solution)/shard_map/w1y/ppermute | solution.py:64
  41.4 1.9 %shard_map.69 = (bf16[128,1920]{1,0:T(8,128)(2,1)S(1)}, bf16[128,1920]{1,0:T(8,128)(2,1)S(1)}, bf16[4,64,64]{2,1,0:T(8,128)(2,1)S(1)}) custom-call(s32[1]{0:T(128)} %bitcast.5.me_ref, bf16[64,1920]{1,0:T(8,128)(2,1)} %collective-permute-done.2.refs_0_, bf16[64,1920]{1,0:T(8,128)(2,1)S(1)} %collective-permute-done.4.refs_1_, ...), custom_call_target="tpu_custom_call" | custom-call | flops 34359738368 | bytes 1 | tf_op jit(solution)/shard_map/pallas_call | solution.py:103
  44.0 1.7 %shard_map.70 = (bf16[64,3712]{1,0:T(8,128)(2,1)S(1)}, bf16[64,3712]{1,0:T(8,128)(2,1)S(1)}, bf16[2,64,64]{2,1,0:T(8,128)(2,1)S(1)}) custom-call(s32[1]{0:T(128)} %bitcast.6.me_ref, bf16[64,1920]{1,0:T(8,128)(2,1)S(1)} %collective-permute-done.7.refs_0_, bf16[64,1792]{1,0:T(8,128)(2,1)} %collective-permute-done.6.refs_1_, ...), custom_call_target="tpu_custom_call" | custom-call | flops 1 | bytes 1 | tf_op jit(solution)/shard_map/pallas_call | solution.py:103
  46.9 2.6 %shard_map.71 = (f32[256,1024]{1,0:T(8,128)S(1)}, f32[256,1024]{1,0:T(8,128)S(1)}) custom-call(s32[2]{0:T(128)S(1)} %pad_add_fusion.scalar_ref, bf16[128,1920]{1,0:T(8,128)(2,1)S(1)} %get-tuple-element.79.keep_ref.refs_2_, bf16[128,1920]{1,0:T(8,128)(2,1)S(1)} %collective-permute-done.13.got_ref.refs_3_, bf16[1,3584,1024]{2,1,0:T(8,128)(2,1)S(1)} %bitcast.29, ...), custom_call_target="tpu_custom_call" | custom-call | flops 1 | bytes 1 | tf_op jit(solution)/shard_map/pallas_call | solution.py:103
  50.2 2.8 %shard_map.73.hidden_ref = bf16[128,1024]{1,0:T(8,128)(2,1)S(1)} custom-call(s32[2]{0:T(128)S(1)} %pad_add_fusion.scalar_ref, bf16[64,3712]{1,0:T(8,128)(2,1)S(1)} %get-tuple-element.82.keep_ref, bf16[64,3712]{1,0:T(8,128)(2,1)S(1)} %collective-permute-done.15.got_ref, bf16[1,3584,1024]{2,1,0:T(8,128)(2,1)S(1)} %bitcast.29, bf16[1,3584,1024]{2,1,0:T(8,128)(2,1)S(1)} %copy-done.2), custom_call_target="tpu_custom_call" | custom-call | flops 1 | bytes 1 | tf_op jit(solution)/shard_map/pallas_call | solution.py:103
  53.0 1.7 %shard_map.74 = (bf16[2,64,1792]{2,1,0:T(8,128)(2,1)S(1)}, bf16[2,64,1792]{2,1,0:T(8,128)(2,1)S(1)}) custom-call(s32[2]{0:T(128)S(1)} %pad_add_fusion.scalar_ref, bf16[128,1024]{1,0:T(8,128)(2,1)S(1)} %shard_map.73.hidden_ref, bf16[1,1024,3584]{2,1,0:T(8,128)(2,1)S(1)} %copy-done.3), custom_call_target="tpu_custom_call" | custom-call | flops 1 | bytes 1 | tf_op jit(solution)/shard_map/pallas_call | solution.py:103
  55.3 3.0 %shard_map.75.hidden_ref = bf16[256,1024]{1,0:T(8,128)(2,1)S(1)} custom-call(s32[2]{0:T(128)S(1)} %pad_add_fusion.scalar_ref, bf16[128,1792]{1,0:T(8,128)(2,1)S(1)} %get-tuple-element.87.keep_ref, bf16[128,1792]{1,0:T(8,128)(2,1)S(1)} %collective-permute-done.16.got_ref, bf16[1,3584,1024]{2,1,0:T(8,128)(2,1)S(1)} %bitcast.29, ...), custom_call_target="tpu_custom_call" | custom-call | flops 1 | bytes 1 | tf_op jit(solution)/shard_map/pallas_call | solution.py:103
  58.3 1.7 %shard_map.76 = (bf16[2,64,1792]{2,1,0:T(8,128)(2,1)S(1)}, bf16[2,64,1792]{2,1,0:T(8,128)(2,1)S(1)}) custom-call(s32[2]{0:T(128)S(1)} %pad_add_fusion.scalar_ref, bf16[256,1024]{1,0:T(8,128)(2,1)S(1)} %shard_map.75.hidden_ref, bf16[1,1024,3584]{2,1,0:T(8,128)(2,1)S(1)} %copy-done.3, f32[16,128]{1,0:T(8,128)S(1)} %shard_map.65.refs_0_), custom_call_target="tpu_custom_call" | custom-call | flops 1 | bytes 1 | tf_op jit(solution)/shard_map/pallas_call | solution.py:103
  60.4 1.7 %shard_map.78 = (bf16[2,64,1792]{2,1,0:T(8,128)(2,1)S(1)}, bf16[2,64,1792]{2,1,0:T(8,128)(2,1)S(1)}) custom-call(s32[2]{0:T(128)S(1)} %pad_add_fusion.scalar_ref, bf16[256,1024]{1,0:T(8,128)(2,1)S(1)} %shard_map.75.hidden_ref, bf16[1,1024,3584]{2,1,0:T(8,128)(2,1)S(1)} %copy-done.3), custom_call_target="tpu_custom_call" | custom-call | flops 1 | bytes 1 | tf_op jit(solution)/shard_map/pallas_call | solution.py:103
  63.1 1.5 %collective-permute-start.22 = (bf16[2,64,1792]{2,1,0:T(8,128)(2,1)S(1)}, bf16[2,64,1792]{2,1,0:T(8,128)(2,1)S(1)}, u32[]{:S(2)}, u32[]{:S(2)}) collective-permute-start(bf16[2,64,1792]{2,1,0:T(8,128)(2,1)S(1)} %get-tuple-element.107), channel_id=1, source_target_pairs={{0,16},{1,3},{2,18},{3,1},{4,20},{5,7},{6,22},{7,5},{8,24},{9,11},... | collective-permute-start | bytes 1376264 | tf_op jit(solution)/shard_map/u3/ppermute | solution.py:92
  66.5 5.2 %collective-permute-done.22 = bf16[2,64,1792]{2,1,0:T(8,128)(2,1)S(1)} collective-permute-done((bf16[2,64,1792]{2,1,0:T(8,128)(2,1)S(1)}, bf16[2,64,1792]{2,1,0:T(8,128)(2,1)S(1)}, u32[]{:S(2)}, u32[]{:S(2)}) %collective-permute-start.22) | collective-permute-done | bytes 458784 | tf_op jit(solution)/shard_map/u3/ppermute | solution.py:92
  71.8 4.8 %collective-permute-done.24 = bf16[2,64,1792]{2,1,0:T(8,128)(2,1)S(1)} collective-permute-done((bf16[2,64,1792]{2,1,0:T(8,128)(2,1)S(1)}, bf16[2,64,1792]{2,1,0:T(8,128)(2,1)S(1)}, u32[]{:S(2)}, u32[]{:S(2)}) %collective-permute-start.24) | collective-permute-done | bytes 458784 | tf_op jit(solution)/shard_map/u2/ppermute | solution.py:92
  78.9 3.9 %collective-permute-done.23 = bf16[64,1792]{1,0:T(8,128)(2,1)S(1)} collective-permute-done((bf16[64,1792]{1,0:T(8,128)(2,1)S(1)}, bf16[64,1792]{1,0:T(8,128)(2,1)S(1)}, u32[]{:S(2)}, u32[]{:S(2)}) %collective-permute-start.23) | collective-permute-done | bytes 229408 | tf_op jit(solution)/shard_map/v3/ppermute | solution.py:92
  83.4 4.6 %collective-permute-done.21 = bf16[4,64,1792]{2,1,0:T(8,128)(2,1)S(1)} collective-permute-done((bf16[4,64,1792]{2,1,0:T(8,128)(2,1)S(1)}, bf16[4,64,1792]{2,1,0:T(8,128)(2,1)S(1)}, u32[]{:S(2)}, u32[]{:S(2)}) %collective-permute-start.21) | collective-permute-done | bytes 917536 | tf_op jit(solution)/shard_map/n/ppermute | solution.py:64
  88.8 2.3 %collective-permute-done.28 = bf16[64,1792]{1,0:T(8,128)(2,1)S(1)} collective-permute-done((bf16[64,1792]{1,0:T(8,128)(2,1)S(1)}, bf16[64,1792]{1,0:T(8,128)(2,1)S(1)}, u32[]{:S(2)}, u32[]{:S(2)}) %collective-permute-start.28) | collective-permute-done | bytes 229408 | tf_op jit(solution)/shard_map/s3/ppermute | solution.py:64
  91.1 3.2 %collective-permute-start.29 = (bf16[64,1792]{1,0:T(8,128)(2,1)S(1)}, bf16[64,1792]{1,0:T(8,128)(2,1)S(1)}, u32[]{:S(2)}, u32[]{:S(2)}) collective-permute-start(bf16[64,1792]{1,0:T(8,128)(2,1)S(1)} %fusion.1), channel_id=1, source_target_pairs={{0,8},{1,9},{2,10},{3,11},{4,12},{5,13},{6,14},{7,15},{8,0},{9,1},... | collective-permute-start | bytes 688136 | tf_op jit(solution)/shard_map/s2/ppermute | solution.py:64
  94.3 2.5 %collective-permute-done.25 = bf16[2,64,1792]{2,1,0:T(8,128)(2,1)S(1)} collective-permute-done((bf16[2,64,1792]{2,1,0:T(8,128)(2,1)S(1)}, bf16[2,64,1792]{2,1,0:T(8,128)(2,1)S(1)}, u32[]{:S(2)}, u32[]{:S(2)}) %collective-permute-start.25) | collective-permute-done | bytes 458784 | tf_op jit(solution)/shard_map/u0/ppermute | solution.py:92
  97.7 6.8 %collective-permute-done.29 = bf16[64,1792]{1,0:T(8,128)(2,1)S(1)} collective-permute-done((bf16[64,1792]{1,0:T(8,128)(2,1)S(1)}, bf16[64,1792]{1,0:T(8,128)(2,1)S(1)}, u32[]{:S(2)}, u32[]{:S(2)}) %collective-permute-start.29) | collective-permute-done | bytes 229408 | tf_op jit(solution)/shard_map/s2/ppermute | solution.py:64
  (75 shorter events, 19.2 us)
Async XLA Ops:
  1.9 16.7 %collective-permute-start.2 = (bf16[64,1920]{1,0:T(8,128)(2,1)}, bf16[64,1920]{1,0:T(8,128)(2,1)}, u32[]{:S(2)}, u32[]{:S(2)}) collective-permute-start(bf16[64,1920]{1,0:T(8,128)(2,1)} %get-tuple-element.60.refs_0_), channel_id=1, source_target_pairs={{0,8},{1,9},{2,10},{3,11},{4,12},{5,13},{6,14},{7,15},{8,0},{9,1},... | collective-permute-start | bytes 737288 | tf_op jit(solution)/shard_map/m2/ppermute | solution.py:64
  5.9 12.7 %collective-permute-start.1 = (bf16[64,1920]{1,0:T(8,128)(2,1)}, bf16[64,1920]{1,0:T(8,128)(2,1)}, u32[]{:S(2)}, u32[]{:S(2)}) collective-permute-start(bf16[64,1920]{1,0:T(8,128)(2,1)} %get-tuple-element.60.refs_0_), channel_id=1, source_target_pairs={{0,2},{1,3},{2,0},{3,1},{4,6},{5,7},{6,4},{7,5},{8,10},{9,11},{10,... | collective-permute-start | bytes 737288 | tf_op jit(solution)/shard_map/m0y/ppermute | solution.py:64
  7.4 11.1 %collective-permute-start = (bf16[64,1792]{1,0:T(8,128)(2,1)}, bf16[64,1792]{1,0:T(8,128)(2,1)}, u32[]{:S(2)}, u32[]{:S(2)}) collective-permute-start(bf16[64,1792]{1,0:T(8,128)(2,1)} %get-tuple-element.59.refs_1_), channel_id=1, source_target_pairs={{0,2},{1,3},{2,0},{3,1},{4,6},{5,7},{6,4},{7,5},{8,10},{9,11},{10,... | collective-permute-start | bytes 688136 | tf_op jit(solution)/shard_map/f0y/ppermute | solution.py:64
  8.0 19.1 %collective-permute-start.6 = (bf16[64,1792]{1,0:T(8,128)(2,1)}, bf16[64,1792]{1,0:T(8,128)(2,1)}, u32[]{:S(2)}, u32[]{:S(2)}) collective-permute-start(bf16[64,1792]{1,0:T(8,128)(2,1)} %get-tuple-element.59.refs_1_), channel_id=1, source_target_pairs={{0,4},{1,5},{2,6},{3,7},{4,0},{5,1},{6,2},{7,3},{8,12},{9,13},{10,... | collective-permute-start | bytes 688136 | tf_op jit(solution)/shard_map/f1/ppermute | solution.py:64
  9.5 17.6 %collective-permute-start.7 = (bf16[64,1920]{1,0:T(8,128)(2,1)}, bf16[64,1920]{1,0:T(8,128)(2,1)S(1)}, u32[]{:S(2)}, u32[]{:S(2)}) collective-permute-start(bf16[64,1920]{1,0:T(8,128)(2,1)} %get-tuple-element.60.refs_0_), channel_id=1, source_target_pairs={{0,4},{1,5},{2,6},{3,7},{4,0},{5,1},{6,2},{7,3},{8,12},{9,13},{10,... | collective-permute-start | bytes 737288 | tf_op jit(solution)/shard_map/m1/ppermute | solution.py:64
  16.1 16.8 %slice-start = ((s8[7340032]{0:T(1024)(128)(4,1)}), s8[3145728]{0:T(1024)(128)(4,1)S(1)}, s32[]{:S(2)}) async-start(s8[7340032]{0:T(1024)(128)(4,1)} %bitcast.28), calls=%async_computation | async-start | bytes 6291456
  18.6 10.7 %collective-permute-start.5 = (bf16[64,1920]{1,0:T(8,128)(2,1)}, bf16[64,1920]{1,0:T(8,128)(2,1)S(1)}, u32[]{:S(2)}, u32[]{:S(2)}) collective-permute-start(bf16[64,1920]{1,0:T(8,128)(2,1)} %collective-permute-done.2.refs_0_), channel_id=1, source_target_pairs={{0,4},{1,5},{2,6},{3,7},{4,0},{5,1},{6,2},{7,3},{8,12},{9,13},{10,... | collective-permute-start | bytes 737288 | tf_op jit(solution)/shard_map/m3/ppermute | solution.py:64
  20.2 9.1 %collective-permute-start.4 = (bf16[64,1920]{1,0:T(8,128)(2,1)}, bf16[64,1920]{1,0:T(8,128)(2,1)S(1)}, u32[]{:S(2)}, u32[]{:S(2)}) collective-permute-start(bf16[64,1920]{1,0:T(8,128)(2,1)} %collective-permute-done.2.refs_0_), channel_id=1, source_target_pairs={{0,2},{1,17},{2,0},{3,19},{4,6},{5,21},{6,4},{7,23},{8,10},{9,25},... | collective-permute-start | bytes 737288 | tf_op jit(solution)/shard_map/r2/ppermute | solution.py:92
  21.7 6.4 %collective-permute-start.3 = (bf16[64,1920]{1,0:T(8,128)(2,1)}, bf16[64,1920]{1,0:T(8,128)(2,1)S(1)}, u32[]{:S(2)}, u32[]{:S(2)}) collective-permute-start(bf16[64,1920]{1,0:T(8,128)(2,1)} %collective-permute-done.2.refs_0_), channel_id=1, source_target_pairs={{0,16},{1,3},{2,18},{3,1},{4,20},{5,7},{6,22},{7,5},{8,24},{9,11},... | collective-permute-start | bytes 737288 | tf_op jit(solution)/shard_map/q2/ppermute | solution.py:92
  25.1 7.9 %copy-start.2 = (bf16[1,3584,1024]{2,1,0:T(8,128)(2,1)S(1)}, bf16[1,3584,1024]{2,1,0:T(8,128)(2,1)}, u32[]{:S(2)}) copy-start(bf16[1,3584,1024]{2,1,0:T(8,128)(2,1)} %up_ref.7) | copy-start | bytes 22020100
  28.1 4.9 %collective-permute-start.8 = (bf16[64,3712]{1,0:T(8,128)(2,1)S(1)}, bf16[64,3712]{1,0:T(8,128)(2,1)S(1)}, u32[]{:S(2)}, u32[]{:S(2)}) collective-permute-start(bf16[64,3712]{1,0:T(8,128)(2,1)S(1)} %get-tuple-element.72), channel_id=1, source_target_pairs={{0,1},{1,0},{2,3},{3,2},{4,5},{5,4},{6,7},{7,6},{8,9},{9,8},{10,11... | collective-permute-start | bytes 1425416 | tf_op jit(solution)/shard_map/rows_0/ppermute | solution.py:64
  28.1 13.3 %collective-permute-start.9 = (bf16[64,3712]{1,0:T(8,128)(2,1)S(1)}, bf16[64,3712]{1,0:T(8,128)(2,1)S(1)}, u32[]{:S(2)}, u32[]{:S(2)}) collective-permute-start(bf16[64,3712]{1,0:T(8,128)(2,1)S(1)} %get-tuple-element.74), channel_id=1, source_target_pairs={{0,4},{1,5},{2,6},{3,7},{4,0},{5,1},{6,2},{7,3},{8,12},{9,13},{10,... | collective-permute-start | bytes 1425416 | tf_op jit(solution)/shard_map/w1y/ppermute | solution.py:64
  29.3 12.1 %collective-permute-start.10 = (bf16[64,1920]{1,0:T(8,128)(2,1)S(1)}, bf16[64,1920]{1,0:T(8,128)(2,1)S(1)}, u32[]{:S(2)}, u32[]{:S(2)}) collective-permute-start(bf16[64,1920]{1,0:T(8,128)(2,1)S(1)} %collective-permute-done.3.refs_2_.refs_0_), channel_id=1, source_target_pairs={{0,2},{1,17},{2,0},{3,19},{4,6},{5,21},{6,4},{7,23},{8,10},{9,25},... | collective-permute-start | bytes 737288 | tf_op jit(solution)/shard_map/t2/ppermute | solution.py:92
  30.9 10.5 %collective-permute-start.12 = (bf16[64,1920]{1,0:T(8,128)(2,1)S(1)}, bf16[64,1920]{1,0:T(8,128)(2,1)S(1)}, u32[]{:S(2)}, u32[]{:S(2)}) collective-permute-start(bf16[64,1920]{1,0:T(8,128)(2,1)S(1)} %collective-permute-done.5.refs_3_), channel_id=1, source_target_pairs={{0,16},{1,3},{2,18},{3,1},{4,20},{5,7},{6,22},{7,5},{8,24},{9,11},... | collective-permute-start | bytes 737288 | tf_op jit(solution)/shard_map/q3/ppermute | solution.py:92
  32.4 9.0 %collective-permute-start.11 = (bf16[64,1920]{1,0:T(8,128)(2,1)S(1)}, bf16[64,1920]{1,0:T(8,128)(2,1)S(1)}, u32[]{:S(2)}, u32[]{:S(2)}) collective-permute-start(bf16[64,1920]{1,0:T(8,128)(2,1)S(1)} %collective-permute-done.5.refs_3_), channel_id=1, source_target_pairs={{0,2},{1,17},{2,0},{3,19},{4,6},{5,21},{6,4},{7,23},{8,10},{9,25},... | collective-permute-start | bytes 737288 | tf_op jit(solution)/shard_map/r3/ppermute | solution.py:92
  43.3 3.6 %collective-permute-start.13 = (bf16[128,1920]{1,0:T(8,128)(2,1)S(1)}, bf16[128,1920]{1,0:T(8,128)(2,1)S(1)}, u32[]{:S(2)}, u32[]{:S(2)}) collective-permute-start(bf16[128,1920]{1,0:T(8,128)(2,1)S(1)} %get-tuple-element.84), channel_id=1, source_target_pairs={{0,1},{1,0},{2,3},{3,2},{4,5},{5,4},{6,7},{7,6},{8,9},{9,8},{10,11... | collective-permute-start | bytes 1474568 | tf_op jit(solution)/shard_map/rows_m/ppermute | solution.py:64
  43.4 6.3 %collective-permute-start.14 = (bf16[64,1920]{1,0:T(8,128)(2,1)S(1)}, bf16[64,1920]{1,0:T(8,128)(2,1)S(1)}, u32[]{:S(2)}, u32[]{:S(2)}) collective-permute-start(bf16[64,1920]{1,0:T(8,128)(2,1)S(1)} %collective-permute-done.12.refs_5_.refs_3_), channel_id=1, source_target_pairs={{0,2},{1,17},{2,0},{3,19},{4,6},{5,21},{6,4},{7,23},{8,10},{9,25},... | collective-permute-start | bytes 737288 | tf_op jit(solution)/shard_map/t3/ppermute | solution.py:92
  45.7 4.5 %collective-permute-start.15 = (bf16[64,3712]{1,0:T(8,128)(2,1)S(1)}, bf16[64,3712]{1,0:T(8,128)(2,1)S(1)}, u32[]{:S(2)}, u32[]{:S(2)}) collective-permute-start(bf16[64,3712]{1,0:T(8,128)(2,1)S(1)} %get-tuple-element.89), channel_id=1, source_target_pairs={{0,1},{1,0},{2,3},{3,2},{4,5},{5,4},{6,7},{7,6},{8,9},{9,8},{10,11... | collective-permute-start | bytes 1425416 | tf_op jit(solution)/shard_map/rows_1/ppermute | solution.py:64
  50.1 5.2 %collective-permute-start.16 = (bf16[128,1792]{1,0:T(8,128)(2,1)S(1)}, bf16[128,1792]{1,0:T(8,128)(2,1)S(1)}, u32[]{:S(2)}, u32[]{:S(2)}) collective-permute-start(bf16[128,1792]{1,0:T(8,128)(2,1)S(1)} %get-tuple-element.92), channel_id=1, source_target_pairs={{0,1},{1,0},{2,3},{3,2},{4,5},{5,4},{6,7},{7,6},{8,9},{9,8},{10,11... | collective-permute-start | bytes 1376264 | tf_op jit(solution)/shard_map/rows_f/ppermute | solution.py:64
  54.7 5.3 %collective-permute-start.17 = (bf16[2,64,1792]{2,1,0:T(8,128)(2,1)S(1)}, bf16[2,64,1792]{2,1,0:T(8,128)(2,1)S(1)}, u32[]{:S(2)}, u32[]{:S(2)}) collective-permute-start(bf16[2,64,1792]{2,1,0:T(8,128)(2,1)S(1)} %get-tuple-element.96), channel_id=1, source_target_pairs={{0,1},{1,0},{2,3},{3,2},{4,5},{5,4},{6,7},{7,6},{8,9},{9,8},{10,11... | collective-permute-start | bytes 1376264 | tf_op jit(solution)/shard_map/back_1/ppermute | solution.py:64
  60.0 2.8 %collective-permute-start.18 = (bf16[2,64,1792]{2,1,0:T(8,128)(2,1)S(1)}, bf16[2,64,1792]{2,1,0:T(8,128)(2,1)S(1)}, u32[]{:S(2)}, u32[]{:S(2)}) collective-permute-start(bf16[2,64,1792]{2,1,0:T(8,128)(2,1)S(1)} %get-tuple-element.100), channel_id=1, source_target_pairs={{0,1},{1,0},{2,3},{3,2},{4,5},{5,4},{6,7},{7,6},{8,9},{9,8},{10,11... | collective-permute-start | bytes 1376264 | tf_op jit(solution)/shard_map/back_3/ppermute | solution.py:64
  62.1 3.0 %collective-permute-start.19 = (bf16[2,64,1792]{2,1,0:T(8,128)(2,1)S(1)}, bf16[2,64,1792]{2,1,0:T(8,128)(2,1)S(1)}, u32[]{:S(2)}, u32[]{:S(2)}) collective-permute-start(bf16[2,64,1792]{2,1,0:T(8,128)(2,1)S(1)} %get-tuple-element.103), channel_id=1, source_target_pairs={{0,1},{1,0},{2,3},{3,2},{4,5},{5,4},{6,7},{7,6},{8,9},{9,8},{10,11... | collective-permute-start | bytes 1376264 | tf_op jit(solution)/shard_map/back_2/ppermute | solution.py:64
  62.7 3.5 %collective-permute-start.20 = (bf16[2,64,1792]{2,1,0:T(8,128)(2,1)S(1)}, bf16[2,64,1792]{2,1,0:T(8,128)(2,1)S(1)}, u32[]{:S(2)}, u32[]{:S(2)}) collective-permute-start(bf16[2,64,1792]{2,1,0:T(8,128)(2,1)S(1)} %get-tuple-element.106), channel_id=1, source_target_pairs={{0,1},{1,0},{2,3},{3,2},{4,5},{5,4},{6,7},{7,6},{8,9},{9,8},{10,11... | collective-permute-start | bytes 1376264 | tf_op jit(solution)/shard_map/back_0/ppermute | solution.py:64
  63.1 8.5 %collective-permute-start.22 = (bf16[2,64,1792]{2,1,0:T(8,128)(2,1)S(1)}, bf16[2,64,1792]{2,1,0:T(8,128)(2,1)S(1)}, u32[]{:S(2)}, u32[]{:S(2)}) collective-permute-start(bf16[2,64,1792]{2,1,0:T(8,128)(2,1)S(1)} %get-tuple-element.107), channel_id=1, source_target_pairs={{0,16},{1,3},{2,18},{3,1},{4,20},{5,7},{6,22},{7,5},{8,24},{9,11},... | collective-permute-start | bytes 1376264 | tf_op jit(solution)/shard_map/u3/ppermute | solution.py:92
  64.7 23.3 %collective-permute-start.21 = (bf16[4,64,1792]{2,1,0:T(8,128)(2,1)S(1)}, bf16[4,64,1792]{2,1,0:T(8,128)(2,1)S(1)}, u32[]{:S(2)}, u32[]{:S(2)}) collective-permute-start(bf16[4,64,1792]{2,1,0:T(8,128)(2,1)S(1)} %shard_map.77), channel_id=1, source_target_pairs={{0,4},{1,5},{2,6},{3,7},{4,0},{5,1},{6,2},{7,3},{8,12},{9,13},{10,... | collective-permute-start | bytes 2752520 | tf_op jit(solution)/shard_map/n/ppermute | solution.py:64
  65.5 11.1 %collective-permute-start.24 = (bf16[2,64,1792]{2,1,0:T(8,128)(2,1)S(1)}, bf16[2,64,1792]{2,1,0:T(8,128)(2,1)S(1)}, u32[]{:S(2)}, u32[]{:S(2)}) collective-permute-start(bf16[2,64,1792]{2,1,0:T(8,128)(2,1)S(1)} %get-tuple-element.109), channel_id=1, source_target_pairs={{0,16},{1,3},{2,18},{3,1},{4,20},{5,7},{6,22},{7,5},{8,24},{9,11},... | collective-permute-start | bytes 1376264 | tf_op jit(solution)/shard_map/u2/ppermute | solution.py:92
  76.7 6.1 %collective-permute-start.23 = (bf16[64,1792]{1,0:T(8,128)(2,1)S(1)}, bf16[64,1792]{1,0:T(8,128)(2,1)S(1)}, u32[]{:S(2)}, u32[]{:S(2)}) collective-permute-start(bf16[64,1792]{1,0:T(8,128)(2,1)S(1)} %slice_bitcast_fusion.4), channel_id=1, source_target_pairs={{0,2},{1,17},{2,0},{3,19},{4,6},{5,21},{6,4},{7,23},{8,10},{9,25},... | collective-permute-start | bytes 688136 | tf_op jit(solution)/shard_map/v3/ppermute | solution.py:92
  77.6 11.2 %collective-permute-start.27 = (bf16[64,1792]{1,0:T(8,128)(2,1)S(1)}, bf16[64,1792]{1,0:T(8,128)(2,1)S(1)}, u32[]{:S(2)}, u32[]{:S(2)}) collective-permute-start(bf16[64,1792]{1,0:T(8,128)(2,1)S(1)} %slice_bitcast_fusion), channel_id=1, source_target_pairs={{0,2},{1,17},{2,0},{3,19},{4,6},{5,21},{6,4},{7,23},{8,10},{9,25},... | collective-permute-start | bytes 688136 | tf_op jit(solution)/shard_map/v2/ppermute | solution.py:92
  82.9 8.2 %collective-permute-start.28 = (bf16[64,1792]{1,0:T(8,128)(2,1)S(1)}, bf16[64,1792]{1,0:T(8,128)(2,1)S(1)}, u32[]{:S(2)}, u32[]{:S(2)}) collective-permute-start(bf16[64,1792]{1,0:T(8,128)(2,1)S(1)} %fusion.4), channel_id=1, source_target_pairs={{0,4},{1,5},{2,6},{3,7},{4,0},{5,1},{6,2},{7,3},{8,12},{9,13},{10,... | collective-permute-start | bytes 688136 | tf_op jit(solution)/shard_map/s3/ppermute | solution.py:64
  88.2 8.6 %collective-permute-start.25 = (bf16[2,64,1792]{2,1,0:T(8,128)(2,1)S(1)}, bf16[2,64,1792]{2,1,0:T(8,128)(2,1)S(1)}, u32[]{:S(2)}, u32[]{:S(2)}) collective-permute-start(bf16[2,64,1792]{2,1,0:T(8,128)(2,1)S(1)} %slice.35), channel_id=1, source_target_pairs={{0,16},{1,3},{2,18},{3,1},{4,20},{5,7},{6,22},{7,5},{8,24},{9,11},... | collective-permute-start | bytes 1376264 | tf_op jit(solution)/shard_map/u0/ppermute | solution.py:92
  91.1 13.3 %collective-permute-start.29 = (bf16[64,1792]{1,0:T(8,128)(2,1)S(1)}, bf16[64,1792]{1,0:T(8,128)(2,1)S(1)}, u32[]{:S(2)}, u32[]{:S(2)}) collective-permute-start(bf16[64,1792]{1,0:T(8,128)(2,1)S(1)} %fusion.1), channel_id=1, source_target_pairs={{0,8},{1,9},{2,10},{3,11},{4,12},{5,13},{6,14},{7,15},{8,0},{9,1},... | collective-permute-start | bytes 688136 | tf_op jit(solution)/shard_map/s2/ppermute | solution.py:64
  97.0 7.5 %collective-permute-start.26 = (bf16[64,1792]{1,0:T(8,128)(2,1)S(1)}, bf16[64,1792]{1,0:T(8,128)(2,1)S(1)}, u32[]{:S(2)}, u32[]{:S(2)}) collective-permute-start(bf16[64,1792]{1,0:T(8,128)(2,1)S(1)} %slice_bitcast_fusion.2), channel_id=1, source_target_pairs={{0,2},{1,17},{2,0},{3,19},{4,6},{5,21},{6,4},{7,23},{8,10},{9,25},... | collective-permute-start | bytes 688136 | tf_op jit(solution)/shard_map/v0/ppermute | solution.py:92
  (6 other events, 19.0 us)

commit v6 on v5

--- a/solution.py
+++ b/solution.py
@@ -399,27 +399,29 @@
     hidden = gate_up(after(scalars, near_1), keep_f, got_f, gate_proj, up_proj, 2, [*first, keep, got])
     near_3, away = down(scalars, hidden, down_proj, 1, 2, touched)
     back_3 = swap_core(away, "back_3")
-    k1 = spread(me, after(put_1, near_3), near_1, back_1, 0, False)
-    near_2, away = down(after(scalars, k1), hidden, down_proj, 0, 2)
+    give_1, keep_1 = spread(me, after(put_1, near_3), near_1, back_1, 0, True)
+    near_2, away = down(after(scalars, keep_1), hidden, down_proj, 0, 2)
     back_2 = swap_core(away, "back_2")
     give_3, keep_3 = spread(me, after(put, near_2), near_3, back_3, 2, True)
     give_2, keep_2 = spread(me, after(put, keep_3), near_2, back_2, 0, True)
-    own = spread(me, after(put_0, keep_2), near_0, back_0, 0, False)
-
-    n = swap_z(k1, 1, "n")
+    give_0, keep_0 = spread(me, after(put_0, keep_2), near_0, back_0, 0, True)
+
+    nk = swap_z(keep_1, 1, "nk")
     u3 = swap_xy(give_3, True, "u3")
-    u3 = add(keep_3, after(u3, keep_2))
+    ng = swap_z(give_1, 1, "ng")
+    u3 = add(keep_3, after(u3, keep_2, ng))
     v3 = swap_xy(u3[1], False, "v3")
     u2 = swap_xy(give_2, True, "u2")
     u2 = add(keep_2, after(u2, u3))
     v2 = swap_xy(u2[1], False, "v2")
     s3 = add(u3[0], after(v3, u2))
-    n = add(own, after(n, s3))
+    ng = add(give_0, after(ng, s3))
+    nk = add(keep_0, after(nk, s3))
     s3 = swap_z(s3, 1, "s3")
     s2 = add(u2[0], v2, s3)
-    u0 = swap_xy(n[:2], True, "u0")
+    u0 = swap_xy(ng, True, "u0")
     s2 = swap_z(s2, 2, "s2")
-    u0 = add(n[2:], u0)
+    u0 = add(nk, u0)
     v0 = swap_xy(u0[1], False, "v0")
     return add(u0[0], v0, s2)
 

time: 106 us -> 103 us (0.972)
  waiting for transfers between devices: 38 us -> 32.3 us
  starting transfers between devices: 29.5 us -> 32.6 us
    ppermute x12, waiting for transfers between devices: 17.5 us -> 7.39 us  [swap_xy(): return lax.ppermute(value, ('dp', 'expert'), pairs)]
    ppermute x18 -> x19, waiting for transfers between devices: 20.5 us -> 24.9 us  [swap_expert(): return lax.ppermute(value, 'expert', pairs)]
    ppermute x18 -> x19, starting transfers between devices: 16.8 us -> 18.8 us  [swap_expert(): return lax.ppermute(value, 'expert', pairs)]
    ppermute x12, starting transfers between devices: 12.7 us -> 13.8 us  [swap_xy(): return lax.ppermute(value, ('dp', 'expert'), pairs)]
  transfers between devices with their start and end apart: 30 -> 31, of which waited for: 12 -> 12; matrix products, arithmetic and copies ran while one was open for 1% -> 1% of each run, Pallas kernels for 23% -> 23%
where the time goes in v6:
time: 103 us; the launch traced here: 102 us
  starting transfers between devices  32.6 us (32%)
  waiting for transfers between devices  32.3 us (31%)
  Pallas kernels  27.5 us (27%)
  local copies, waits for them, and re-layouts  8.34 us (8%)
  other arithmetic  1.51 us (1%)
    pallas_call x17, Pallas kernels, call(): pl.pallas_call(kernel, out_shape=out, in_specs=spec, out_specs=jax.tree.m...  25.7 us
    ppermute x19, waiting for transfers between devices, swap_expert(): return lax.ppermute(value, 'expert', pairs)  24.9 us
    ppermute x19, starting transfers between devices, swap_expert(): return lax.ppermute(value, 'expert', pairs)  18.8 us
    ppermute x12, starting transfers between devices, swap_xy(): return lax.ppermute(value, ('dp', 'expert'), pairs)  13.8 us
    unnamed x16, local copies, waits for them, and re-layouts  8.29 us
    ppermute x12, waiting for transfers between devices, swap_xy(): return lax.ppermute(value, ('dp', 'expert'), pairs)  7.39 us
  transfers between devices with their start and end apart: 31, of which 12 were waited for; matrix products, arithmetic and copies ran while one was open for 1% of the time, Pallas kernels for 23%

profile of v6, /device:TPU:0, one launch (start us, length us, event | category | flops | bytes accessed | tf_op | source)
XLA Modules:
  0.0 102.5 jit_solution(15370846110655824042)
XLA Ops:
  0.0 1.9 %shard_map.64 = (bf16[64,1920]{1,0:T(8,128)(2,1)}, bf16[64,1792]{1,0:T(8,128)(2,1)}) custom-call(s32[1]{0:T(128)} %bitcast.1.x_ref, bf16[64,3584]{1,0:T(8,128)(2,1)} %tokens_ref.1, s32[8,64]{1,0:T(8,128)} %bitcast.30, s32[8,64]{1,0:T(8,128)} %bitcast.31), custom_call_target="tpu_custom_call" | custom-call | flops 1 | bytes 1 | tf_op jit(solution)/shard_map/pallas_call | solution.py:135
  1.9 4.0 %collective-permute-start.2 = (bf16[64,1920]{1,0:T(8,128)(2,1)}, bf16[64,1920]{1,0:T(8,128)(2,1)}, u32[]{:S(2)}, u32[]{:S(2)}) collective-permute-start(bf16[64,1920]{1,0:T(8,128)(2,1)} %get-tuple-element.65.refs_0_), channel_id=1, source_target_pairs={{0,8},{1,9},{2,10},{3,11},{4,12},{5,13},{6,14},{7,15},{8,0},{9,1},... | collective-permute-start | bytes 737288 | tf_op jit(solution)/shard_map/m2/ppermute | solution.py:64
  5.9 1.5 %collective-permute-start.1 = (bf16[64,1920]{1,0:T(8,128)(2,1)}, bf16[64,1920]{1,0:T(8,128)(2,1)}, u32[]{:S(2)}, u32[]{:S(2)}) collective-permute-start(bf16[64,1920]{1,0:T(8,128)(2,1)} %get-tuple-element.65.refs_0_), channel_id=1, source_target_pairs={{0,2},{1,3},{2,0},{3,1},{4,6},{5,7},{6,4},{7,5},{8,10},{9,11},{10,... | collective-permute-start | bytes 737288 | tf_op jit(solution)/shard_map/m0y/ppermute | solution.py:64
  7.9 1.6 %collective-permute-start.6 = (bf16[64,1792]{1,0:T(8,128)(2,1)}, bf16[64,1792]{1,0:T(8,128)(2,1)}, u32[]{:S(2)}, u32[]{:S(2)}) collective-permute-start(bf16[64,1792]{1,0:T(8,128)(2,1)} %get-tuple-element.64.refs_1_), channel_id=1, source_target_pairs={{0,4},{1,5},{2,6},{3,7},{4,0},{5,1},{6,2},{7,3},{8,12},{9,13},{10,... | collective-permute-start | bytes 688136 | tf_op jit(solution)/shard_map/f1/ppermute | solution.py:64
  10.0 3.1 %copy-done = bf16[1,3584,1024]{2,1,0:T(8,128)(2,1)S(1)} copy-done((bf16[1,3584,1024]{2,1,0:T(8,128)(2,1)S(1)}, bf16[1,3584,1024]{2,1,0:T(8,128)(2,1)}, u32[]{:S(2)}) %copy-start) | copy-done | bytes 7340056
  13.1 3.1 %copy-done.1 = bf16[1,3584,1024]{2,1,0:T(8,128)(2,1)S(1)} copy-done((bf16[1,3584,1024]{2,1,0:T(8,128)(2,1)S(1)}, bf16[1,3584,1024]{2,1,0:T(8,128)(2,1)}, u32[]{:S(2)}) %copy-start.1) | copy-done | bytes 7340056
  16.1 2.4 %collective-permute-done.refs_3_ = bf16[64,1792]{1,0:T(8,128)(2,1)} collective-permute-done((bf16[64,1792]{1,0:T(8,128)(2,1)}, bf16[64,1792]{1,0:T(8,128)(2,1)}, u32[]{:S(2)}, u32[]{:S(2)}) %collective-permute-start) | collective-permute-done | bytes 229408 | tf_op jit(solution)/shard_map/f0y/ppermute | solution.py:64
  18.6 1.6 %collective-permute-start.5 = (bf16[64,1920]{1,0:T(8,128)(2,1)}, bf16[64,1920]{1,0:T(8,128)(2,1)S(1)}, u32[]{:S(2)}, u32[]{:S(2)}) collective-permute-start(bf16[64,1920]{1,0:T(8,128)(2,1)} %collective-permute-done.2.refs_0_), channel_id=1, source_target_pairs={{0,4},{1,5},{2,6},{3,7},{4,0},{5,1},{6,2},{7,3},{8,12},{9,13},{10,... | collective-permute-start | bytes 737288 | tf_op jit(solution)/shard_map/m3/ppermute | solution.py:64
  20.1 1.5 %collective-permute-start.4 = (bf16[64,1920]{1,0:T(8,128)(2,1)}, bf16[64,1920]{1,0:T(8,128)(2,1)S(1)}, u32[]{:S(2)}, u32[]{:S(2)}) collective-permute-start(bf16[64,1920]{1,0:T(8,128)(2,1)} %collective-permute-done.2.refs_0_), channel_id=1, source_target_pairs={{0,2},{1,17},{2,0},{3,19},{4,6},{5,21},{6,4},{7,23},{8,10},{9,25},... | collective-permute-start | bytes 737288 | tf_op jit(solution)/shard_map/r2/ppermute | solution.py:92
  21.7 1.5 %collective-permute-start.3 = (bf16[64,1920]{1,0:T(8,128)(2,1)}, bf16[64,1920]{1,0:T(8,128)(2,1)S(1)}, u32[]{:S(2)}, u32[]{:S(2)}) collective-permute-start(bf16[64,1920]{1,0:T(8,128)(2,1)} %collective-permute-done.2.refs_0_), channel_id=1, source_target_pairs={{0,16},{1,3},{2,18},{3,1},{4,20},{5,7},{6,22},{7,5},{8,24},{9,11},... | collective-permute-start | bytes 737288 | tf_op jit(solution)/shard_map/q2/ppermute | solution.py:92
  25.0 2.0 %shard_map.66 = (bf16[64,3712]{1,0:T(8,128)(2,1)S(1)}, bf16[64,3712]{1,0:T(8,128)(2,1)S(1)}, bf16[2,64,64]{2,1,0:T(8,128)(2,1)S(1)}, bf16[64,3712]{1,0:T(8,128)(2,1)S(1)}) custom-call(s32[1]{0:T(128)} %bitcast.4.me_ref, bf16[64,1920]{1,0:T(8,128)(2,1)S(1)} %copy-done.4, bf16[64,1792]{1,0:T(8,128)(2,1)S(1)} %copy-done.5, ...), custom_call_target="tpu_custom_call" | custom-call | flops 34359738368 | bytes 1 | tf_op jit(solution)/shard_map/pallas_call | solution.py:103
  29.3 1.6 %collective-permute-start.10 = (bf16[64,1920]{1,0:T(8,128)(2,1)S(1)}, bf16[64,1920]{1,0:T(8,128)(2,1)S(1)}, u32[]{:S(2)}, u32[]{:S(2)}) collective-permute-start(bf16[64,1920]{1,0:T(8,128)(2,1)S(1)} %collective-permute-done.3.refs_2_.refs_0_), channel_id=1, source_target_pairs={{0,2},{1,17},{2,0},{3,19},{4,6},{5,21},{6,4},{7,23},{8,10},{9,25},... | collective-permute-start | bytes 737288 | tf_op jit(solution)/shard_map/t2/ppermute | solution.py:92
  33.0 2.8 %shard_map.67.hidden_ref = bf16[128,1024]{1,0:T(8,128)(2,1)S(1)} custom-call(s32[2]{0:T(128)S(1)} %pad_add_fusion.scalar_ref, bf16[64,3712]{1,0:T(8,128)(2,1)S(1)} %get-tuple-element.75.keep_ref, bf16[64,3712]{1,0:T(8,128)(2,1)S(1)} %collective-permute-done.8.got_ref, bf16[1,3584,1024]{2,1,0:T(8,128)(2,1)S(1)} %bitcast.29, bf16[1,3584,1024]{2,1,0:T(8,128)(2,1)S(1)} %copy-done.2), custom_call_target="tpu_custom_call" | custom-call | flops 1 | bytes 1 | tf_op jit(solution)/shard_map/pallas_call | solution.py:103
  36.1 1.7 %shard_map.68 = (bf16[2,64,1792]{2,1,0:T(8,128)(2,1)S(1)}, bf16[2,64,1792]{2,1,0:T(8,128)(2,1)S(1)}) custom-call(s32[2]{0:T(128)S(1)} %pad_add_fusion.scalar_ref, bf16[128,1024]{1,0:T(8,128)(2,1)S(1)} %shard_map.67.hidden_ref, bf16[1,1024,3584]{2,1,0:T(8,128)(2,1)S(1)} %copy-done.3), custom_call_target="tpu_custom_call" | custom-call | flops 1 | bytes 1 | tf_op jit(solution)/shard_map/pallas_call | solution.py:103
  37.7 3.6 %collective-permute-done.9.refs_2_ = bf16[64,3712]{1,0:T(8,128)(2,1)S(1)} collective-permute-done((bf16[64,3712]{1,0:T(8,128)(2,1)S(1)}, bf16[64,3712]{1,0:T(8,128)(2,1)S(1)}, u32[]{:S(2)}, u32[]{:S(2)}) %collective-permute-start.9) | collective-permute-done | bytes 475168 | tf_op jit(solution)/shard_map/w1y/ppermute | solution.py:64
  41.4 1.9 %shard_map.69 = (bf16[128,1920]{1,0:T(8,128)(2,1)S(1)}, bf16[128,1920]{1,0:T(8,128)(2,1)S(1)}, bf16[4,64,64]{2,1,0:T(8,128)(2,1)S(1)}) custom-call(s32[1]{0:T(128)} %bitcast.5.me_ref, bf16[64,1920]{1,0:T(8,128)(2,1)} %collective-permute-done.2.refs_0_, bf16[64,1920]{1,0:T(8,128)(2,1)S(1)} %collective-permute-done.4.refs_1_, ...), custom_call_target="tpu_custom_call" | custom-call | flops 34359738368 | bytes 1 | tf_op jit(solution)/shard_map/pallas_call | solution.py:103
  43.9 1.7 %shard_map.70 = (bf16[64,3712]{1,0:T(8,128)(2,1)S(1)}, bf16[64,3712]{1,0:T(8,128)(2,1)S(1)}, bf16[2,64,64]{2,1,0:T(8,128)(2,1)S(1)}) custom-call(s32[1]{0:T(128)} %bitcast.6.me_ref, bf16[64,1920]{1,0:T(8,128)(2,1)S(1)} %collective-permute-done.7.refs_0_, bf16[64,1792]{1,0:T(8,128)(2,1)} %collective-permute-done.6.refs_1_, ...), custom_call_target="tpu_custom_call" | custom-call | flops 1 | bytes 1 | tf_op jit(solution)/shard_map/pallas_call | solution.py:103
  46.9 2.7 %shard_map.71 = (f32[256,1024]{1,0:T(8,128)S(1)}, f32[256,1024]{1,0:T(8,128)S(1)}) custom-call(s32[2]{0:T(128)S(1)} %pad_add_fusion.scalar_ref, bf16[128,1920]{1,0:T(8,128)(2,1)S(1)} %get-tuple-element.84.keep_ref.refs_2_, bf16[128,1920]{1,0:T(8,128)(2,1)S(1)} %collective-permute-done.13.got_ref.refs_3_, bf16[1,3584,1024]{2,1,0:T(8,128)(2,1)S(1)} %bitcast.29, ...), custom_call_target="tpu_custom_call" | custom-call | flops 1 | bytes 1 | tf_op jit(solution)/shard_map/pallas_call | solution.py:103
  50.2 2.8 %shard_map.73.hidden_ref = bf16[128,1024]{1,0:T(8,128)(2,1)S(1)} custom-call(s32[2]{0:T(128)S(1)} %pad_add_fusion.scalar_ref, bf16[64,3712]{1,0:T(8,128)(2,1)S(1)} %get-tuple-element.87.keep_ref, bf16[64,3712]{1,0:T(8,128)(2,1)S(1)} %collective-permute-done.15.got_ref, bf16[1,3584,1024]{2,1,0:T(8,128)(2,1)S(1)} %bitcast.29, bf16[1,3584,1024]{2,1,0:T(8,128)(2,1)S(1)} %copy-done.2), custom_call_target="tpu_custom_call" | custom-call | flops 1 | bytes 1 | tf_op jit(solution)/shard_map/pallas_call | solution.py:103
  53.0 1.7 %shard_map.74 = (bf16[2,64,1792]{2,1,0:T(8,128)(2,1)S(1)}, bf16[2,64,1792]{2,1,0:T(8,128)(2,1)S(1)}) custom-call(s32[2]{0:T(128)S(1)} %pad_add_fusion.scalar_ref, bf16[128,1024]{1,0:T(8,128)(2,1)S(1)} %shard_map.73.hidden_ref, bf16[1,1024,3584]{2,1,0:T(8,128)(2,1)S(1)} %copy-done.3), custom_call_target="tpu_custom_call" | custom-call | flops 1 | bytes 1 | tf_op jit(solution)/shard_map/pallas_call | solution.py:103
  55.3 3.0 %shard_map.75.hidden_ref = bf16[256,1024]{1,0:T(8,128)(2,1)S(1)} custom-call(s32[2]{0:T(128)S(1)} %pad_add_fusion.scalar_ref, bf16[128,1792]{1,0:T(8,128)(2,1)S(1)} %get-tuple-element.92.keep_ref, bf16[128,1792]{1,0:T(8,128)(2,1)S(1)} %collective-permute-done.16.got_ref, bf16[1,3584,1024]{2,1,0:T(8,128)(2,1)S(1)} %bitcast.29, ...), custom_call_target="tpu_custom_call" | custom-call | flops 1 | bytes 1 | tf_op jit(solution)/shard_map/pallas_call | solution.py:103
  58.2 1.7 %shard_map.76 = (bf16[2,64,1792]{2,1,0:T(8,128)(2,1)S(1)}, bf16[2,64,1792]{2,1,0:T(8,128)(2,1)S(1)}) custom-call(s32[2]{0:T(128)S(1)} %pad_add_fusion.scalar_ref, bf16[256,1024]{1,0:T(8,128)(2,1)S(1)} %shard_map.75.hidden_ref, bf16[1,1024,3584]{2,1,0:T(8,128)(2,1)S(1)} %copy-done.3, f32[16,128]{1,0:T(8,128)S(1)} %shard_map.65.refs_0_), custom_call_target="tpu_custom_call" | custom-call | flops 1 | bytes 1 | tf_op jit(solution)/shard_map/pallas_call | solution.py:103
  60.4 1.7 %shard_map.78 = (bf16[2,64,1792]{2,1,0:T(8,128)(2,1)S(1)}, bf16[2,64,1792]{2,1,0:T(8,128)(2,1)S(1)}) custom-call(s32[2]{0:T(128)S(1)} %pad_add_fusion.scalar_ref, bf16[256,1024]{1,0:T(8,128)(2,1)S(1)} %shard_map.75.hidden_ref, bf16[1,1024,3584]{2,1,0:T(8,128)(2,1)S(1)} %copy-done.3), custom_call_target="tpu_custom_call" | custom-call | flops 1 | bytes 1 | tf_op jit(solution)/shard_map/pallas_call | solution.py:103
  63.6 1.5 %collective-permute-start.22 = (bf16[2,64,1792]{2,1,0:T(8,128)(2,1)S(1)}, bf16[2,64,1792]{2,1,0:T(8,128)(2,1)S(1)}, u32[]{:S(2)}, u32[]{:S(2)}) collective-permute-start(bf16[2,64,1792]{2,1,0:T(8,128)(2,1)S(1)} %get-tuple-element.114), channel_id=1, source_target_pairs={{0,16},{1,3},{2,18},{3,1},{4,20},{5,7},{6,22},{7,5},{8,24},{9,11},... | collective-permute-start | bytes 1376264 | tf_op jit(solution)/shard_map/u3/ppermute | solution.py:92
  65.1 1.6 %collective-permute-start.21 = (bf16[2,64,1792]{2,1,0:T(8,128)(2,1)S(1)}, bf16[2,64,1792]{2,1,0:T(8,128)(2,1)S(1)}, u32[]{:S(2)}, u32[]{:S(2)}) collective-permute-start(bf16[2,64,1792]{2,1,0:T(8,128)(2,1)S(1)} %get-tuple-element.102), channel_id=1, source_target_pairs={{0,4},{1,5},{2,6},{3,7},{4,0},{5,1},{6,2},{7,3},{8,12},{9,13},{10,... | collective-permute-start | bytes 1376264 | tf_op jit(solution)/shard_map/nk/ppermute | solution.py:64
  68.1 8.0 %collective-permute-done.23 = bf16[2,64,1792]{2,1,0:T(8,128)(2,1)S(1)} collective-permute-done((bf16[2,64,1792]{2,1,0:T(8,128)(2,1)S(1)}, bf16[2,64,1792]{2,1,0:T(8,128)(2,1)S(1)}, u32[]{:S(2)}, u32[]{:S(2)}) %collective-permute-start.23) | collective-permute-done | bytes 458784 | tf_op jit(solution)/shard_map/ng/ppermute | solution.py:64
  79.3 3.9 %collective-permute-done.24 = bf16[64,1792]{1,0:T(8,128)(2,1)S(1)} collective-permute-done((bf16[64,1792]{1,0:T(8,128)(2,1)S(1)}, bf16[64,1792]{1,0:T(8,128)(2,1)S(1)}, u32[]{:S(2)}, u32[]{:S(2)}) %collective-permute-start.24) | collective-permute-done | bytes 229408 | tf_op jit(solution)/shard_map/v3/ppermute | solution.py:92
  83.3 1.6 %collective-permute-start.29 = (bf16[64,1792]{1,0:T(8,128)(2,1)S(1)}, bf16[64,1792]{1,0:T(8,128)(2,1)S(1)}, u32[]{:S(2)}, u32[]{:S(2)}) collective-permute-start(bf16[64,1792]{1,0:T(8,128)(2,1)S(1)} %fusion.4), channel_id=1, source_target_pairs={{0,4},{1,5},{2,6},{3,7},{4,0},{5,1},{6,2},{7,3},{8,12},{9,13},{10,... | collective-permute-start | bytes 688136 | tf_op jit(solution)/shard_map/s3/ppermute | solution.py:64
  87.4 3.0 %collective-permute-done.29 = bf16[64,1792]{1,0:T(8,128)(2,1)S(1)} collective-permute-done((bf16[64,1792]{1,0:T(8,128)(2,1)S(1)}, bf16[64,1792]{1,0:T(8,128)(2,1)S(1)}, u32[]{:S(2)}, u32[]{:S(2)}) %collective-permute-start.29) | collective-permute-done | bytes 229408 | tf_op jit(solution)/shard_map/s3/ppermute | solution.py:64
  90.5 2.4 %collective-permute-start.30 = (bf16[64,1792]{1,0:T(8,128)(2,1)S(1)}, bf16[64,1792]{1,0:T(8,128)(2,1)S(1)}, u32[]{:S(2)}, u32[]{:S(2)}) collective-permute-start(bf16[64,1792]{1,0:T(8,128)(2,1)S(1)} %fusion.1), channel_id=1, source_target_pairs={{0,8},{1,9},{2,10},{3,11},{4,12},{5,13},{6,14},{7,15},{8,0},{9,1},... | collective-permute-start | bytes 688136 | tf_op jit(solution)/shard_map/s2/ppermute | solution.py:64
  92.8 1.5 %collective-permute-done.26 = bf16[2,64,1792]{2,1,0:T(8,128)(2,1)S(1)} collective-permute-done((bf16[2,64,1792]{2,1,0:T(8,128)(2,1)S(1)}, bf16[2,64,1792]{2,1,0:T(8,128)(2,1)S(1)}, u32[]{:S(2)}, u32[]{:S(2)}) %collective-permute-start.26) | collective-permute-done | bytes 458784 | tf_op jit(solution)/shard_map/u0/ppermute | solution.py:92
  95.4 6.3 %collective-permute-done.30 = bf16[64,1792]{1,0:T(8,128)(2,1)S(1)} collective-permute-done((bf16[64,1792]{1,0:T(8,128)(2,1)S(1)}, bf16[64,1792]{1,0:T(8,128)(2,1)S(1)}, u32[]{:S(2)}, u32[]{:S(2)}) %collective-permute-start.30) | collective-permute-done | bytes 229408 | tf_op jit(solution)/shard_map/s2/ppermute | solution.py:64
  (76 shorter events, 21.4 us)
Async XLA Ops:
  1.9 16.7 %collective-permute-start.2 = (bf16[64,1920]{1,0:T(8,128)(2,1)}, bf16[64,1920]{1,0:T(8,128)(2,1)}, u32[]{:S(2)}, u32[]{:S(2)}) collective-permute-start(bf16[64,1920]{1,0:T(8,128)(2,1)} %get-tuple-element.65.refs_0_), channel_id=1, source_target_pairs={{0,8},{1,9},{2,10},{3,11},{4,12},{5,13},{6,14},{7,15},{8,0},{9,1},... | collective-permute-start | bytes 737288 | tf_op jit(solution)/shard_map/m2/ppermute | solution.py:64
  5.9 12.7 %collective-permute-start.1 = (bf16[64,1920]{1,0:T(8,128)(2,1)}, bf16[64,1920]{1,0:T(8,128)(2,1)}, u32[]{:S(2)}, u32[]{:S(2)}) collective-permute-start(bf16[64,1920]{1,0:T(8,128)(2,1)} %get-tuple-element.65.refs_0_), channel_id=1, source_target_pairs={{0,2},{1,3},{2,0},{3,1},{4,6},{5,7},{6,4},{7,5},{8,10},{9,11},{10,... | collective-permute-start | bytes 737288 | tf_op jit(solution)/shard_map/m0y/ppermute | solution.py:64
  7.4 11.1 %collective-permute-start = (bf16[64,1792]{1,0:T(8,128)(2,1)}, bf16[64,1792]{1,0:T(8,128)(2,1)}, u32[]{:S(2)}, u32[]{:S(2)}) collective-permute-start(bf16[64,1792]{1,0:T(8,128)(2,1)} %get-tuple-element.64.refs_1_), channel_id=1, source_target_pairs={{0,2},{1,3},{2,0},{3,1},{4,6},{5,7},{6,4},{7,5},{8,10},{9,11},{10,... | collective-permute-start | bytes 688136 | tf_op jit(solution)/shard_map/f0y/ppermute | solution.py:64
  7.9 19.1 %collective-permute-start.6 = (bf16[64,1792]{1,0:T(8,128)(2,1)}, bf16[64,1792]{1,0:T(8,128)(2,1)}, u32[]{:S(2)}, u32[]{:S(2)}) collective-permute-start(bf16[64,1792]{1,0:T(8,128)(2,1)} %get-tuple-element.64.refs_1_), channel_id=1, source_target_pairs={{0,4},{1,5},{2,6},{3,7},{4,0},{5,1},{6,2},{7,3},{8,12},{9,13},{10,... | collective-permute-start | bytes 688136 | tf_op jit(solution)/shard_map/f1/ppermute | solution.py:64
  9.5 17.6 %collective-permute-start.7 = (bf16[64,1920]{1,0:T(8,128)(2,1)}, bf16[64,1920]{1,0:T(8,128)(2,1)S(1)}, u32[]{:S(2)}, u32[]{:S(2)}) collective-permute-start(bf16[64,1920]{1,0:T(8,128)(2,1)} %get-tuple-element.65.refs_0_), channel_id=1, source_target_pairs={{0,4},{1,5},{2,6},{3,7},{4,0},{5,1},{6,2},{7,3},{8,12},{9,13},{10,... | collective-permute-start | bytes 737288 | tf_op jit(solution)/shard_map/m1/ppermute | solution.py:64
  16.1 16.8 %slice-start = ((s8[7340032]{0:T(1024)(128)(4,1)}), s8[3145728]{0:T(1024)(128)(4,1)S(1)}, s32[]{:S(2)}) async-start(s8[7340032]{0:T(1024)(128)(4,1)} %bitcast.28), calls=%async_computation | async-start | bytes 6291456
  18.6 10.7 %collective-permute-start.5 = (bf16[64,1920]{1,0:T(8,128)(2,1)}, bf16[64,1920]{1,0:T(8,128)(2,1)S(1)}, u32[]{:S(2)}, u32[]{:S(2)}) collective-permute-start(bf16[64,1920]{1,0:T(8,128)(2,1)} %collective-permute-done.2.refs_0_), channel_id=1, source_target_pairs={{0,4},{1,5},{2,6},{3,7},{4,0},{5,1},{6,2},{7,3},{8,12},{9,13},{10,... | collective-permute-start | bytes 737288 | tf_op jit(solution)/shard_map/m3/ppermute | solution.py:64
  20.1 9.1 %collective-permute-start.4 = (bf16[64,1920]{1,0:T(8,128)(2,1)}, bf16[64,1920]{1,0:T(8,128)(2,1)S(1)}, u32[]{:S(2)}, u32[]{:S(2)}) collective-permute-start(bf16[64,1920]{1,0:T(8,128)(2,1)} %collective-permute-done.2.refs_0_), channel_id=1, source_target_pairs={{0,2},{1,17},{2,0},{3,19},{4,6},{5,21},{6,4},{7,23},{8,10},{9,25},... | collective-permute-start | bytes 737288 | tf_op jit(solution)/shard_map/r2/ppermute | solution.py:92
  21.7 6.4 %collective-permute-start.3 = (bf16[64,1920]{1,0:T(8,128)(2,1)}, bf16[64,1920]{1,0:T(8,128)(2,1)S(1)}, u32[]{:S(2)}, u32[]{:S(2)}) collective-permute-start(bf16[64,1920]{1,0:T(8,128)(2,1)} %collective-permute-done.2.refs_0_), channel_id=1, source_target_pairs={{0,16},{1,3},{2,18},{3,1},{4,20},{5,7},{6,22},{7,5},{8,24},{9,11},... | collective-permute-start | bytes 737288 | tf_op jit(solution)/shard_map/q2/ppermute | solution.py:92
  28.1 4.9 %collective-permute-start.8 = (bf16[64,3712]{1,0:T(8,128)(2,1)S(1)}, bf16[64,3712]{1,0:T(8,128)(2,1)S(1)}, u32[]{:S(2)}, u32[]{:S(2)}) collective-permute-start(bf16[64,3712]{1,0:T(8,128)(2,1)S(1)} %get-tuple-element.77), channel_id=1, source_target_pairs={{0,1},{1,0},{2,3},{3,2},{4,5},{5,4},{6,7},{7,6},{8,9},{9,8},{10,11... | collective-permute-start | bytes 1425416 | tf_op jit(solution)/shard_map/rows_0/ppermute | solution.py:64
  28.1 13.3 %collective-permute-start.9 = (bf16[64,3712]{1,0:T(8,128)(2,1)S(1)}, bf16[64,3712]{1,0:T(8,128)(2,1)S(1)}, u32[]{:S(2)}, u32[]{:S(2)}) collective-permute-start(bf16[64,3712]{1,0:T(8,128)(2,1)S(1)} %get-tuple-element.79), channel_id=1, source_target_pairs={{0,4},{1,5},{2,6},{3,7},{4,0},{5,1},{6,2},{7,3},{8,12},{9,13},{10,... | collective-permute-start | bytes 1425416 | tf_op jit(solution)/shard_map/w1y/ppermute | solution.py:64
  29.3 12.1 %collective-permute-start.10 = (bf16[64,1920]{1,0:T(8,128)(2,1)S(1)}, bf16[64,1920]{1,0:T(8,128)(2,1)S(1)}, u32[]{:S(2)}, u32[]{:S(2)}) collective-permute-start(bf16[64,1920]{1,0:T(8,128)(2,1)S(1)} %collective-permute-done.3.refs_2_.refs_0_), channel_id=1, source_target_pairs={{0,2},{1,17},{2,0},{3,19},{4,6},{5,21},{6,4},{7,23},{8,10},{9,25},... | collective-permute-start | bytes 737288 | tf_op jit(solution)/shard_map/t2/ppermute | solution.py:92
  30.9 10.5 %collective-permute-start.12 = (bf16[64,1920]{1,0:T(8,128)(2,1)S(1)}, bf16[64,1920]{1,0:T(8,128)(2,1)S(1)}, u32[]{:S(2)}, u32[]{:S(2)}) collective-permute-start(bf16[64,1920]{1,0:T(8,128)(2,1)S(1)} %collective-permute-done.5.refs_3_), channel_id=1, source_target_pairs={{0,16},{1,3},{2,18},{3,1},{4,20},{5,7},{6,22},{7,5},{8,24},{9,11},... | collective-permute-start | bytes 737288 | tf_op jit(solution)/shard_map/q3/ppermute | solution.py:92
  32.4 9.0 %collective-permute-start.11 = (bf16[64,1920]{1,0:T(8,128)(2,1)S(1)}, bf16[64,1920]{1,0:T(8,128)(2,1)S(1)}, u32[]{:S(2)}, u32[]{:S(2)}) collective-permute-start(bf16[64,1920]{1,0:T(8,128)(2,1)S(1)} %collective-permute-done.5.refs_3_), channel_id=1, source_target_pairs={{0,2},{1,17},{2,0},{3,19},{4,6},{5,21},{6,4},{7,23},{8,10},{9,25},... | collective-permute-start | bytes 737288 | tf_op jit(solution)/shard_map/r3/ppermute | solution.py:92
  43.3 3.6 %collective-permute-start.13 = (bf16[128,1920]{1,0:T(8,128)(2,1)S(1)}, bf16[128,1920]{1,0:T(8,128)(2,1)S(1)}, u32[]{:S(2)}, u32[]{:S(2)}) collective-permute-start(bf16[128,1920]{1,0:T(8,128)(2,1)S(1)} %get-tuple-element.89), channel_id=1, source_target_pairs={{0,1},{1,0},{2,3},{3,2},{4,5},{5,4},{6,7},{7,6},{8,9},{9,8},{10,11... | collective-permute-start | bytes 1474568 | tf_op jit(solution)/shard_map/rows_m/ppermute | solution.py:64
  43.4 6.3 %collective-permute-start.14 = (bf16[64,1920]{1,0:T(8,128)(2,1)S(1)}, bf16[64,1920]{1,0:T(8,128)(2,1)S(1)}, u32[]{:S(2)}, u32[]{:S(2)}) collective-permute-start(bf16[64,1920]{1,0:T(8,128)(2,1)S(1)} %collective-permute-done.12.refs_5_.refs_3_), channel_id=1, source_target_pairs={{0,2},{1,17},{2,0},{3,19},{4,6},{5,21},{6,4},{7,23},{8,10},{9,25},... | collective-permute-start | bytes 737288 | tf_op jit(solution)/shard_map/t3/ppermute | solution.py:92
  45.7 4.5 %collective-permute-start.15 = (bf16[64,3712]{1,0:T(8,128)(2,1)S(1)}, bf16[64,3712]{1,0:T(8,128)(2,1)S(1)}, u32[]{:S(2)}, u32[]{:S(2)}) collective-permute-start(bf16[64,3712]{1,0:T(8,128)(2,1)S(1)} %get-tuple-element.94), channel_id=1, source_target_pairs={{0,1},{1,0},{2,3},{3,2},{4,5},{5,4},{6,7},{7,6},{8,9},{9,8},{10,11... | collective-permute-start | bytes 1425416 | tf_op jit(solution)/shard_map/rows_1/ppermute | solution.py:64
  50.1 5.2 %collective-permute-start.16 = (bf16[128,1792]{1,0:T(8,128)(2,1)S(1)}, bf16[128,1792]{1,0:T(8,128)(2,1)S(1)}, u32[]{:S(2)}, u32[]{:S(2)}) collective-permute-start(bf16[128,1792]{1,0:T(8,128)(2,1)S(1)} %get-tuple-element.97), channel_id=1, source_target_pairs={{0,1},{1,0},{2,3},{3,2},{4,5},{5,4},{6,7},{7,6},{8,9},{9,8},{10,11... | collective-permute-start | bytes 1376264 | tf_op jit(solution)/shard_map/rows_f/ppermute | solution.py:64
  54.7 5.3 %collective-permute-start.17 = (bf16[2,64,1792]{2,1,0:T(8,128)(2,1)S(1)}, bf16[2,64,1792]{2,1,0:T(8,128)(2,1)S(1)}, u32[]{:S(2)}, u32[]{:S(2)}) collective-permute-start(bf16[2,64,1792]{2,1,0:T(8,128)(2,1)S(1)} %get-tuple-element.101), channel_id=1, source_target_pairs={{0,1},{1,0},{2,3},{3,2},{4,5},{5,4},{6,7},{7,6},{8,9},{9,8},{10,11... | collective-permute-start | bytes 1376264 | tf_op jit(solution)/shard_map/back_1/ppermute | solution.py:64
  59.9 3.3 %collective-permute-start.18 = (bf16[2,64,1792]{2,1,0:T(8,128)(2,1)S(1)}, bf16[2,64,1792]{2,1,0:T(8,128)(2,1)S(1)}, u32[]{:S(2)}, u32[]{:S(2)}) collective-permute-start(bf16[2,64,1792]{2,1,0:T(8,128)(2,1)S(1)} %get-tuple-element.106), channel_id=1, source_target_pairs={{0,1},{1,0},{2,3},{3,2},{4,5},{5,4},{6,7},{7,6},{8,9},{9,8},{10,11... | collective-permute-start | bytes 1376264 | tf_op jit(solution)/shard_map/back_3/ppermute | solution.py:64
  62.1 4.6 %collective-permute-start.19 = (bf16[2,64,1792]{2,1,0:T(8,128)(2,1)S(1)}, bf16[2,64,1792]{2,1,0:T(8,128)(2,1)S(1)}, u32[]{:S(2)}, u32[]{:S(2)}) collective-permute-start(bf16[2,64,1792]{2,1,0:T(8,128)(2,1)S(1)} %get-tuple-element.109), channel_id=1, source_target_pairs={{0,1},{1,0},{2,3},{3,2},{4,5},{5,4},{6,7},{7,6},{8,9},{9,8},{10,11... | collective-permute-start | bytes 1376264 | tf_op jit(solution)/shard_map/back_2/ppermute | solution.py:64
  62.7 5.1 %collective-permute-start.20 = (bf16[2,64,1792]{2,1,0:T(8,128)(2,1)S(1)}, bf16[2,64,1792]{2,1,0:T(8,128)(2,1)S(1)}, u32[]{:S(2)}, u32[]{:S(2)}) collective-permute-start(bf16[2,64,1792]{2,1,0:T(8,128)(2,1)S(1)} %get-tuple-element.112), channel_id=1, source_target_pairs={{0,1},{1,0},{2,3},{3,2},{4,5},{5,4},{6,7},{7,6},{8,9},{9,8},{10,11... | collective-permute-start | bytes 1376264 | tf_op jit(solution)/shard_map/back_0/ppermute | solution.py:64
  62.7 13.3 %collective-permute-start.23 = (bf16[2,64,1792]{2,1,0:T(8,128)(2,1)S(1)}, bf16[2,64,1792]{2,1,0:T(8,128)(2,1)S(1)}, u32[]{:S(2)}, u32[]{:S(2)}) collective-permute-start(bf16[2,64,1792]{2,1,0:T(8,128)(2,1)S(1)} %get-tuple-element.115), channel_id=1, source_target_pairs={{0,4},{1,5},{2,6},{3,7},{4,0},{5,1},{6,2},{7,3},{8,12},{9,13},{10,... | collective-permute-start | bytes 1376264 | tf_op jit(solution)/shard_map/ng/ppermute | solution.py:64
  63.6 12.5 %collective-permute-start.22 = (bf16[2,64,1792]{2,1,0:T(8,128)(2,1)S(1)}, bf16[2,64,1792]{2,1,0:T(8,128)(2,1)S(1)}, u32[]{:S(2)}, u32[]{:S(2)}) collective-permute-start(bf16[2,64,1792]{2,1,0:T(8,128)(2,1)S(1)} %get-tuple-element.114), channel_id=1, source_target_pairs={{0,16},{1,3},{2,18},{3,1},{4,20},{5,7},{6,22},{7,5},{8,24},{9,11},... | collective-permute-start | bytes 1376264 | tf_op jit(solution)/shard_map/u3/ppermute | solution.py:92
  65.1 20.8 %collective-permute-start.21 = (bf16[2,64,1792]{2,1,0:T(8,128)(2,1)S(1)}, bf16[2,64,1792]{2,1,0:T(8,128)(2,1)S(1)}, u32[]{:S(2)}, u32[]{:S(2)}) collective-permute-start(bf16[2,64,1792]{2,1,0:T(8,128)(2,1)S(1)} %get-tuple-element.102), channel_id=1, source_target_pairs={{0,4},{1,5},{2,6},{3,7},{4,0},{5,1},{6,2},{7,3},{8,12},{9,13},{10,... | collective-permute-start | bytes 1376264 | tf_op jit(solution)/shard_map/nk/ppermute | solution.py:64
  67.1 10.0 %collective-permute-start.25 = (bf16[2,64,1792]{2,1,0:T(8,128)(2,1)S(1)}, bf16[2,64,1792]{2,1,0:T(8,128)(2,1)S(1)}, u32[]{:S(2)}, u32[]{:S(2)}) collective-permute-start(bf16[2,64,1792]{2,1,0:T(8,128)(2,1)S(1)} %get-tuple-element.117), channel_id=1, source_target_pairs={{0,16},{1,3},{2,18},{3,1},{4,20},{5,7},{6,22},{7,5},{8,24},{9,11},... | collective-permute-start | bytes 1376264 | tf_op jit(solution)/shard_map/u2/ppermute | solution.py:92
  77.2 6.1 %collective-permute-start.24 = (bf16[64,1792]{1,0:T(8,128)(2,1)S(1)}, bf16[64,1792]{1,0:T(8,128)(2,1)S(1)}, u32[]{:S(2)}, u32[]{:S(2)}) collective-permute-start(bf16[64,1792]{1,0:T(8,128)(2,1)S(1)} %slice_bitcast_fusion.4), channel_id=1, source_target_pairs={{0,2},{1,17},{2,0},{3,19},{4,6},{5,21},{6,4},{7,23},{8,10},{9,25},... | collective-permute-start | bytes 688136 | tf_op jit(solution)/shard_map/v3/ppermute | solution.py:92
  78.0 9.4 %collective-permute-start.28 = (bf16[64,1792]{1,0:T(8,128)(2,1)S(1)}, bf16[64,1792]{1,0:T(8,128)(2,1)S(1)}, u32[]{:S(2)}, u32[]{:S(2)}) collective-permute-start(bf16[64,1792]{1,0:T(8,128)(2,1)S(1)} %slice_bitcast_fusion), channel_id=1, source_target_pairs={{0,2},{1,17},{2,0},{3,19},{4,6},{5,21},{6,4},{7,23},{8,10},{9,25},... | collective-permute-start | bytes 688136 | tf_op jit(solution)/shard_map/v2/ppermute | solution.py:92
  83.3 7.1 %collective-permute-start.29 = (bf16[64,1792]{1,0:T(8,128)(2,1)S(1)}, bf16[64,1792]{1,0:T(8,128)(2,1)S(1)}, u32[]{:S(2)}, u32[]{:S(2)}) collective-permute-start(bf16[64,1792]{1,0:T(8,128)(2,1)S(1)} %fusion.4), channel_id=1, source_target_pairs={{0,4},{1,5},{2,6},{3,7},{4,0},{5,1},{6,2},{7,3},{8,12},{9,13},{10,... | collective-permute-start | bytes 688136 | tf_op jit(solution)/shard_map/s3/ppermute | solution.py:64
  85.9 8.5 %collective-permute-start.26 = (bf16[2,64,1792]{2,1,0:T(8,128)(2,1)S(1)}, bf16[2,64,1792]{2,1,0:T(8,128)(2,1)S(1)}, u32[]{:S(2)}, u32[]{:S(2)}) collective-permute-start(bf16[2,64,1792]{2,1,0:T(8,128)(2,1)S(1)} %add_convert_fusion.1), channel_id=1, source_target_pairs={{0,16},{1,3},{2,18},{3,1},{4,20},{5,7},{6,22},{7,5},{8,24},{9,11},... | collective-permute-start | bytes 1376264 | tf_op jit(solution)/shard_map/u0/ppermute | solution.py:92
  90.5 11.2 %collective-permute-start.30 = (bf16[64,1792]{1,0:T(8,128)(2,1)S(1)}, bf16[64,1792]{1,0:T(8,128)(2,1)S(1)}, u32[]{:S(2)}, u32[]{:S(2)}) collective-permute-start(bf16[64,1792]{1,0:T(8,128)(2,1)S(1)} %fusion.1), channel_id=1, source_target_pairs={{0,8},{1,9},{2,10},{3,11},{4,12},{5,13},{6,14},{7,15},{8,0},{9,1},... | collective-permute-start | bytes 688136 | tf_op jit(solution)/shard_map/s2/ppermute | solution.py:64
  94.6 7.1 %collective-permute-start.27 = (bf16[64,1792]{1,0:T(8,128)(2,1)S(1)}, bf16[64,1792]{1,0:T(8,128)(2,1)S(1)}, u32[]{:S(2)}, u32[]{:S(2)}) collective-permute-start(bf16[64,1792]{1,0:T(8,128)(2,1)S(1)} %slice_bitcast_fusion.2), channel_id=1, source_target_pairs={{0,2},{1,17},{2,0},{3,19},{4,6},{5,21},{6,4},{7,23},{8,10},{9,25},... | collective-permute-start | bytes 688136 | tf_op jit(solution)/shard_map/v0/ppermute | solution.py:92
  (7 other events, 27.0 us)

commit v7 on v6

--- a/solution.py
+++ b/solution.py
@@ -409,7 +409,7 @@
     nk = swap_z(keep_1, 1, "nk")
     u3 = swap_xy(give_3, True, "u3")
     ng = swap_z(give_1, 1, "ng")
-    u3 = add(keep_3, after(u3, keep_2, ng))
+    u3 = add(keep_3, after(u3, ng))
     v3 = swap_xy(u3[1], False, "v3")
     u2 = swap_xy(give_2, True, "u2")
     u2 = add(keep_2, after(u2, u3))

time: 103 us -> 103 us (level)
  no operation moved by 1% of the time
where the time goes in v7:
time: 103 us; the launch traced here: 102 us
  starting transfers between devices  32.6 us (32%)
  waiting for transfers between devices  32.3 us (31%)
  Pallas kernels  27.5 us (27%)
  local copies, waits for them, and re-layouts  8.34 us (8%)
  other arithmetic  1.51 us (1%)
    pallas_call x17, Pallas kernels, call(): pl.pallas_call(kernel, out_shape=out, in_specs=spec, out_specs=jax.tree.m...  25.7 us
    ppermute x19, waiting for transfers between devices, swap_expert(): return lax.ppermute(value, 'expert', pairs)  24.9 us
    ppermute x19, starting transfers between devices, swap_expert(): return lax.ppermute(value, 'expert', pairs)  18.8 us
    ppermute x12, starting transfers between devices, swap_xy(): return lax.ppermute(value, ('dp', 'expert'), pairs)  13.8 us
    unnamed x16, local copies, waits for them, and re-layouts  8.29 us
    ppermute x12, waiting for transfers between devices, swap_xy(): return lax.ppermute(value, ('dp', 'expert'), pairs)  7.39 us
  transfers between devices with their start and end apart: 31, of which 12 were waited for; matrix products, arithmetic and copies ran while one was open for 1% of the time, Pallas kernels for 23%

profile of v7, /device:TPU:0, one launch (start us, length us, event | category | flops | bytes accessed | tf_op | source)
XLA Modules:
  0.0 102.5 jit_solution(15370846110655824042)
XLA Ops:
  0.0 1.9 %shard_map.64 = (bf16[64,1920]{1,0:T(8,128)(2,1)}, bf16[64,1792]{1,0:T(8,128)(2,1)}) custom-call(s32[1]{0:T(128)} %bitcast.1.x_ref, bf16[64,3584]{1,0:T(8,128)(2,1)} %tokens_ref.1, s32[8,64]{1,0:T(8,128)} %bitcast.30, s32[8,64]{1,0:T(8,128)} %bitcast.31), custom_call_target="tpu_custom_call" | custom-call | flops 1 | bytes 1 | tf_op jit(solution)/shard_map/pallas_call | solution.py:135
  1.9 4.0 %collective-permute-start.2 = (bf16[64,1920]{1,0:T(8,128)(2,1)}, bf16[64,1920]{1,0:T(8,128)(2,1)}, u32[]{:S(2)}, u32[]{:S(2)}) collective-permute-start(bf16[64,1920]{1,0:T(8,128)(2,1)} %get-tuple-element.65.refs_0_), channel_id=1, source_target_pairs={{0,8},{1,9},{2,10},{3,11},{4,12},{5,13},{6,14},{7,15},{8,0},{9,1},... | collective-permute-start | bytes 737288 | tf_op jit(solution)/shard_map/m2/ppermute | solution.py:64
  5.9 1.5 %collective-permute-start.1 = (bf16[64,1920]{1,0:T(8,128)(2,1)}, bf16[64,1920]{1,0:T(8,128)(2,1)}, u32[]{:S(2)}, u32[]{:S(2)}) collective-permute-start(bf16[64,1920]{1,0:T(8,128)(2,1)} %get-tuple-element.65.refs_0_), channel_id=1, source_target_pairs={{0,2},{1,3},{2,0},{3,1},{4,6},{5,7},{6,4},{7,5},{8,10},{9,11},{10,... | collective-permute-start | bytes 737288 | tf_op jit(solution)/shard_map/m0y/ppermute | solution.py:64
  7.9 1.6 %collective-permute-start.6 = (bf16[64,1792]{1,0:T(8,128)(2,1)}, bf16[64,1792]{1,0:T(8,128)(2,1)}, u32[]{:S(2)}, u32[]{:S(2)}) collective-permute-start(bf16[64,1792]{1,0:T(8,128)(2,1)} %get-tuple-element.64.refs_1_), channel_id=1, source_target_pairs={{0,4},{1,5},{2,6},{3,7},{4,0},{5,1},{6,2},{7,3},{8,12},{9,13},{10,... | collective-permute-start | bytes 688136 | tf_op jit(solution)/shard_map/f1/ppermute | solution.py:64
  10.0 3.1 %copy-done = bf16[1,3584,1024]{2,1,0:T(8,128)(2,1)S(1)} copy-done((bf16[1,3584,1024]{2,1,0:T(8,128)(2,1)S(1)}, bf16[1,3584,1024]{2,1,0:T(8,128)(2,1)}, u32[]{:S(2)}) %copy-start) | copy-done | bytes 7340056
  13.1 3.1 %copy-done.1 = bf16[1,3584,1024]{2,1,0:T(8,128)(2,1)S(1)} copy-done((bf16[1,3584,1024]{2,1,0:T(8,128)(2,1)S(1)}, bf16[1,3584,1024]{2,1,0:T(8,128)(2,1)}, u32[]{:S(2)}) %copy-start.1) | copy-done | bytes 7340056
  16.1 2.4 %collective-permute-done.refs_3_ = bf16[64,1792]{1,0:T(8,128)(2,1)} collective-permute-done((bf16[64,1792]{1,0:T(8,128)(2,1)}, bf16[64,1792]{1,0:T(8,128)(2,1)}, u32[]{:S(2)}, u32[]{:S(2)}) %collective-permute-start) | collective-permute-done | bytes 229408 | tf_op jit(solution)/shard_map/f0y/ppermute | solution.py:64
  18.6 1.6 %collective-permute-start.5 = (bf16[64,1920]{1,0:T(8,128)(2,1)}, bf16[64,1920]{1,0:T(8,128)(2,1)S(1)}, u32[]{:S(2)}, u32[]{:S(2)}) collective-permute-start(bf16[64,1920]{1,0:T(8,128)(2,1)} %collective-permute-done.2.refs_0_), channel_id=1, source_target_pairs={{0,4},{1,5},{2,6},{3,7},{4,0},{5,1},{6,2},{7,3},{8,12},{9,13},{10,... | collective-permute-start | bytes 737288 | tf_op jit(solution)/shard_map/m3/ppermute | solution.py:64
  20.1 1.5 %collective-permute-start.4 = (bf16[64,1920]{1,0:T(8,128)(2,1)}, bf16[64,1920]{1,0:T(8,128)(2,1)S(1)}, u32[]{:S(2)}, u32[]{:S(2)}) collective-permute-start(bf16[64,1920]{1,0:T(8,128)(2,1)} %collective-permute-done.2.refs_0_), channel_id=1, source_target_pairs={{0,2},{1,17},{2,0},{3,19},{4,6},{5,21},{6,4},{7,23},{8,10},{9,25},... | collective-permute-start | bytes 737288 | tf_op jit(solution)/shard_map/r2/ppermute | solution.py:92
  21.7 1.5 %collective-permute-start.3 = (bf16[64,1920]{1,0:T(8,128)(2,1)}, bf16[64,1920]{1,0:T(8,128)(2,1)S(1)}, u32[]{:S(2)}, u32[]{:S(2)}) collective-permute-start(bf16[64,1920]{1,0:T(8,128)(2,1)} %collective-permute-done.2.refs_0_), channel_id=1, source_target_pairs={{0,16},{1,3},{2,18},{3,1},{4,20},{5,7},{6,22},{7,5},{8,24},{9,11},... | collective-permute-start | bytes 737288 | tf_op jit(solution)/shard_map/q2/ppermute | solution.py:92
  25.0 2.0 %shard_map.66 = (bf16[64,3712]{1,0:T(8,128)(2,1)S(1)}, bf16[64,3712]{1,0:T(8,128)(2,1)S(1)}, bf16[2,64,64]{2,1,0:T(8,128)(2,1)S(1)}, bf16[64,3712]{1,0:T(8,128)(2,1)S(1)}) custom-call(s32[1]{0:T(128)} %bitcast.4.me_ref, bf16[64,1920]{1,0:T(8,128)(2,1)S(1)} %copy-done.4, bf16[64,1792]{1,0:T(8,128)(2,1)S(1)} %copy-done.5, ...), custom_call_target="tpu_custom_call" | custom-call | flops 34359738368 | bytes 1 | tf_op jit(solution)/shard_map/pallas_call | solution.py:103
  29.3 1.6 %collective-permute-start.10 = (bf16[64,1920]{1,0:T(8,128)(2,1)S(1)}, bf16[64,1920]{1,0:T(8,128)(2,1)S(1)}, u32[]{:S(2)}, u32[]{:S(2)}) collective-permute-start(bf16[64,1920]{1,0:T(8,128)(2,1)S(1)} %collective-permute-done.3.refs_2_.refs_0_), channel_id=1, source_target_pairs={{0,2},{1,17},{2,0},{3,19},{4,6},{5,21},{6,4},{7,23},{8,10},{9,25},... | collective-permute-start | bytes 737288 | tf_op jit(solution)/shard_map/t2/ppermute | solution.py:92
  33.0 2.8 %shard_map.67.hidden_ref = bf16[128,1024]{1,0:T(8,128)(2,1)S(1)} custom-call(s32[2]{0:T(128)S(1)} %pad_add_fusion.scalar_ref, bf16[64,3712]{1,0:T(8,128)(2,1)S(1)} %get-tuple-element.75.keep_ref, bf16[64,3712]{1,0:T(8,128)(2,1)S(1)} %collective-permute-done.8.got_ref, bf16[1,3584,1024]{2,1,0:T(8,128)(2,1)S(1)} %bitcast.29, bf16[1,3584,1024]{2,1,0:T(8,128)(2,1)S(1)} %copy-done.2), custom_call_target="tpu_custom_call" | custom-call | flops 1 | bytes 1 | tf_op jit(solution)/shard_map/pallas_call | solution.py:103
  36.1 1.7 %shard_map.68 = (bf16[2,64,1792]{2,1,0:T(8,128)(2,1)S(1)}, bf16[2,64,1792]{2,1,0:T(8,128)(2,1)S(1)}) custom-call(s32[2]{0:T(128)S(1)} %pad_add_fusion.scalar_ref, bf16[128,1024]{1,0:T(8,128)(2,1)S(1)} %shard_map.67.hidden_ref, bf16[1,1024,3584]{2,1,0:T(8,128)(2,1)S(1)} %copy-done.3), custom_call_target="tpu_custom_call" | custom-call | flops 1 | bytes 1 | tf_op jit(solution)/shard_map/pallas_call | solution.py:103
  37.7 3.6 %collective-permute-done.9.refs_2_ = bf16[64,3712]{1,0:T(8,128)(2,1)S(1)} collective-permute-done((bf16[64,3712]{1,0:T(8,128)(2,1)S(1)}, bf16[64,3712]{1,0:T(8,128)(2,1)S(1)}, u32[]{:S(2)}, u32[]{:S(2)}) %collective-permute-start.9) | collective-permute-done | bytes 475168 | tf_op jit(solution)/shard_map/w1y/ppermute | solution.py:64
  41.4 1.9 %shard_map.69 = (bf16[128,1920]{1,0:T(8,128)(2,1)S(1)}, bf16[128,1920]{1,0:T(8,128)(2,1)S(1)}, bf16[4,64,64]{2,1,0:T(8,128)(2,1)S(1)}) custom-call(s32[1]{0:T(128)} %bitcast.5.me_ref, bf16[64,1920]{1,0:T(8,128)(2,1)} %collective-permute-done.2.refs_0_, bf16[64,1920]{1,0:T(8,128)(2,1)S(1)} %collective-permute-done.4.refs_1_, ...), custom_call_target="tpu_custom_call" | custom-call | flops 34359738368 | bytes 1 | tf_op jit(solution)/shard_map/pallas_call | solution.py:103
  43.9 1.7 %shard_map.70 = (bf16[64,3712]{1,0:T(8,128)(2,1)S(1)}, bf16[64,3712]{1,0:T(8,128)(2,1)S(1)}, bf16[2,64,64]{2,1,0:T(8,128)(2,1)S(1)}) custom-call(s32[1]{0:T(128)} %bitcast.6.me_ref, bf16[64,1920]{1,0:T(8,128)(2,1)S(1)} %collective-permute-done.7.refs_0_, bf16[64,1792]{1,0:T(8,128)(2,1)} %collective-permute-done.6.refs_1_, ...), custom_call_target="tpu_custom_call" | custom-call | flops 1 | bytes 1 | tf_op jit(solution)/shard_map/pallas_call | solution.py:103
  46.9 2.7 %shard_map.71 = (f32[256,1024]{1,0:T(8,128)S(1)}, f32[256,1024]{1,0:T(8,128)S(1)}) custom-call(s32[2]{0:T(128)S(1)} %pad_add_fusion.scalar_ref, bf16[128,1920]{1,0:T(8,128)(2,1)S(1)} %get-tuple-element.84.keep_ref.refs_2_, bf16[128,1920]{1,0:T(8,128)(2,1)S(1)} %collective-permute-done.13.got_ref.refs_3_, bf16[1,3584,1024]{2,1,0:T(8,128)(2,1)S(1)} %bitcast.29, ...), custom_call_target="tpu_custom_call" | custom-call | flops 1 | bytes 1 | tf_op jit(solution)/shard_map/pallas_call | solution.py:103
  50.2 2.8 %shard_map.73.hidden_ref = bf16[128,1024]{1,0:T(8,128)(2,1)S(1)} custom-call(s32[2]{0:T(128)S(1)} %pad_add_fusion.scalar_ref, bf16[64,3712]{1,0:T(8,128)(2,1)S(1)} %get-tuple-element.87.keep_ref, bf16[64,3712]{1,0:T(8,128)(2,1)S(1)} %collective-permute-done.15.got_ref, bf16[1,3584,1024]{2,1,0:T(8,128)(2,1)S(1)} %bitcast.29, bf16[1,3584,1024]{2,1,0:T(8,128)(2,1)S(1)} %copy-done.2), custom_call_target="tpu_custom_call" | custom-call | flops 1 | bytes 1 | tf_op jit(solution)/shard_map/pallas_call | solution.py:103
  53.0 1.7 %shard_map.74 = (bf16[2,64,1792]{2,1,0:T(8,128)(2,1)S(1)}, bf16[2,64,1792]{2,1,0:T(8,128)(2,1)S(1)}) custom-call(s32[2]{0:T(128)S(1)} %pad_add_fusion.scalar_ref, bf16[128,1024]{1,0:T(8,128)(2,1)S(1)} %shard_map.73.hidden_ref, bf16[1,1024,3584]{2,1,0:T(8,128)(2,1)S(1)} %copy-done.3), custom_call_target="tpu_custom_call" | custom-call | flops 1 | bytes 1 | tf_op jit(solution)/shard_map/pallas_call | solution.py:103
  55.3 3.0 %shard_map.75.hidden_ref = bf16[256,1024]{1,0:T(8,128)(2,1)S(1)} custom-call(s32[2]{0:T(128)S(1)} %pad_add_fusion.scalar_ref, bf16[128,1792]{1,0:T(8,128)(2,1)S(1)} %get-tuple-element.92.keep_ref, bf16[128,1792]{1,0:T(8,128)(2,1)S(1)} %collective-permute-done.16.got_ref, bf16[1,3584,1024]{2,1,0:T(8,128)(2,1)S(1)} %bitcast.29, ...), custom_call_target="tpu_custom_call" | custom-call | flops 1 | bytes 1 | tf_op jit(solution)/shard_map/pallas_call | solution.py:103
  58.2 1.7 %shard_map.76 = (bf16[2,64,1792]{2,1,0:T(8,128)(2,1)S(1)}, bf16[2,64,1792]{2,1,0:T(8,128)(2,1)S(1)}) custom-call(s32[2]{0:T(128)S(1)} %pad_add_fusion.scalar_ref, bf16[256,1024]{1,0:T(8,128)(2,1)S(1)} %shard_map.75.hidden_ref, bf16[1,1024,3584]{2,1,0:T(8,128)(2,1)S(1)} %copy-done.3, f32[16,128]{1,0:T(8,128)S(1)} %shard_map.65.refs_0_), custom_call_target="tpu_custom_call" | custom-call | flops 1 | bytes 1 | tf_op jit(solution)/shard_map/pallas_call | solution.py:103
  60.4 1.7 %shard_map.78 = (bf16[2,64,1792]{2,1,0:T(8,128)(2,1)S(1)}, bf16[2,64,1792]{2,1,0:T(8,128)(2,1)S(1)}) custom-call(s32[2]{0:T(128)S(1)} %pad_add_fusion.scalar_ref, bf16[256,1024]{1,0:T(8,128)(2,1)S(1)} %shard_map.75.hidden_ref, bf16[1,1024,3584]{2,1,0:T(8,128)(2,1)S(1)} %copy-done.3), custom_call_target="tpu_custom_call" | custom-call | flops 1 | bytes 1 | tf_op jit(solution)/shard_map/pallas_call | solution.py:103
  63.6 1.5 %collective-permute-start.22 = (bf16[2,64,1792]{2,1,0:T(8,128)(2,1)S(1)}, bf16[2,64,1792]{2,1,0:T(8,128)(2,1)S(1)}, u32[]{:S(2)}, u32[]{:S(2)}) collective-permute-start(bf16[2,64,1792]{2,1,0:T(8,128)(2,1)S(1)} %get-tuple-element.114), channel_id=1, source_target_pairs={{0,16},{1,3},{2,18},{3,1},{4,20},{5,7},{6,22},{7,5},{8,24},{9,11},... | collective-permute-start | bytes 1376264 | tf_op jit(solution)/shard_map/u3/ppermute | solution.py:92
  65.1 1.6 %collective-permute-start.21 = (bf16[2,64,1792]{2,1,0:T(8,128)(2,1)S(1)}, bf16[2,64,1792]{2,1,0:T(8,128)(2,1)S(1)}, u32[]{:S(2)}, u32[]{:S(2)}) collective-permute-start(bf16[2,64,1792]{2,1,0:T(8,128)(2,1)S(1)} %get-tuple-element.102), channel_id=1, source_target_pairs={{0,4},{1,5},{2,6},{3,7},{4,0},{5,1},{6,2},{7,3},{8,12},{9,13},{10,... | collective-permute-start | bytes 1376264 | tf_op jit(solution)/shard_map/nk/ppermute | solution.py:64
  68.1 8.0 %collective-permute-done.23 = bf16[2,64,1792]{2,1,0:T(8,128)(2,1)S(1)} collective-permute-done((bf16[2,64,1792]{2,1,0:T(8,128)(2,1)S(1)}, bf16[2,64,1792]{2,1,0:T(8,128)(2,1)S(1)}, u32[]{:S(2)}, u32[]{:S(2)}) %collective-permute-start.23) | collective-permute-done | bytes 458784 | tf_op jit(solution)/shard_map/ng/ppermute | solution.py:64
  79.3 3.9 %collective-permute-done.24 = bf16[64,1792]{1,0:T(8,128)(2,1)S(1)} collective-permute-done((bf16[64,1792]{1,0:T(8,128)(2,1)S(1)}, bf16[64,1792]{1,0:T(8,128)(2,1)S(1)}, u32[]{:S(2)}, u32[]{:S(2)}) %collective-permute-start.24) | collective-permute-done | bytes 229408 | tf_op jit(solution)/shard_map/v3/ppermute | solution.py:92
  83.3 1.6 %collective-permute-start.29 = (bf16[64,1792]{1,0:T(8,128)(2,1)S(1)}, bf16[64,1792]{1,0:T(8,128)(2,1)S(1)}, u32[]{:S(2)}, u32[]{:S(2)}) collective-permute-start(bf16[64,1792]{1,0:T(8,128)(2,1)S(1)} %fusion.4), channel_id=1, source_target_pairs={{0,4},{1,5},{2,6},{3,7},{4,0},{5,1},{6,2},{7,3},{8,12},{9,13},{10,... | collective-permute-start | bytes 688136 | tf_op jit(solution)/shard_map/s3/ppermute | solution.py:64
  87.4 3.0 %collective-permute-done.29 = bf16[64,1792]{1,0:T(8,128)(2,1)S(1)} collective-permute-done((bf16[64,1792]{1,0:T(8,128)(2,1)S(1)}, bf16[64,1792]{1,0:T(8,128)(2,1)S(1)}, u32[]{:S(2)}, u32[]{:S(2)}) %collective-permute-start.29) | collective-permute-done | bytes 229408 | tf_op jit(solution)/shard_map/s3/ppermute | solution.py:64
  90.5 2.4 %collective-permute-start.30 = (bf16[64,1792]{1,0:T(8,128)(2,1)S(1)}, bf16[64,1792]{1,0:T(8,128)(2,1)S(1)}, u32[]{:S(2)}, u32[]{:S(2)}) collective-permute-start(bf16[64,1792]{1,0:T(8,128)(2,1)S(1)} %fusion.1), channel_id=1, source_target_pairs={{0,8},{1,9},{2,10},{3,11},{4,12},{5,13},{6,14},{7,15},{8,0},{9,1},... | collective-permute-start | bytes 688136 | tf_op jit(solution)/shard_map/s2/ppermute | solution.py:64
  92.8 1.5 %collective-permute-done.26 = bf16[2,64,1792]{2,1,0:T(8,128)(2,1)S(1)} collective-permute-done((bf16[2,64,1792]{2,1,0:T(8,128)(2,1)S(1)}, bf16[2,64,1792]{2,1,0:T(8,128)(2,1)S(1)}, u32[]{:S(2)}, u32[]{:S(2)}) %collective-permute-start.26) | collective-permute-done | bytes 458784 | tf_op jit(solution)/shard_map/u0/ppermute | solution.py:92
  95.4 6.3 %collective-permute-done.30 = bf16[64,1792]{1,0:T(8,128)(2,1)S(1)} collective-permute-done((bf16[64,1792]{1,0:T(8,128)(2,1)S(1)}, bf16[64,1792]{1,0:T(8,128)(2,1)S(1)}, u32[]{:S(2)}, u32[]{:S(2)}) %collective-permute-start.30) | collective-permute-done | bytes 229408 | tf_op jit(solution)/shard_map/s2/ppermute | solution.py:64
  (76 shorter events, 21.4 us)
Async XLA Ops:
  1.9 16.7 %collective-permute-start.2 = (bf16[64,1920]{1,0:T(8,128)(2,1)}, bf16[64,1920]{1,0:T(8,128)(2,1)}, u32[]{:S(2)}, u32[]{:S(2)}) collective-permute-start(bf16[64,1920]{1,0:T(8,128)(2,1)} %get-tuple-element.65.refs_0_), channel_id=1, source_target_pairs={{0,8},{1,9},{2,10},{3,11},{4,12},{5,13},{6,14},{7,15},{8,0},{9,1},... | collective-permute-start | bytes 737288 | tf_op jit(solution)/shard_map/m2/ppermute | solution.py:64
  5.9 12.7 %collective-permute-start.1 = (bf16[64,1920]{1,0:T(8,128)(2,1)}, bf16[64,1920]{1,0:T(8,128)(2,1)}, u32[]{:S(2)}, u32[]{:S(2)}) collective-permute-start(bf16[64,1920]{1,0:T(8,128)(2,1)} %get-tuple-element.65.refs_0_), channel_id=1, source_target_pairs={{0,2},{1,3},{2,0},{3,1},{4,6},{5,7},{6,4},{7,5},{8,10},{9,11},{10,... | collective-permute-start | bytes 737288 | tf_op jit(solution)/shard_map/m0y/ppermute | solution.py:64
  7.4 11.1 %collective-permute-start = (bf16[64,1792]{1,0:T(8,128)(2,1)}, bf16[64,1792]{1,0:T(8,128)(2,1)}, u32[]{:S(2)}, u32[]{:S(2)}) collective-permute-start(bf16[64,1792]{1,0:T(8,128)(2,1)} %get-tuple-element.64.refs_1_), channel_id=1, source_target_pairs={{0,2},{1,3},{2,0},{3,1},{4,6},{5,7},{6,4},{7,5},{8,10},{9,11},{10,... | collective-permute-start | bytes 688136 | tf_op jit(solution)/shard_map/f0y/ppermute | solution.py:64
  7.9 19.1 %collective-permute-start.6 = (bf16[64,1792]{1,0:T(8,128)(2,1)}, bf16[64,1792]{1,0:T(8,128)(2,1)}, u32[]{:S(2)}, u32[]{:S(2)}) collective-permute-start(bf16[64,1792]{1,0:T(8,128)(2,1)} %get-tuple-element.64.refs_1_), channel_id=1, source_target_pairs={{0,4},{1,5},{2,6},{3,7},{4,0},{5,1},{6,2},{7,3},{8,12},{9,13},{10,... | collective-permute-start | bytes 688136 | tf_op jit(solution)/shard_map/f1/ppermute | solution.py:64
  9.5 17.6 %collective-permute-start.7 = (bf16[64,1920]{1,0:T(8,128)(2,1)}, bf16[64,1920]{1,0:T(8,128)(2,1)S(1)}, u32[]{:S(2)}, u32[]{:S(2)}) collective-permute-start(bf16[64,1920]{1,0:T(8,128)(2,1)} %get-tuple-element.65.refs_0_), channel_id=1, source_target_pairs={{0,4},{1,5},{2,6},{3,7},{4,0},{5,1},{6,2},{7,3},{8,12},{9,13},{10,... | collective-permute-start | bytes 737288 | tf_op jit(solution)/shard_map/m1/ppermute | solution.py:64
  16.1 16.8 %slice-start = ((s8[7340032]{0:T(1024)(128)(4,1)}), s8[3145728]{0:T(1024)(128)(4,1)S(1)}, s32[]{:S(2)}) async-start(s8[7340032]{0:T(1024)(128)(4,1)} %bitcast.28), calls=%async_computation | async-start | bytes 6291456
  18.6 10.7 %collective-permute-start.5 = (bf16[64,1920]{1,0:T(8,128)(2,1)}, bf16[64,1920]{1,0:T(8,128)(2,1)S(1)}, u32[]{:S(2)}, u32[]{:S(2)}) collective-permute-start(bf16[64,1920]{1,0:T(8,128)(2,1)} %collective-permute-done.2.refs_0_), channel_id=1, source_target_pairs={{0,4},{1,5},{2,6},{3,7},{4,0},{5,1},{6,2},{7,3},{8,12},{9,13},{10,... | collective-permute-start | bytes 737288 | tf_op jit(solution)/shard_map/m3/ppermute | solution.py:64
  20.1 9.1 %collective-permute-start.4 = (bf16[64,1920]{1,0:T(8,128)(2,1)}, bf16[64,1920]{1,0:T(8,128)(2,1)S(1)}, u32[]{:S(2)}, u32[]{:S(2)}) collective-permute-start(bf16[64,1920]{1,0:T(8,128)(2,1)} %collective-permute-done.2.refs_0_), channel_id=1, source_target_pairs={{0,2},{1,17},{2,0},{3,19},{4,6},{5,21},{6,4},{7,23},{8,10},{9,25},... | collective-permute-start | bytes 737288 | tf_op jit(solution)/shard_map/r2/ppermute | solution.py:92
  21.7 6.4 %collective-permute-start.3 = (bf16[64,1920]{1,0:T(8,128)(2,1)}, bf16[64,1920]{1,0:T(8,128)(2,1)S(1)}, u32[]{:S(2)}, u32[]{:S(2)}) collective-permute-start(bf16[64,1920]{1,0:T(8,128)(2,1)} %collective-permute-done.2.refs_0_), channel_id=1, source_target_pairs={{0,16},{1,3},{2,18},{3,1},{4,20},{5,7},{6,22},{7,5},{8,24},{9,11},... | collective-permute-start | bytes 737288 | tf_op jit(solution)/shard_map/q2/ppermute | solution.py:92
  28.1 4.9 %collective-permute-start.8 = (bf16[64,3712]{1,0:T(8,128)(2,1)S(1)}, bf16[64,3712]{1,0:T(8,128)(2,1)S(1)}, u32[]{:S(2)}, u32[]{:S(2)}) collective-permute-start(bf16[64,3712]{1,0:T(8,128)(2,1)S(1)} %get-tuple-element.77), channel_id=1, source_target_pairs={{0,1},{1,0},{2,3},{3,2},{4,5},{5,4},{6,7},{7,6},{8,9},{9,8},{10,11... | collective-permute-start | bytes 1425416 | tf_op jit(solution)/shard_map/rows_0/ppermute | solution.py:64
  28.1 13.3 %collective-permute-start.9 = (bf16[64,3712]{1,0:T(8,128)(2,1)S(1)}, bf16[64,3712]{1,0:T(8,128)(2,1)S(1)}, u32[]{:S(2)}, u32[]{:S(2)}) collective-permute-start(bf16[64,3712]{1,0:T(8,128)(2,1)S(1)} %get-tuple-element.79), channel_id=1, source_target_pairs={{0,4},{1,5},{2,6},{3,7},{4,0},{5,1},{6,2},{7,3},{8,12},{9,13},{10,... | collective-permute-start | bytes 1425416 | tf_op jit(solution)/shard_map/w1y/ppermute | solution.py:64
  29.3 12.1 %collective-permute-start.10 = (bf16[64,1920]{1,0:T(8,128)(2,1)S(1)}, bf16[64,1920]{1,0:T(8,128)(2,1)S(1)}, u32[]{:S(2)}, u32[]{:S(2)}) collective-permute-start(bf16[64,1920]{1,0:T(8,128)(2,1)S(1)} %collective-permute-done.3.refs_2_.refs_0_), channel_id=1, source_target_pairs={{0,2},{1,17},{2,0},{3,19},{4,6},{5,21},{6,4},{7,23},{8,10},{9,25},... | collective-permute-start | bytes 737288 | tf_op jit(solution)/shard_map/t2/ppermute | solution.py:92
  30.9 10.5 %collective-permute-start.12 = (bf16[64,1920]{1,0:T(8,128)(2,1)S(1)}, bf16[64,1920]{1,0:T(8,128)(2,1)S(1)}, u32[]{:S(2)}, u32[]{:S(2)}) collective-permute-start(bf16[64,1920]{1,0:T(8,128)(2,1)S(1)} %collective-permute-done.5.refs_3_), channel_id=1, source_target_pairs={{0,16},{1,3},{2,18},{3,1},{4,20},{5,7},{6,22},{7,5},{8,24},{9,11},... | collective-permute-start | bytes 737288 | tf_op jit(solution)/shard_map/q3/ppermute | solution.py:92
  32.4 9.0 %collective-permute-start.11 = (bf16[64,1920]{1,0:T(8,128)(2,1)S(1)}, bf16[64,1920]{1,0:T(8,128)(2,1)S(1)}, u32[]{:S(2)}, u32[]{:S(2)}) collective-permute-start(bf16[64,1920]{1,0:T(8,128)(2,1)S(1)} %collective-permute-done.5.refs_3_), channel_id=1, source_target_pairs={{0,2},{1,17},{2,0},{3,19},{4,6},{5,21},{6,4},{7,23},{8,10},{9,25},... | collective-permute-start | bytes 737288 | tf_op jit(solution)/shard_map/r3/ppermute | solution.py:92
  43.3 3.6 %collective-permute-start.13 = (bf16[128,1920]{1,0:T(8,128)(2,1)S(1)}, bf16[128,1920]{1,0:T(8,128)(2,1)S(1)}, u32[]{:S(2)}, u32[]{:S(2)}) collective-permute-start(bf16[128,1920]{1,0:T(8,128)(2,1)S(1)} %get-tuple-element.89), channel_id=1, source_target_pairs={{0,1},{1,0},{2,3},{3,2},{4,5},{5,4},{6,7},{7,6},{8,9},{9,8},{10,11... | collective-permute-start | bytes 1474568 | tf_op jit(solution)/shard_map/rows_m/ppermute | solution.py:64
  43.4 6.3 %collective-permute-start.14 = (bf16[64,1920]{1,0:T(8,128)(2,1)S(1)}, bf16[64,1920]{1,0:T(8,128)(2,1)S(1)}, u32[]{:S(2)}, u32[]{:S(2)}) collective-permute-start(bf16[64,1920]{1,0:T(8,128)(2,1)S(1)} %collective-permute-done.12.refs_5_.refs_3_), channel_id=1, source_target_pairs={{0,2},{1,17},{2,0},{3,19},{4,6},{5,21},{6,4},{7,23},{8,10},{9,25},... | collective-permute-start | bytes 737288 | tf_op jit(solution)/shard_map/t3/ppermute | solution.py:92
  45.7 4.5 %collective-permute-start.15 = (bf16[64,3712]{1,0:T(8,128)(2,1)S(1)}, bf16[64,3712]{1,0:T(8,128)(2,1)S(1)}, u32[]{:S(2)}, u32[]{:S(2)}) collective-permute-start(bf16[64,3712]{1,0:T(8,128)(2,1)S(1)} %get-tuple-element.94), channel_id=1, source_target_pairs={{0,1},{1,0},{2,3},{3,2},{4,5},{5,4},{6,7},{7,6},{8,9},{9,8},{10,11... | collective-permute-start | bytes 1425416 | tf_op jit(solution)/shard_map/rows_1/ppermute | solution.py:64
  50.1 5.2 %collective-permute-start.16 = (bf16[128,1792]{1,0:T(8,128)(2,1)S(1)}, bf16[128,1792]{1,0:T(8,128)(2,1)S(1)}, u32[]{:S(2)}, u32[]{:S(2)}) collective-permute-start(bf16[128,1792]{1,0:T(8,128)(2,1)S(1)} %get-tuple-element.97), channel_id=1, source_target_pairs={{0,1},{1,0},{2,3},{3,2},{4,5},{5,4},{6,7},{7,6},{8,9},{9,8},{10,11... | collective-permute-start | bytes 1376264 | tf_op jit(solution)/shard_map/rows_f/ppermute | solution.py:64
  54.7 5.3 %collective-permute-start.17 = (bf16[2,64,1792]{2,1,0:T(8,128)(2,1)S(1)}, bf16[2,64,1792]{2,1,0:T(8,128)(2,1)S(1)}, u32[]{:S(2)}, u32[]{:S(2)}) collective-permute-start(bf16[2,64,1792]{2,1,0:T(8,128)(2,1)S(1)} %get-tuple-element.101), channel_id=1, source_target_pairs={{0,1},{1,0},{2,3},{3,2},{4,5},{5,4},{6,7},{7,6},{8,9},{9,8},{10,11... | collective-permute-start | bytes 1376264 | tf_op jit(solution)/shard_map/back_1/ppermute | solution.py:64
  59.9 3.3 %collective-permute-start.18 = (bf16[2,64,1792]{2,1,0:T(8,128)(2,1)S(1)}, bf16[2,64,1792]{2,1,0:T(8,128)(2,1)S(1)}, u32[]{:S(2)}, u32[]{:S(2)}) collective-permute-start(bf16[2,64,1792]{2,1,0:T(8,128)(2,1)S(1)} %get-tuple-element.106), channel_id=1, source_target_pairs={{0,1},{1,0},{2,3},{3,2},{4,5},{5,4},{6,7},{7,6},{8,9},{9,8},{10,11... | collective-permute-start | bytes 1376264 | tf_op jit(solution)/shard_map/back_3/ppermute | solution.py:64
  62.1 4.6 %collective-permute-start.19 = (bf16[2,64,1792]{2,1,0:T(8,128)(2,1)S(1)}, bf16[2,64,1792]{2,1,0:T(8,128)(2,1)S(1)}, u32[]{:S(2)}, u32[]{:S(2)}) collective-permute-start(bf16[2,64,1792]{2,1,0:T(8,128)(2,1)S(1)} %get-tuple-element.109), channel_id=1, source_target_pairs={{0,1},{1,0},{2,3},{3,2},{4,5},{5,4},{6,7},{7,6},{8,9},{9,8},{10,11... | collective-permute-start | bytes 1376264 | tf_op jit(solution)/shard_map/back_2/ppermute | solution.py:64
  62.7 5.1 %collective-permute-start.20 = (bf16[2,64,1792]{2,1,0:T(8,128)(2,1)S(1)}, bf16[2,64,1792]{2,1,0:T(8,128)(2,1)S(1)}, u32[]{:S(2)}, u32[]{:S(2)}) collective-permute-start(bf16[2,64,1792]{2,1,0:T(8,128)(2,1)S(1)} %get-tuple-element.112), channel_id=1, source_target_pairs={{0,1},{1,0},{2,3},{3,2},{4,5},{5,4},{6,7},{7,6},{8,9},{9,8},{10,11... | collective-permute-start | bytes 1376264 | tf_op jit(solution)/shard_map/back_0/ppermute | solution.py:64
  62.7 13.3 %collective-permute-start.23 = (bf16[2,64,1792]{2,1,0:T(8,128)(2,1)S(1)}, bf16[2,64,1792]{2,1,0:T(8,128)(2,1)S(1)}, u32[]{:S(2)}, u32[]{:S(2)}) collective-permute-start(bf16[2,64,1792]{2,1,0:T(8,128)(2,1)S(1)} %get-tuple-element.115), channel_id=1, source_target_pairs={{0,4},{1,5},{2,6},{3,7},{4,0},{5,1},{6,2},{7,3},{8,12},{9,13},{10,... | collective-permute-start | bytes 1376264 | tf_op jit(solution)/shard_map/ng/ppermute | solution.py:64
  63.6 12.5 %collective-permute-start.22 = (bf16[2,64,1792]{2,1,0:T(8,128)(2,1)S(1)}, bf16[2,64,1792]{2,1,0:T(8,128)(2,1)S(1)}, u32[]{:S(2)}, u32[]{:S(2)}) collective-permute-start(bf16[2,64,1792]{2,1,0:T(8,128)(2,1)S(1)} %get-tuple-element.114), channel_id=1, source_target_pairs={{0,16},{1,3},{2,18},{3,1},{4,20},{5,7},{6,22},{7,5},{8,24},{9,11},... | collective-permute-start | bytes 1376264 | tf_op jit(solution)/shard_map/u3/ppermute | solution.py:92
  65.1 20.8 %collective-permute-start.21 = (bf16[2,64,1792]{2,1,0:T(8,128)(2,1)S(1)}, bf16[2,64,1792]{2,1,0:T(8,128)(2,1)S(1)}, u32[]{:S(2)}, u32[]{:S(2)}) collective-permute-start(bf16[2,64,1792]{2,1,0:T(8,128)(2,1)S(1)} %get-tuple-element.102), channel_id=1, source_target_pairs={{0,4},{1,5},{2,6},{3,7},{4,0},{5,1},{6,2},{7,3},{8,12},{9,13},{10,... | collective-permute-start | bytes 1376264 | tf_op jit(solution)/shard_map/nk/ppermute | solution.py:64
  67.1 10.0 %collective-permute-start.25 = (bf16[2,64,1792]{2,1,0:T(8,128)(2,1)S(1)}, bf16[2,64,1792]{2,1,0:T(8,128)(2,1)S(1)}, u32[]{:S(2)}, u32[]{:S(2)}) collective-permute-start(bf16[2,64,1792]{2,1,0:T(8,128)(2,1)S(1)} %get-tuple-element.117), channel_id=1, source_target_pairs={{0,16},{1,3},{2,18},{3,1},{4,20},{5,7},{6,22},{7,5},{8,24},{9,11},... | collective-permute-start | bytes 1376264 | tf_op jit(solution)/shard_map/u2/ppermute | solution.py:92
  77.2 6.1 %collective-permute-start.24 = (bf16[64,1792]{1,0:T(8,128)(2,1)S(1)}, bf16[64,1792]{1,0:T(8,128)(2,1)S(1)}, u32[]{:S(2)}, u32[]{:S(2)}) collective-permute-start(bf16[64,1792]{1,0:T(8,128)(2,1)S(1)} %slice_bitcast_fusion.4), channel_id=1, source_target_pairs={{0,2},{1,17},{2,0},{3,19},{4,6},{5,21},{6,4},{7,23},{8,10},{9,25},... | collective-permute-start | bytes 688136 | tf_op jit(solution)/shard_map/v3/ppermute | solution.py:92
  78.0 9.4 %collective-permute-start.28 = (bf16[64,1792]{1,0:T(8,128)(2,1)S(1)}, bf16[64,1792]{1,0:T(8,128)(2,1)S(1)}, u32[]{:S(2)}, u32[]{:S(2)}) collective-permute-start(bf16[64,1792]{1,0:T(8,128)(2,1)S(1)} %slice_bitcast_fusion), channel_id=1, source_target_pairs={{0,2},{1,17},{2,0},{3,19},{4,6},{5,21},{6,4},{7,23},{8,10},{9,25},... | collective-permute-start | bytes 688136 | tf_op jit(solution)/shard_map/v2/ppermute | solution.py:92
  83.3 7.1 %collective-permute-start.29 = (bf16[64,1792]{1,0:T(8,128)(2,1)S(1)}, bf16[64,1792]{1,0:T(8,128)(2,1)S(1)}, u32[]{:S(2)}, u32[]{:S(2)}) collective-permute-start(bf16[64,1792]{1,0:T(8,128)(2,1)S(1)} %fusion.4), channel_id=1, source_target_pairs={{0,4},{1,5},{2,6},{3,7},{4,0},{5,1},{6,2},{7,3},{8,12},{9,13},{10,... | collective-permute-start | bytes 688136 | tf_op jit(solution)/shard_map/s3/ppermute | solution.py:64
  85.9 8.5 %collective-permute-start.26 = (bf16[2,64,1792]{2,1,0:T(8,128)(2,1)S(1)}, bf16[2,64,1792]{2,1,0:T(8,128)(2,1)S(1)}, u32[]{:S(2)}, u32[]{:S(2)}) collective-permute-start(bf16[2,64,1792]{2,1,0:T(8,128)(2,1)S(1)} %add_convert_fusion.1), channel_id=1, source_target_pairs={{0,16},{1,3},{2,18},{3,1},{4,20},{5,7},{6,22},{7,5},{8,24},{9,11},... | collective-permute-start | bytes 1376264 | tf_op jit(solution)/shard_map/u0/ppermute | solution.py:92
  90.5 11.2 %collective-permute-start.30 = (bf16[64,1792]{1,0:T(8,128)(2,1)S(1)}, bf16[64,1792]{1,0:T(8,128)(2,1)S(1)}, u32[]{:S(2)}, u32[]{:S(2)}) collective-permute-start(bf16[64,1792]{1,0:T(8,128)(2,1)S(1)} %fusion.1), channel_id=1, source_target_pairs={{0,8},{1,9},{2,10},{3,11},{4,12},{5,13},{6,14},{7,15},{8,0},{9,1},... | collective-permute-start | bytes 688136 | tf_op jit(solution)/shard_map/s2/ppermute | solution.py:64
  94.6 7.1 %collective-permute-start.27 = (bf16[64,1792]{1,0:T(8,128)(2,1)S(1)}, bf16[64,1792]{1,0:T(8,128)(2,1)S(1)}, u32[]{:S(2)}, u32[]{:S(2)}) collective-permute-start(bf16[64,1792]{1,0:T(8,128)(2,1)S(1)} %slice_bitcast_fusion.2), channel_id=1, source_target_pairs={{0,2},{1,17},{2,0},{3,19},{4,6},{5,21},{6,4},{7,23},{8,10},{9,25},... | collective-permute-start | bytes 688136 | tf_op jit(solution)/shard_map/v0/ppermute | solution.py:92
  (7 other events, 27.0 us)
